TPU v7x, 1024 devices: a whole 8x8x8 slice. The times are simulated.
1024 devices in a mesh: node: 16 (over z, core), local: 64 (over x, y).
Axes of the slice: x: 8, y: 8, z: 8, core: 2. Of those that a mesh axis runs over, the one named last changes fastest.
Arguments:
- out_grad: bfloat16 [8192, 7168], P('local', 'node'), may hold values from -0.796875 to 0.796875
- gate_weights: bfloat16 [8192, 8], P('local'), may hold values from 0.049804688 to 0.5
- expert_ids: int32 [8192, 8], P('local'), may hold values from 0 to 63, all different within a row; in each aligned block of 128 rows (0 to 127, 128 to 255, ...) at most 21 rows name the same one
- w_gate: bfloat16 [64, 7168, 1024], P('local', 'node'), may hold values from -0.1875 to 0.1875
- w_up: bfloat16 [64, 7168, 1024], P('local', 'node'), may hold values from -0.1875 to 0.1875
- w_down: bfloat16 [64, 1024, 7168], P('local', None, 'node'), may hold values from -0.0625 to 0.0625
- saved_gate: bfloat16 [64, 1024, 1344], P('local', 'node'), may hold values from -6 to 6
- saved_up: bfloat16 [64, 1024, 1344], P('local', 'node'), may hold values from -6 to 6
Outputs:
- input_grad: bfloat16 [8192, 7168], P('local', 'node')
- combine_grad: bfloat16 [8192, 8], P('local')
Inputs may be any that keep to these rules, and one draw needn't show every extreme that they name: `expert_ids`: each row names 8 different experts; within the tokens of one index of local no expert is named by more than 21 rows, a bound that some block reaches.
All inputs are finite; a program needn't handle non-finite values.
Results may differ from a plain program's by a relative error of at most 0.0057.
Values may be sent and summed in bfloat16 or wider, within the bound.
No kernel may reach another device: no remote copies, remote signals or barrier semaphores. Data moves between devices by JAX's collectives and lax.ppermute only.
A program may use at most 64 MiB of HBM per device.

v0:
```python
import jax
import jax.numpy as jnp
from jax import lax
from jax.sharding import PartitionSpec as P


def local_slots(expert_ids, experts, capacity):
    flat_ids = expert_ids.reshape(-1)
    onehot = (flat_ids[:, None] == jnp.arange(experts, dtype=jnp.int32)[None, :]).astype(jnp.int32)
    before = jnp.cumsum(onehot, axis=0) - onehot
    within = jnp.sum(before * onehot, axis=1)
    return flat_ids * capacity + within


def hidden_math(raw_grad, saved_g, saved_u, slot_gate):
    pre_gate = saved_g.astype(jnp.float32)
    pre_up = saved_u.astype(jnp.float32)
    sigma = jax.nn.sigmoid(pre_gate)
    activ = pre_gate * sigma
    slope = sigma * (1.0 + pre_gate * (1.0 - sigma))
    combine_part = jnp.sum(raw_grad * activ * pre_up, axis=0)
    hidden_grad = raw_grad * slot_gate[None, :]
    gate_pre = (hidden_grad * pre_up * slope).astype(jnp.bfloat16)
    up_pre = (hidden_grad * activ).astype(jnp.bfloat16)
    return (gate_pre, up_pre, combine_part)


def contract_hidden(hidden_rows, columns):
    return lax.dot_general(
        hidden_rows, columns, (((0,), (1,)), ((), ())), preferred_element_type=jnp.float32
    )


def body(out_grad, gate_weights, expert_ids, w_gate, w_up, w_down, saved_gate, saved_up):
    experts = lax.axis_size("local")
    slot_count = saved_gate.shape[2]
    capacity = slot_count // experts
    feature_part = out_grad.shape[1]
    token_rows = out_grad.shape[0]
    top_count = expert_ids.shape[1]
    flat = local_slots(expert_ids, experts, capacity)
    outgoing = jnp.zeros((experts * capacity, feature_part), jnp.bfloat16)
    outgoing = (
        outgoing.at[flat]
        .set(jnp.repeat(out_grad, top_count, axis=0))
        .reshape(experts, capacity, feature_part)
    )
    outgoing_gate = jnp.zeros((experts * capacity,), jnp.bfloat16)
    outgoing_gate = outgoing_gate.at[flat].set(gate_weights.reshape(-1)).reshape(experts, capacity)
    arrived, arrived_gate = (
        lax.all_to_all(outgoing, "local", split_axis=0, concat_axis=0, tiled=True),
        lax.all_to_all(outgoing_gate, "local", split_axis=0, concat_axis=0, tiled=True),
    )
    slot_rows = arrived.reshape(slot_count, feature_part)
    slot_gate = arrived_gate.reshape(slot_count).astype(jnp.float32)
    down_part = w_down[0]
    gate_part = w_gate[0]
    up_part = w_up[0]
    raw_grad = lax.psum_scatter(
        lax.dot_general(
            down_part, slot_rows, (((1,), (1,)), ((), ())), preferred_element_type=jnp.float32
        ),
        "node",
        scatter_dimension=0,
        tiled=True,
    )
    gate_pre, up_pre, combine_part = hidden_math(raw_grad, saved_gate[0], saved_up[0], slot_gate)
    combine_slot = lax.psum(combine_part, "node")
    gate_piece = lax.all_gather(gate_pre, "node", axis=0, tiled=True)
    up_piece = lax.all_gather(up_pre, "node", axis=0, tiled=True)
    slot_input = contract_hidden(gate_piece, gate_part) + contract_hidden(up_piece, up_part)
    back_rows = slot_input.astype(jnp.bfloat16).reshape(experts, capacity, feature_part)
    back_combine = combine_slot.astype(jnp.bfloat16).reshape(experts, capacity)
    returned, returned_combine = (
        lax.all_to_all(back_rows, "local", split_axis=0, concat_axis=0, tiled=True),
        lax.all_to_all(back_combine, "local", split_axis=0, concat_axis=0, tiled=True),
    )
    picked = returned.reshape(experts * capacity, feature_part)[flat].reshape(
        token_rows, top_count, feature_part
    )
    input_grad = jnp.sum(picked.astype(jnp.float32), axis=1).astype(jnp.bfloat16)
    combine_grad = returned_combine.reshape(-1)[flat].reshape(token_rows, top_count)
    return (input_grad, combine_grad)


def solution(mesh):
    in_specs = (
        P("local", "node"),
        P("local", None),
        P("local", None),
        P("local", "node", None),
        P("local", "node", None),
        P("local", None, "node"),
        P("local", "node", None),
        P("local", "node", None),
    )
    out_specs = (P("local", "node"), P("local", None))
    return jax.shard_map(body, mesh=mesh, in_specs=in_specs, out_specs=out_specs, check_vma=False)
```

profile of v0, /device:TPU:22, one launch (start us, length us, event | category | flops | bytes accessed | tf_op | source)
XLA Modules:
  0.0 355.2 jit_solution(9099108870853560428)
XLA Ops:
  9.0 18.0 %reduce-window.6 = s32[64,8,128]{2,1,0:T(8,128)S(1)} reduce-window(s32[64,8,128]{2,1,0:T(8,128)S(1)} %fusion.20, s32[]{:T(128)} %constant.8.clone.1), window={size=1x1x128 pad=0_0x0_0x127_0}, to_apply=%region_0.0 | reduce-window | flops 8323072 | bytes 524292 | tf_op jit(solution)/shard_map/reduce-window
  28.0 6.3 %scatter_custom_fusion = bf16[1344,448]{1,0:T(8,128)(2,1)} fusion(s32[1024]{0:T(1024)S(1)} %bitcast.55, bf16[]{:T(256)} %constant.6.clone.1, bf16[128,448]{1,0:T(8,128)(2,1)S(1)} %copy.46), kind=kCustom, calls=%fused_computation.8 | custom fusion | bytes 1335298 | tf_op jit(solution)/shard_map/scatter | solution.py:45
  34.3 2.5 reshape.101
  36.8 52.9 %all_to_all.30 = bf16[64,21,448]{2,1,0:T(8,128)(2,1)} all-to-all(bf16[64,21,448]{2,1,0:T(8,128)(2,1)S(1)} %reshape.101), channel_id=1, replica_groups=mesh['node'=16,'local'=64] {'local'}, dimensions={0} | all-to-all | bytes 2408448 | tf_op jit(solution)/shard_map/all_to_all | solution.py:51
  89.7 2.5 reshape.102
  92.2 4.0 %convolution_bitcast_fusion = f32[1024,1344]{0,1:T(8,128)} fusion(bf16[1344,448]{1,0:T(8,128)(2,1)S(1)} %reshape.102, bf16[1,1024,448]{1,2,0:T(8,128)(2,1)S(1)} %copy-done), kind=kOutput, calls=%fused_computation.4 | convolution fusion | flops 1233125376 | bytes 7626752 | tf_op jit(solution)/shard_map/dot_general | solution.py:60
  96.3 6.2 %copy.55 = f32[1024,1344]{1,0:T(8,128)} copy(f32[1024,1344]{0,1:T(8,128)} %convolution_bitcast_fusion) | data formatting | bytes 11010048
  103.4 7.6 %scatter_custom_fusion.1 = bf16[1344]{0:T(1024)(128)(2,1)S(1)} fusion(s32[1024]{0:T(1024)S(1)} %bitcast.56, bf16[1024]{0:T(1024)(128)(2,1)S(1)} %reshape.140, bf16[]{:T(256)} %constant.6.clone.1), kind=kCustom, calls=%fused_computation.41 | custom fusion | bytes 2690 | tf_op jit(solution)/shard_map/scatter | solution.py:49
  111.2 16.4 %all_to_all.31 = bf16[64,1,21]{2,1,0:T(2,128)(2,1)S(1)} all-to-all(bf16[64,1,21]{2,1,0:T(2,128)(2,1)S(1)} %all_to_all.24), channel_id=1, replica_groups=mesh['node'=16,'local'=64] {'local'}, dimensions={0} | all-to-all | bytes 5376 | tf_op jit(solution)/shard_map/all_to_all | solution.py:52
  127.8 55.5 %reduce-scatter.4.cloned.1.call-done = f32[64,1344]{1,0:T(8,128)} async-done(((f32[1024,1344]{1,0:T(8,128)}), f32[64,1344]{1,0:T(8,128)}) %reduce-scatter.4.cloned.1.call-update) | async-done | bytes 344080 | tf_op jit(solution)/shard_map/reduce_scatter | solution.py:59
  183.3 2.0 fusion.11
  186.1 24.6 %psum.7 = bf16[1344]{0:T(1024)(128)(2,1)S(1)} all-reduce(f32[1344]{0:T(1024)S(1)} %get-tuple-element.8), channel_id=1, replica_groups=mesh['node'=16,'local'=64] {'node'}, use_global_device_ids=true, to_apply=%region_8.9 | all-reduce | flops 1344 | bytes 8064 | tf_op jit(solution)/shard_map/psum | solution.py:68
  211.5 12.3 %all-to-all-start.3 = ((bf16[64,1,21]{2,1,0:T(2,128)(2,1)}), bf16[64,1,21]{2,1,0:T(2,128)(2,1)}, u32[]{:S(2)}, u32[]{:S(2)}) async-start(bf16[64,1,21]{2,1,0:T(2,128)(2,1)} %all_to_all.25), calls=%async_computation.3 | async-start | bytes 65536 | tf_op jit(solution)/shard_map/all_to_all | solution.py:76
  223.8 7.2 %all-gather.3.cloned.1.call-done = bf16[1024,1344]{1,0:T(8,128)(2,1)} async-done(((bf16[64,1344]{1,0:T(8,128)(2,1)}), bf16[1024,1344]{1,0:T(8,128)(2,1)}) %all-gather.3.cloned.1.call-update) | async-done | bytes 2752528 | tf_op jit(solution)/shard_map/all_gather | solution.py:69
  231.0 4.9 %fusion.4 = f32[1344,448]{0,1:T(8,128)} fusion(bf16[1024,1344]{1,0:T(8,128)(2,1)} %all-gather.3.cloned.1.call-done, bf16[1,448,1024]{2,1,0:T(8,128)(2,1)S(1)} %copy-done.7), kind=kOutput, calls=%fused_computation.11 | convolution fusion | flops 1233125376 | bytes 6078464 | tf_op jit(solution)/shard_map/dot_general | solution.py:29
  235.9 43.5 %all-gather.5.cloned.1.call-done = bf16[1024,1344]{1,0:T(8,128)(2,1)} async-done(((bf16[64,1344]{1,0:T(8,128)(2,1)}), bf16[1024,1344]{1,0:T(8,128)(2,1)}) %all-gather.5.cloned.1.call-update) | async-done | bytes 2752528 | tf_op jit(solution)/shard_map/all_gather | solution.py:70
  279.3 4.5 %fusion = bf16[1344,448]{0,1:T(8,128)(2,1)S(1)} fusion(f32[1344,448]{0,1:T(8,128)} %fusion.4, bf16[1024,1344]{1,0:T(8,128)(2,1)} %all-gather.5.cloned.1.call-done, bf16[1,448,1024]{2,1,0:T(8,128)(2,1)} %param.12), kind=kOutput, calls=%fused_computation.6 | convolution fusion | flops 1234329600 | bytes 7282688 | tf_op jit(solution)/shard_map/dot_general | solution.py:29
  283.8 0.9 copy.50
  284.7 1.4 reshape.104
  286.1 12.9 %all-to-all-start.2 = ((bf16[64,21,448]{2,1,0:T(8,128)(2,1)}), bf16[64,21,448]{2,1,0:T(8,128)(2,1)}, u32[]{:S(2)}, u32[]{:S(2)}) async-start(bf16[64,21,448]{2,1,0:T(8,128)(2,1)} %reshape.104), calls=%async_computation.2 | async-start | bytes 3145728 | tf_op jit(solution)/shard_map/all_to_all | solution.py:75
  300.1 6.8 %gather_fusion.1 = bf16[1024]{0:T(1024)(128)(2,1)S(1)} fusion(bf16[1344]{0:T(1024)(128)(2,1)S(1)} %reshape.107, s32[1024]{0:T(1024)S(1)} %broadcast_clamp_fusion), kind=kCustom, calls=%fused_computation.1 | custom fusion | bytes 8192 | tf_op jit(solution)/shard_map/gather | solution.py:82
  307.6 33.0 %all-to-all-done.2 = bf16[64,21,448]{2,1,0:T(8,128)(2,1)} async-done(((bf16[64,21,448]{2,1,0:T(8,128)(2,1)}), bf16[64,21,448]{2,1,0:T(8,128)(2,1)}, u32[]{:S(2)}, u32[]{:S(2)}) %all-to-all-start.2) | async-done | bytes 1204256 | tf_op jit(solution)/shard_map/all_to_all | solution.py:75
  340.7 2.5 reshape.105
  343.2 4.0 %gather_fusion = bf16[1024,448]{1,0:T(8,128)(2,1)S(1)} fusion(bf16[1344,448]{1,0:T(8,128)(2,1)S(1)} %reshape.105, s32[1024]{0:T(1024)S(1)} %broadcast_clamp_fusion), kind=kCustom, calls=%fused_computation | custom fusion | bytes 1839104 | tf_op jit(solution)/shard_map/gather | solution.py:78
  (52 shorter events, 8.7 us)
Async XLA Ops:
  7.2 85.1 %copy-start = (bf16[1,1024,448]{1,2,0:T(8,128)(2,1)S(1)}, bf16[1,1024,448]{1,2,0:T(8,128)(2,1)}, u32[]{:S(2)}) copy-start(bf16[1,1024,448]{1,2,0:T(8,128)(2,1)} %param.13) | copy-start | bytes 2752516
  7.2 20.6 %copy-start.3 = (bf16[128,448]{0,1:T(8,128)(2,1)S(1)}, bf16[128,448]{0,1:T(8,128)(2,1)}, u32[]{:S(2)}) copy-start(bf16[128,448]{0,1:T(8,128)(2,1)} %param.8) | copy-start | bytes 344068
  7.2 176.1 %reduce-scatter.4.cloned.1.call-start = ((), (), s32[]{:S(2)}) async-start(), calls=%async_computation.7 | async-start | bytes 6127616 | tf_op jit(solution)/shard_map/reduce_scatter | solution.py:59
  28.0 75.4 %copy-start.4 = (s32[1024,1]{0,1:T(1,128)}, s32[1024,1]{0,1:T(1,128)S(1)}, u32[]{:S(2)}) copy-start(s32[1024,1]{0,1:T(1,128)S(1)} %compare_select_fusion) | copy-start | bytes 12292
  102.5 0.7 copy-start.6
  102.5 80.8 %copy-start.1 = (bf16[1,64,1344]{2,1,0:T(8,128)(2,1)S(1)}, bf16[1,64,1344]{2,1,0:T(8,128)(2,1)}, u32[]{:S(2)}) copy-start(bf16[1,64,1344]{2,1,0:T(8,128)(2,1)} %param.15) | copy-start | bytes 516100
  102.5 80.8 %copy-start.2 = (bf16[1,64,1344]{2,1,0:T(8,128)(2,1)S(1)}, bf16[1,64,1344]{2,1,0:T(8,128)(2,1)}, u32[]{:S(2)}) copy-start(bf16[1,64,1344]{2,1,0:T(8,128)(2,1)} %param.14) | copy-start | bytes 516100
  102.5 128.5 %copy-start.7 = (bf16[1,448,1024]{2,1,0:T(8,128)(2,1)S(1)}, bf16[1,448,1024]{2,1,0:T(8,128)(2,1)}, u32[]{:S(2)}) copy-start(bf16[1,448,1024]{2,1,0:T(8,128)(2,1)} %param.11) | copy-start | bytes 2752516
  102.5 128.5 %all-gather.3.cloned.1.call-start = ((), (), s32[]{:S(2)}) async-start(), calls=%async_computation.5 | async-start | bytes 3063808 | tf_op jit(solution)/shard_map/all_gather | solution.py:69
  185.3 94.0 %all-gather.5.cloned.1.call-start = ((), (), s32[]{:S(2)}) async-start(), calls=%async_computation.6 | async-start | bytes 3063808 | tf_op jit(solution)/shard_map/all_gather | solution.py:70
  211.5 74.6 %all-to-all-start.3 = ((bf16[64,1,21]{2,1,0:T(2,128)(2,1)}), bf16[64,1,21]{2,1,0:T(2,128)(2,1)}, u32[]{:S(2)}, u32[]{:S(2)}) async-start(bf16[64,1,21]{2,1,0:T(2,128)(2,1)} %all_to_all.25), calls=%async_computation.3 | async-start | bytes 65536 | tf_op jit(solution)/shard_map/all_to_all | solution.py:76
  286.1 12.9 %copy-start.5 = (s32[1024,1]{0,1:T(1,128)S(1)}, s32[1024,1]{0,1:T(1,128)}, u32[]{:S(2)}) copy-start(s32[1024,1]{0,1:T(1,128)} %copy-done.4) | copy-start | bytes 12292
  286.1 54.5 %all-to-all-start.2 = ((bf16[64,21,448]{2,1,0:T(8,128)(2,1)}), bf16[64,21,448]{2,1,0:T(8,128)(2,1)}, u32[]{:S(2)}, u32[]{:S(2)}) async-start(bf16[64,21,448]{2,1,0:T(8,128)(2,1)} %reshape.104), calls=%async_computation.2 | async-start | bytes 3145728 | tf_op jit(solution)/shard_map/all_to_all | solution.py:75
Sparse Core Ops, SparseCore 0:
  102.6 80.6 reduce-scatter.3
  186.0 44.9 all-gather.2
  233.7 45.5 all-gather.4
where the time goes:
time: 356 us; the launch traced here: 355 us
  waiting for transfers between devices  140 us (39%)
  blocking collectives  93.9 us (26%)
  local copies, waits for them, and re-layouts  46.1 us (13%)
  starting transfers between devices  25.3 us (7%)
  other arithmetic  22.6 us (6%)
  between operations  14 us (4%)
  matrix products  13.4 us (4%)
    reduce_scatter x1, waiting for transfers between devices, body(): lax.psum_scatter(lax.dot_general(down_part, slot_rows, (((1,), (1,)), (()...  55.5 us
    all_to_all x1, blocking collectives, body(): lax.all_to_all(outgoing, 'local', split_axis=0, concat_axis=0, tiled=True)  52.9 us
    all_gather x1, waiting for transfers between devices, body(): up_piece = lax.all_gather(up_pre, 'node', axis=0, tiled=True)  43.5 us
    all_to_all x1, waiting for transfers between devices, body(): lax.all_to_all(back_rows, 'local', split_axis=0, concat_axis=0, tiled=True)  33 us
    psum x1, blocking collectives, body(): combine_slot = lax.psum(combine_part, 'node')  24.6 us
    another operation x3, other arithmetic  18.2 us
    all_to_all x1, blocking collectives, body(): lax.all_to_all(outgoing_gate, 'local', split_axis=0, concat_axis=0, tiled...  16.4 us
    all_to_all x1, starting transfers between devices, body(): lax.all_to_all(back_rows, 'local', split_axis=0, concat_axis=0, tiled=True)  12.9 us
  transfers between devices with their start and end apart: 5, of which 4 were waited for; matrix products, arithmetic and copies ran while one was open for 8% of the time, Pallas kernels for 0%

commit v1 on v0

v1 whole, which is shorter than its diff:
```python
import jax
import jax.numpy as jnp
from jax import lax
from jax.experimental import pallas as pl
from jax.experimental.pallas import tpu as pltpu
from jax.sharding import PartitionSpec as P

BF = jnp.bfloat16
F32 = jnp.float32
PAD = 24
WIDE = 512
GROUP = 16
EXTRA = 16


def call(kernel, outs, *operands, smem=0, scratch=()):
    spec = [pl.BlockSpec(memory_space=pltpu.SMEM)] * smem
    spec += [pl.BlockSpec(memory_space=pltpu.VMEM)] * (len(operands) - smem)
    return pl.pallas_call(
        kernel,
        out_shape=outs,
        in_specs=spec,
        out_specs=jax.tree.map(lambda _: pl.BlockSpec(memory_space=pltpu.VMEM), outs),
        scratch_shapes=list(scratch),
        compiler_params=pltpu.CompilerParams(vmem_limit_bytes=48 * 2**20),
    )(*operands)


def dot(a, b, dims):
    return lax.dot_general(a, b, (dims, ((), ())), preferred_element_type=F32)


NN = ((1,), (0,))
NT = ((1,), (1,))


def one_hot_rows(rank, experts, tokens):
    place = lax.broadcasted_iota(jnp.int32, (experts, PAD, tokens), 1).astype(F32)
    return jnp.where(rank[:, None, :] == place, 1.0, 0.0).astype(F32)


def packing(capacity, wide_first):
    tight, wide = GROUP * capacity, GROUP * PAD
    shape = (wide, tight) if wide_first else (tight, wide)
    r = lax.broadcasted_iota(jnp.int32, shape, 1 if wide_first else 0)
    q = lax.broadcasted_iota(jnp.int32, shape, 0 if wide_first else 1)
    source = jnp.zeros(shape, jnp.int32)
    for s in range(1, GROUP):
        source += jnp.where(r >= s * capacity, 1, 0)
    return jnp.where(q == r + source * (PAD - capacity), 1.0, 0.0).astype(BF)


def dispatch_kernel(ids_ref, gates_ref, grad_ref, send_ref, rank_ref):
    experts, tokens = rank_ref.shape
    expert = lax.broadcasted_iota(jnp.int32, (experts, tokens), 0)
    mask = jnp.zeros((experts, tokens), F32)
    weight = jnp.zeros((experts, tokens), F32)
    for k in range(ids_ref.shape[0]):
        hit = ids_ref[k : k + 1, :] == expert
        mask = jnp.where(hit, 1.0, mask)
        weight = jnp.where(hit, gates_ref[k : k + 1, :].astype(F32), weight)
    earlier = lax.broadcasted_iota(jnp.int32, (tokens, tokens), 0) < lax.broadcasted_iota(
        jnp.int32, (tokens, tokens), 1
    )
    rank = dot(mask.astype(BF), jnp.where(earlier, 1.0, 0.0).astype(BF), NN)
    rank = jnp.where(mask > 0.0, rank, -1.0)
    rank_ref[...] = rank
    pick = one_hot_rows(rank, experts, tokens)
    gate = jnp.sum(pick * weight[:, None, :], axis=2, keepdims=True)
    features = grad_ref.shape[0]
    flat = pick.reshape(experts * PAD, tokens).astype(BF)
    send_ref[:, :features] = dot(flat, grad_ref[...], NT).astype(BF)
    send_ref[:, features:] = jnp.broadcast_to(
        gate.reshape(experts * PAD, 1), (experts * PAD, WIDE - features)
    ).astype(BF)


def weights_kernel(core_ref, own_ref, other_ref, out_ref):
    core = core_ref[0]
    features, hidden = own_ref.shape
    half = hidden // 2
    for i, ref in enumerate((own_ref, other_ref)):
        rows = ref[...].astype(F32).T.reshape(hidden // 128, 128, features)
        rows = jnp.where(core == 0, rows[:, :64], rows[:, 64:])
        out_ref[i] = rows.reshape(half, features).astype(BF)


def sum_features_kernel(own_ref, other_ref, weight_ref, out_ref, gate_ref, rows_ref):
    features = weight_ref.shape[2]
    slots = out_ref.shape[1]
    groups = own_ref.shape[0] // (GROUP * PAD)
    tight, wide = slots // groups, GROUP * PAD
    pack = packing(tight // GROUP, False)
    for i, ref in enumerate((own_ref, other_ref)):
        for g in range(groups):
            rows_ref[i, g * tight : (g + 1) * tight, :] = dot(
                pack, ref[g * wide : (g + 1) * wide, :], NN
            ).astype(BF)
    total = dot(weight_ref[0], rows_ref[0, :, :features], NT)
    total += dot(weight_ref[1], rows_ref[1, :, :features], NT)
    out_ref[...] = total.astype(BF)
    lane = lax.broadcasted_iota(jnp.int32, (8, 128), 1)
    at = jnp.where(lane == features % 128, 1.0, 0.0).astype(BF)
    gate_ref[...] = dot(at, rows_ref[0, :, WIDE - 128 :], NT)


def hidden_kernel(parts_ref, gate_ref, up_ref, slot_gate_ref, out_ref):
    raw = parts_ref[0].astype(F32)
    for i in range(1, parts_ref.shape[0]):
        raw += parts_ref[i].astype(F32)
    g = gate_ref[...].astype(F32)
    u = up_ref[...].astype(F32)
    sigma = 1.0 / (1.0 + jnp.exp(-g))
    activ = g * sigma
    slope = sigma * (1.0 + g * (1.0 - sigma))
    combine = jnp.sum(raw * activ * u, axis=0, keepdims=True)
    scaled = raw * slot_gate_ref[0:1, :]
    units = g.shape[0]
    out_ref[:units, :] = (scaled * u * slope).astype(BF)
    out_ref[units : 2 * units, :] = (scaled * activ).astype(BF)
    high = combine.astype(BF).astype(F32)
    row = lax.broadcasted_iota(jnp.int32, (EXTRA, g.shape[1]), 0)
    extra = jnp.where(row == 0, high, jnp.where(row == 1, combine - high, 0.0))
    out_ref[2 * units :, :] = extra.astype(BF)


def input_kernel(all_ref, gate_ref, up_ref, out_ref, wide_ref, rows_ref):
    nodes, height, slots = all_ref.shape
    units = (height - EXTRA) // 2
    features = gate_ref.shape[0]
    gate_pre = all_ref[:, :units, :].reshape(nodes * units, slots)
    up_pre = all_ref[:, units : 2 * units, :].reshape(nodes * units, slots)
    wide_ref[:features, :slots] = dot(gate_ref[...], gate_pre, NN) + dot(up_ref[...], up_pre, NN)
    extra = all_ref[0, 2 * units :, :].astype(F32)
    for n in range(1, nodes):
        extra += all_ref[n, 2 * units :, :].astype(F32)
    wide_ref[features:, :slots] = jnp.broadcast_to(
        extra[0:1] + extra[1:2], (WIDE - features, slots)
    )
    spare = wide_ref.shape[1] - slots
    if spare:
        wide_ref[:, slots:] = jnp.zeros((WIDE, spare), F32)
    rows_ref[...] = wide_ref[...].T.astype(BF)
    groups = out_ref.shape[0] // (GROUP * PAD)
    tight, wide = slots // groups, GROUP * PAD
    unpack = packing(tight // GROUP, True)
    for g in range(groups):
        out_ref[g * wide : (g + 1) * wide, :] = dot(
            unpack, rows_ref[g * tight : (g + 1) * tight, :], NN
        ).astype(BF)


def collect_kernel(back_ref, rank_ref, ids_ref, grad_ref, combine_ref):
    experts, tokens = rank_ref.shape
    features = grad_ref.shape[0]
    pick = one_hot_rows(rank_ref[...], experts, tokens)
    turned = back_ref[...].astype(F32).T.astype(BF)
    flat = pick.reshape(experts * PAD, tokens).astype(BF)
    grad_ref[...] = dot(turned, flat, NN)[:features].astype(BF)
    column = back_ref[:, WIDE - 128 :].astype(F32)[:, features % 128 : features % 128 + 1]
    chosen = jnp.sum(pick * column.reshape(experts, PAD, 1), axis=1)
    expert = lax.broadcasted_iota(jnp.int32, (experts, tokens), 0)
    for k in range(ids_ref.shape[0]):
        hit = ids_ref[k : k + 1, :] == expert
        combine_ref[k : k + 1, :] = jnp.sum(jnp.where(hit, chosen, 0.0), axis=0, keepdims=True)


def body(out_grad, gate_weights, expert_ids, w_gate, w_up, w_down, saved_gate, saved_up):
    experts = lax.axis_size("local")
    nodes = lax.axis_size("node")
    tokens, features = out_grad.shape
    top = expert_ids.shape[1]
    units, slots = saved_gate.shape[1:]
    hidden = w_down.shape[1]
    shape = jax.ShapeDtypeStruct
    swap = [(i, i ^ 1) for i in range(nodes)]
    columns = [list(range(core, nodes, 2)) for core in range(2)]

    ids = expert_ids.T
    send, rank = call(
        dispatch_kernel,
        (shape((experts * PAD, WIDE), BF), shape((experts, tokens), F32)),
        ids,
        gate_weights.T,
        out_grad.T,
    )
    arrived = lax.all_to_all(
        send.reshape(experts, PAD, WIDE), "local", split_axis=0, concat_axis=0, tiled=True
    )
    down = w_down[0].T
    core = (lax.axis_index("node") % 2).astype(jnp.int32).reshape(1)
    weights = call(
        weights_kernel,
        shape((2, hidden // 2, features), BF),
        core,
        down,
        lax.ppermute(down, "node", swap),
        smem=1,
    )
    partner = lax.ppermute(arrived, "node", swap)
    partial, slot_gate = call(
        sum_features_kernel,
        (shape((hidden // 2, slots), BF), shape((8, slots), F32)),
        arrived.reshape(experts * PAD, WIDE),
        partner.reshape(experts * PAD, WIDE),
        weights,
        scratch=[pltpu.VMEM((2, slots, WIDE), BF)],
    )
    parts = lax.all_to_all(
        partial.reshape(nodes // 2, units, slots),
        "node",
        split_axis=0,
        concat_axis=0,
        tiled=True,
        axis_index_groups=columns,
    )
    piece = call(
        hidden_kernel,
        shape((2 * units + EXTRA, slots), BF),
        parts,
        saved_gate[0],
        saved_up[0],
        slot_gate,
    )
    gathered = lax.all_gather(piece, "node", axis=0, tiled=False)
    rounded = -(-slots // 128) * 128
    back = call(
        input_kernel,
        shape((experts * PAD, WIDE), BF),
        gathered,
        w_gate[0],
        w_up[0],
        scratch=[pltpu.VMEM((WIDE, rounded), F32), pltpu.VMEM((rounded, WIDE), BF)],
    )
    returned = lax.all_to_all(
        back.reshape(experts, PAD, WIDE), "local", split_axis=0, concat_axis=0, tiled=True
    )
    grad, combine = call(
        collect_kernel,
        (shape((features, tokens), BF), shape((top, tokens), F32)),
        returned.reshape(experts * PAD, WIDE),
        rank,
        ids,
    )
    return grad.T, combine.T.astype(BF)


def solution(mesh):
    in_specs = (
        P("local", "node"),
        P("local", None),
        P("local", None),
        P("local", "node", None),
        P("local", "node", None),
        P("local", None, "node"),
        P("local", "node", None),
        P("local", "node", None),
    )
    out_specs = (P("local", "node"), P("local", None))
    return jax.shard_map(body, mesh=mesh, in_specs=in_specs, out_specs=out_specs, check_vma=False)
```

time: 356 us -> 248 us (0.70)
  waiting for transfers between devices: 140 us -> 48.4 us
  blocking collectives: 93.9 us -> 162 us
  local copies, waits for them, and re-layouts: 46.1 us -> 2.28 us
  other arithmetic: 22.6 us -> 0.58 us
  starting transfers between devices: 25.3 us -> 4.36 us
  Pallas kernels: 0 us -> 15.5 us
  matrix products: 13.4 us -> 0 us
    all_to_all x2 -> x3, blocking collectives: 69.3 us -> 162 us  [the longest x1 54.9 us: body(): lax.all_to_all(partial.reshape(nodes // 2, units, slots), 'node', split_a...]
    reduce_scatter x1 -> x0, waiting for transfers between devices: 55.5 us -> none  [body(): lax.psum_scatter(lax.dot_general(down_part, slot_rows, (((1,), (1,)), (()...]
    all_to_all x2 -> x0, waiting for transfers between devices: 33 us -> none  [the longest x1 33 us: body(): lax.all_to_all(back_rows, 'local', split_axis=0, concat_axis=0, tiled=True)]
    all_to_all x2 -> x0, starting transfers between devices: 25.2 us -> none  [the longest x1 12.9 us: body(): lax.all_to_all(back_rows, 'local', split_axis=0, concat_axis=0, tiled=True)]
    psum x1 -> x0, blocking collectives: 24.6 us -> none  [body(): combine_slot = lax.psum(combine_part, 'node')]
    another operation x3 -> x0, other arithmetic: 18.2 us -> none
    pallas_call x0 -> x6, Pallas kernels: none -> 15.5 us  [call(): pl.pallas_call(kernel, out_shape=outs, in_specs=spec, out_specs=jax.tree....]
    scatter x2 -> x0, local copies, waits for them, and re-layouts: 13.9 us -> none  [the longest x1 7.59 us: body(): outgoing_gate.at[flat].set(gate_weights.reshape(-1))]
  transfers between devices with their start and end apart: 5 -> 3, of which waited for: 4 -> 2; matrix products, arithmetic and copies ran while one was open for 8% -> 0% of each run, Pallas kernels for 0% -> 1%
where the time goes in v1:
time: 248 us
  blocking collectives  162 us (65%)
  waiting for transfers between devices  48.4 us (20%)
  Pallas kernels  15.5 us (6%)
  between operations  14.1 us (6%)
  starting transfers between devices  4.36 us (2%)
    all_to_all x1, blocking collectives, body(): lax.all_to_all(partial.reshape(nodes // 2, units, slots), 'node', split_a...  54.9 us
    all_to_all x1, blocking collectives, body(): lax.all_to_all(back.reshape(experts, PAD, WIDE), 'local', split_axis=0, c...  54.3 us
    all_to_all x1, blocking collectives, body(): lax.all_to_all(send.reshape(experts, PAD, WIDE), 'local', split_axis=0, c...  53.1 us
    all_gather x1, waiting for transfers between devices, body(): gathered = lax.all_gather(piece, 'node', axis=0, tiled=False)  45.8 us
    pallas_call x6, Pallas kernels, call(): pl.pallas_call(kernel, out_shape=outs, in_specs=spec, out_specs=jax.tree....  15.5 us
  transfers between devices with their start and end apart: 3, of which 2 were waited for; matrix products, arithmetic and copies ran while one was open for 0% of the time, Pallas kernels for 1%

profile of v1, /device:TPU:22, one launch (start us, length us, event | category | flops | bytes accessed | tf_op | source)
XLA Modules:
  0.0 247.5 jit_solution(11058703151748675717)
XLA Ops:
  7.2 0.0 all-gather.3.cloned.1.call-start
  7.2 0.0 copy-start.4
  7.2 0.9 copy-done.4
  8.1 0.7 copy-done.5
  8.8 0.7 copy-done.7
  9.5 0.7 shard_map.95
  10.2 53.1 %all_to_all.15 = bf16[64,24,512]{2,1,0:T(8,128)(2,1)S(1)} all-to-all(bf16[64,24,512]{2,1,0:T(8,128)(2,1)S(1)} %bitcast.24), channel_id=1, replica_groups=mesh['node'=16,'local'=64] {'local'}, dimensions={0} | all-to-all | bytes 3145728 | tf_op jit(solution)/shard_map/all_to_all | solution.py:187
  63.3 1.9 collective-permute-start
  65.2 2.4 collective-permute-start.1
  67.6 2.6 %collective-permute-done.1.other_ref = bf16[448,1024]{1,0:T(8,128)(2,1)} collective-permute-done((bf16[448,1024]{1,0:T(8,128)(2,1)}, bf16[448,1024]{1,0:T(8,128)(2,1)}, u32[]{:S(2)}, u32[]{:S(2)}) %collective-permute-start.1) | collective-permute-done | bytes 917536 | tf_op jit(solution)/shard_map/ppermute | solution.py:197
  70.3 2.1 shard_map.96.weight_ref
  72.3 0.0 collective-permute-done
  72.3 3.3 %shard_map.97 = (bf16[512,1344]{1,0:T(8,128)(2,1)S(1)}, f32[8,1344]{1,0:T(8,128)S(1)}) custom-call(bf16[1536,512]{1,0:T(8,128)(2,1)S(1)} %bitcast.23, bf16[1536,512]{1,0:T(8,128)(2,1)S(1)} %bitcast.25, bf16[2,512,448]{2,1,0:T(8,128)(2,1)S(1)} %shard_map.96.weight_ref), custom_call_target="tpu_custom_call" | custom-call | tf_op jit(solution)/shard_map/pallas_call | solution.py:19
  75.7 54.9 %all_to_all.16.parts_ref = bf16[8,64,1344]{2,1,0:T(8,128)(2,1)S(1)} all-to-all(bf16[8,64,1344]{2,1,0:T(8,128)(2,1)S(1)} %bitcast.26), channel_id=1, replica_groups={{0,128,256,384,512,640,768,896},{64,192,320,448,576,704,832,960},{1,129..., dimensions={0} | all-to-all | bytes 2752512 | tf_op jit(solution)/shard_map/all_to_all | solution.py:209
  130.5 0.0 copy-done.3
  130.6 1.2 shard_map.98
  131.8 0.0 all-gather.3.cloned.1.call-update
  131.8 45.8 %all-gather.3.cloned.1.call-done = bf16[2304,1344]{1,0:T(8,128)(2,1)} async-done(((bf16[144,1344]{1,0:T(8,128)(2,1)}), bf16[2304,1344]{1,0:T(8,128)(2,1)}) %all-gather.3.cloned.1.call-update) | async-done | bytes 6193168 | tf_op jit(solution)/shard_map/all_gather | solution.py:225
  177.6 6.7 %shard_map.99 = bf16[1536,512]{1,0:T(8,128)(2,1)S(1)} custom-call(bf16[16,144,1344]{2,1,0:T(8,128)(2,1)} %bitcast.35, bf16[448,1024]{1,0:T(8,128)(2,1)S(1)} %bitcast.27, bf16[448,1024]{1,0:T(8,128)(2,1)S(1)} %bitcast.28), custom_call_target="tpu_custom_call" | custom-call | tf_op jit(solution)/shard_map/pallas_call | solution.py:19
  184.3 0.0 copy-start.6
  184.3 54.3 %all_to_all.17 = bf16[64,24,512]{2,1,0:T(8,128)(2,1)S(1)} all-to-all(bf16[64,24,512]{2,1,0:T(8,128)(2,1)S(1)} %bitcast.22), channel_id=1, replica_groups=mesh['node'=16,'local'=64] {'local'}, dimensions={0} | all-to-all | bytes 3145728 | tf_op jit(solution)/shard_map/all_to_all | solution.py:235
  238.5 0.0 copy-done.6
  238.5 1.6 shard_map.100
  240.1 0.6 convert_bitcast_fusion
  (9 shorter events, 0.0 us)
Async XLA Ops:
  7.2 170.4 %all-gather.3.cloned.1.call-start = ((), (), s32[]{:S(2)}) async-start(), calls=%async_computation.3 | async-start | bytes 6893568 | tf_op jit(solution)/shard_map/all_gather | solution.py:225
  7.2 0.9 copy-start.4
  8.1 0.7 copy-start.5
  8.8 0.7 copy-start.7
  63.3 9.0 %collective-permute-start = (bf16[64,24,512]{2,1,0:T(8,128)(2,1)S(1)}, bf16[64,24,512]{2,1,0:T(8,128)(2,1)S(1)}, u32[]{:S(2)}, u32[]{:S(2)}) collective-permute-start(bf16[64,24,512]{2,1,0:T(8,128)(2,1)S(1)} %all_to_all.15), channel_id=1, source_target_pairs={{0,64},{64,0},{128,192},{192,128},{256,320},{320,256},{384,448},{4... | collective-permute-start | bytes 4718600 | tf_op jit(solution)/shard_map/ppermute | solution.py:200
  65.2 5.0 %collective-permute-start.1 = (bf16[448,1024]{1,0:T(8,128)(2,1)}, bf16[448,1024]{1,0:T(8,128)(2,1)}, u32[]{:S(2)}, u32[]{:S(2)}) collective-permute-start(bf16[448,1024]{1,0:T(8,128)(2,1)} %bitcast.8.own_ref), channel_id=1, source_target_pairs={{0,64},{64,0},{128,192},{192,128},{256,320},{320,256},{384,448},{4... | collective-permute-start | bytes 2752520 | tf_op jit(solution)/shard_map/ppermute | solution.py:197
  75.7 54.9 %copy-start.2 = (bf16[1,64,1344]{2,1,0:T(8,128)(2,1)S(1)}, bf16[1,64,1344]{2,1,0:T(8,128)(2,1)}, u32[]{:S(2)}) copy-start(bf16[1,64,1344]{2,1,0:T(8,128)(2,1)} %param.14) | copy-start | bytes 516100
  75.7 54.9 %copy-start.3 = (bf16[1,64,1344]{2,1,0:T(8,128)(2,1)S(1)}, bf16[1,64,1344]{2,1,0:T(8,128)(2,1)}, u32[]{:S(2)}) copy-start(bf16[1,64,1344]{2,1,0:T(8,128)(2,1)} %param.15) | copy-start | bytes 516100
  130.5 47.0 %copy-start = (bf16[1,448,1024]{2,1,0:T(8,128)(2,1)S(1)}, bf16[1,448,1024]{2,1,0:T(8,128)(2,1)}, u32[]{:S(2)}) copy-start(bf16[1,448,1024]{2,1,0:T(8,128)(2,1)} %param.11) | copy-start | bytes 2752516
  130.5 47.0 %copy-start.1 = (bf16[1,448,1024]{2,1,0:T(8,128)(2,1)S(1)}, bf16[1,448,1024]{2,1,0:T(8,128)(2,1)}, u32[]{:S(2)}) copy-start(bf16[1,448,1024]{2,1,0:T(8,128)(2,1)} %param.12) | copy-start | bytes 2752516
  184.3 54.3 %copy-start.6 = (s32[128,8]{0,1:T(8,128)S(1)}, s32[128,8]{0,1:T(8,128)}, u32[]{:S(2)}) copy-start(s32[128,8]{0,1:T(8,128)} %param.10) | copy-start | bytes 12292
Sparse Core Ops, SparseCore 0:
  131.9 45.6 all-gather.2

commit v2 on v1

v2 whole, which is shorter than its diff:
```python
import functools

import jax
import jax.numpy as jnp
from jax import lax
from jax.experimental import pallas as pl
from jax.experimental.pallas import tpu as pltpu
from jax.sharding import PartitionSpec as P

BF = jnp.bfloat16
F32 = jnp.float32
LANES = 128
GROUP = 8
EXTRA = 16


def call(kernel, outs, *operands, smem=0, scratch=()):
    spec = [pl.BlockSpec(memory_space=pltpu.SMEM)] * smem
    spec += [pl.BlockSpec(memory_space=pltpu.VMEM)] * (len(operands) - smem)
    return pl.pallas_call(
        kernel,
        out_shape=outs,
        in_specs=spec,
        out_specs=jax.tree.map(lambda _: pl.BlockSpec(memory_space=pltpu.VMEM), outs),
        scratch_shapes=list(scratch),
        compiler_params=pltpu.CompilerParams(vmem_limit_bytes=48 * 2**20),
    )(*operands)


def dot(a, b, dims):
    return lax.dot_general(a, b, (dims, ((), ())), preferred_element_type=F32)


NN = ((1,), (0,))
NT = ((1,), (1,))


def layout(features, capacity):
    full = features // LANES
    scalars = full * capacity + (capacity + 1) // 2
    return full, scalars, -(-(scalars + 1) // 16) * 16


def place_codes(features, capacity):
    full, scalars, rows = layout(features, capacity)
    q = lax.broadcasted_iota(jnp.int32, (rows, LANES), 0)
    codes = []
    for c in range(full):
        at = q - c * capacity
        codes.append(jnp.where((at >= 0) & (at < capacity), at, -2))
    at = 2 * (q - full * capacity)
    tail = (at >= 0) & (q < scalars)
    codes.append(jnp.where(tail, at, -2))
    codes.append(jnp.where(tail & (at + 1 < capacity), at + 1, -2))
    return [code.astype(F32).astype(BF) for code in codes]


def picks(rank, features, capacity):
    experts, tokens = rank.shape
    one, zero = jnp.ones((), BF), jnp.zeros((), BF)
    place = rank.astype(BF)[:, None, :]
    out = []
    for code in place_codes(features, capacity):
        hit = jnp.where(place == code[None], one, zero)
        out.append(hit.reshape(experts * code.shape[0], tokens))
    return out


def slot_diagonal(height):
    j = lax.broadcasted_iota(jnp.int32, (1, height, LANES), 1)
    lane = lax.broadcasted_iota(jnp.int32, (1, height, LANES), 2)
    return jnp.where(j == lane, 1.0, 0.0).astype(F32)


def slot_of_row(shape, dim, capacity):
    r = lax.broadcasted_iota(jnp.int32, shape, dim)
    source = jnp.zeros(shape, jnp.int32)
    for s in range(1, GROUP):
        source += jnp.where(r >= s * capacity, 1, 0)
    return source, r - source * capacity


def packing(features, capacity, rows_first):
    full, scalars, rows = layout(features, capacity)
    tight, wide = GROUP * capacity, GROUP * rows
    shape = (wide, tight) if rows_first else (tight, wide)
    source, slot = slot_of_row(shape, 1 if rows_first else 0, capacity)
    at = lax.broadcasted_iota(jnp.int32, shape, 0 if rows_first else 1) - source * rows
    targets = [slot + c * capacity for c in range(full)]
    targets += [lax.shift_right_logical(slot, 1) + full * capacity, scalars]
    return [jnp.where(at == target, 1.0, 0.0).astype(BF) for target in targets]


def odd(slot):
    return (slot & 1) == 1


def dispatch_kernel(capacity, ids_ref, gates_ref, grad_ref, send_ref, rank_ref):
    experts, tokens = rank_ref.shape
    features = grad_ref.shape[0]
    full, scalars, rows = layout(features, capacity)
    expert = lax.broadcasted_iota(jnp.int32, (experts, tokens), 0)
    mask = jnp.zeros((experts, tokens), F32)
    weight = jnp.zeros((experts, tokens), F32)
    for k in range(ids_ref.shape[0]):
        hit = ids_ref[k : k + 1, :] == expert
        mask = jnp.where(hit, 1.0, mask)
        weight = jnp.where(hit, gates_ref[k : k + 1, :].astype(F32), weight)
    earlier = lax.broadcasted_iota(jnp.int32, (tokens, tokens), 0) < lax.broadcasted_iota(
        jnp.int32, (tokens, tokens), 1
    )
    rank = dot(mask.astype(BF), jnp.where(earlier, 1.0, 0.0).astype(BF), NN)
    rank = jnp.where(mask > 0.0, rank, -1.0)
    rank_ref[...] = rank
    height = -(-capacity // 8) * 8
    j = lax.broadcasted_iota(jnp.int32, (experts, height, tokens), 1).astype(F32)
    gate = jnp.where(rank[:, None, :] == j, weight[:, None, :], 0.0)
    gate = jnp.sum(gate, axis=2, keepdims=True)
    gate = jnp.sum(gate * slot_diagonal(height), axis=1, keepdims=True)
    tail = grad_ref[full * LANES :, :]
    empty = jnp.zeros((LANES - tail.shape[0], tokens), BF)
    pieces = [grad_ref[c * LANES : (c + 1) * LANES, :] for c in range(full)]
    pieces += [jnp.concatenate([tail, empty], axis=0), jnp.concatenate([empty, tail], axis=0)]
    total = jnp.zeros((experts * rows, LANES), F32)
    for pick, piece in zip(picks(rank, features, capacity), pieces):
        total += dot(pick, piece, NT)
    q = lax.broadcasted_iota(jnp.int32, (experts, rows, LANES), 1)
    total = jnp.where(q == scalars, gate, total.reshape(experts, rows, LANES))
    send_ref[...] = total.reshape(experts * rows, LANES).astype(BF)


def weights_kernel(core_ref, down_ref, out_ref):
    core = core_ref[0]
    features, hidden = down_ref.shape
    half = hidden // 2
    rows = down_ref[...].astype(F32).T.reshape(hidden // LANES, LANES, features)
    low, high = rows[:, :64], rows[:, 64:]
    out_ref[0] = jnp.where(core == 0, low, high).reshape(half, features).astype(BF)
    out_ref[1] = jnp.where(core == 0, high, low).reshape(half, features).astype(BF)


def other_half_kernel(capacity, arrived_ref, weight_ref, out_ref, rows_ref, gate_ref):
    features = weight_ref.shape[2]
    full, _, rows = layout(features, capacity)
    tight, wide = GROUP * capacity, GROUP * rows
    groups = arrived_ref.shape[0] // wide
    packs = packing(features, capacity, False)
    _, slot = slot_of_row((tight, LANES), 0, capacity)
    lane = lax.broadcasted_iota(jnp.int32, (tight, LANES), 1)
    for g in range(0, groups, 2):
        pair = jnp.concatenate(
            [arrived_ref[h * wide : (h + 1) * wide, :] for h in (g, g + 1)], axis=1
        )
        at = slice(g * tight, (g + 2) * tight)
        got = [dot(pack, pair, NN) for pack in packs]
        for c in range(full + 1):
            halves = []
            for h in range(2):
                piece = got[c][:, h * LANES : (h + 1) * LANES]
                if c == full:
                    gates = got[full + 1][:, h * LANES : (h + 1) * LANES]
                    gate = jnp.sum(jnp.where(lane == slot, gates, 0.0), axis=1, keepdims=True)
                    piece = jnp.where(odd(slot), pltpu.roll(piece, 64, 1), piece)
                    piece = jnp.where(lane < 64, piece, gate)
                halves.append(piece)
            rows_ref[at, c * LANES : (c + 1) * LANES] = jnp.concatenate(halves, axis=0).astype(BF)
    out_ref[...] = dot(weight_ref[1], rows_ref[:, :features], NT).astype(BF)
    lane = lax.broadcasted_iota(jnp.int32, (8, LANES), 1)
    at = jnp.where(lane == 64, 1.0, 0.0).astype(BF)
    gate_ref[...] = dot(at, rows_ref[:, full * LANES :], NT)


def own_half_kernel(rows_ref, weight_ref, partner_ref, out_ref):
    features = weight_ref.shape[2]
    total = dot(weight_ref[0], rows_ref[:, :features], NT)
    out_ref[...] = (total + partner_ref[...].astype(F32)).astype(BF)


def hidden_kernel(parts_ref, gate_ref, up_ref, slot_gate_ref, out_ref):
    raw = parts_ref[0].astype(F32)
    for i in range(1, parts_ref.shape[0]):
        raw += parts_ref[i].astype(F32)
    g = gate_ref[...].astype(F32)
    u = up_ref[...].astype(F32)
    sigma = 1.0 / (1.0 + jnp.exp(-g))
    activ = g * sigma
    slope = sigma * (1.0 + g * (1.0 - sigma))
    combine = jnp.sum(raw * activ * u, axis=0, keepdims=True)
    scaled = raw * slot_gate_ref[0:1, :]
    units = g.shape[0]
    out_ref[:units, :] = (scaled * u * slope).astype(BF)
    out_ref[units : 2 * units, :] = (scaled * activ).astype(BF)
    high = combine.astype(BF).astype(F32)
    row = lax.broadcasted_iota(jnp.int32, (EXTRA, g.shape[1]), 0)
    extra = jnp.where(row == 0, high, jnp.where(row == 1, combine - high, 0.0))
    out_ref[2 * units :, :] = extra.astype(BF)


def input_kernel(capacity, all_ref, gate_ref, up_ref, out_ref, wide_ref, rows_ref):
    nodes, height, slots = all_ref.shape
    units = (height - EXTRA) // 2
    features = gate_ref.shape[0]
    gate_pre = all_ref[:, :units, :].reshape(nodes * units, slots)
    up_pre = all_ref[:, units : 2 * units, :].reshape(nodes * units, slots)
    wide_ref[:features, :slots] = dot(gate_ref[...], gate_pre, NN) + dot(up_ref[...], up_pre, NN)
    extra = all_ref[0, 2 * units :, :].astype(F32)
    for n in range(1, nodes):
        extra += all_ref[n, 2 * units :, :].astype(F32)
    spare = wide_ref.shape[0] - features
    wide_ref[features:, :slots] = jnp.broadcast_to(extra[0:1] + extra[1:2], (spare, slots))
    beyond = wide_ref.shape[1] - slots
    if beyond:
        wide_ref[:, slots:] = jnp.zeros((wide_ref.shape[0], beyond), F32)
    rows_ref[...] = wide_ref[...].T
    full, _, rows = layout(features, capacity)
    tight, wide = GROUP * capacity, GROUP * rows
    groups = slots // tight
    packs = packing(features, capacity, True)
    _, slot = slot_of_row((tight, LANES), 0, capacity)
    lane = lax.broadcasted_iota(jnp.int32, (tight, LANES), 1)
    for g in range(0, groups, 2):
        pieces = []
        for h in (g, g + 1):
            at = slice(h * tight, (h + 1) * tight)
            mine = [rows_ref[at, c * LANES : (c + 1) * LANES] for c in range(full + 1)]
            tail = mine.pop()
            turned = pltpu.roll(tail, 64, 1)
            mine.append(jnp.where((lane >= 64) == odd(slot), jnp.where(odd(slot), turned, tail), 0.0))
            scalar = jnp.where(lane < 64, turned, tail)
            mine.append(jnp.where(lane == slot, scalar, 0.0))
            pieces.append([piece.astype(BF) for piece in mine])
        total = jnp.zeros((wide, 2 * LANES), F32)
        for pack, low, high in zip(packs, *pieces):
            total += dot(pack, jnp.concatenate([low, high], axis=1), NN)
        for h in range(2):
            out_ref[(g + h) * wide : (g + h + 1) * wide, :] = total[
                :, h * LANES : (h + 1) * LANES
            ].astype(BF)


def collect_kernel(capacity, back_ref, rank_ref, ids_ref, grad_ref, combine_ref):
    experts, tokens = rank_ref.shape
    features = grad_ref.shape[0]
    full, scalars, rows = layout(features, capacity)
    rank = rank_ref[...]
    values = back_ref[...].astype(F32)
    turned = values.T.astype(BF)
    sums = [dot(turned, pick, NN) for pick in picks(rank, features, capacity)]
    for c in range(full):
        grad_ref[c * LANES : (c + 1) * LANES, :] = sums[c].astype(BF)
    grad_ref[full * LANES :, :] = (sums[full][:64] + sums[full + 1][64:]).astype(BF)
    height = -(-capacity // 8) * 8
    carried = values.reshape(experts, rows, LANES)[:, scalars : scalars + 1, :]
    column = jnp.sum(carried * slot_diagonal(height), axis=2, keepdims=True)
    j = lax.broadcasted_iota(jnp.int32, (experts, height, tokens), 1).astype(F32)
    chosen = jnp.sum(jnp.where(rank[:, None, :] == j, column, 0.0), axis=1)
    expert = lax.broadcasted_iota(jnp.int32, (experts, tokens), 0)
    for k in range(ids_ref.shape[0]):
        hit = ids_ref[k : k + 1, :] == expert
        combine_ref[k : k + 1, :] = jnp.sum(jnp.where(hit, chosen, 0.0), axis=0, keepdims=True)


def body(out_grad, gate_weights, expert_ids, w_gate, w_up, w_down, saved_gate, saved_up):
    experts = lax.axis_size("local")
    nodes = lax.axis_size("node")
    tokens, features = out_grad.shape
    top = expert_ids.shape[1]
    units, slots = saved_gate.shape[1:]
    hidden = w_down.shape[1]
    shape = jax.ShapeDtypeStruct
    swap = [(i, i ^ 1) for i in range(nodes)]
    columns = [list(range(core, nodes, 2)) for core in range(2)]

    capacity = slots // experts
    rows = layout(features, capacity)[2]
    lanes = -(-features // LANES) * LANES
    ids = expert_ids.T
    send, rank = call(
        functools.partial(dispatch_kernel, capacity),
        (shape((experts * rows, LANES), BF), shape((experts, tokens), F32)),
        ids,
        gate_weights.T,
        out_grad.T,
    )
    arrived = lax.all_to_all(
        send.reshape(experts, rows, LANES), "local", split_axis=0, concat_axis=0, tiled=True
    )
    core = (lax.axis_index("node") % 2).astype(jnp.int32).reshape(1)
    weights = call(
        weights_kernel, shape((2, hidden // 2, features), BF), core, w_down[0].T, smem=1
    )
    other, packed, slot_gate = call(
        functools.partial(other_half_kernel, capacity),
        (shape((hidden // 2, slots), BF), shape((slots, lanes), BF), shape((8, slots), F32)),
        arrived.reshape(experts * rows, LANES),
        weights,
    )
    partial = call(
        own_half_kernel,
        shape((hidden // 2, slots), BF),
        packed,
        weights,
        lax.ppermute(other, "node", swap),
    )
    parts = lax.all_to_all(
        partial.reshape(nodes // 2, units, slots),
        "node",
        split_axis=0,
        concat_axis=0,
        tiled=True,
        axis_index_groups=columns,
    )
    piece = call(
        hidden_kernel,
        shape((2 * units + EXTRA, slots), BF),
        parts,
        saved_gate[0],
        saved_up[0],
        slot_gate,
    )
    gathered = lax.all_gather(piece, "node", axis=0, tiled=False)
    rounded = -(-slots // 128) * 128
    back = call(
        functools.partial(input_kernel, capacity),
        shape((experts * rows, LANES), BF),
        gathered,
        w_gate[0],
        w_up[0],
        scratch=[pltpu.VMEM((lanes, rounded), F32), pltpu.VMEM((rounded, lanes), F32)],
    )
    returned = lax.all_to_all(
        back.reshape(experts, rows, LANES), "local", split_axis=0, concat_axis=0, tiled=True
    )
    grad, combine = call(
        functools.partial(collect_kernel, capacity),
        (shape((features, tokens), BF), shape((top, tokens), F32)),
        returned.reshape(experts * rows, LANES),
        rank,
        ids,
    )
    return grad.T, combine.T.astype(BF)


def solution(mesh):
    in_specs = (
        P("local", "node"),
        P("local", None),
        P("local", None),
        P("local", "node", None),
        P("local", "node", None),
        P("local", None, "node"),
        P("local", "node", None),
        P("local", "node", None),
    )
    out_specs = (P("local", "node"), P("local", None))
    return jax.shard_map(body, mesh=mesh, in_specs=in_specs, out_specs=out_specs, check_vma=False)
```

time: 248 us -> 244 us (0.984)
  the two profiles are of different devices: /device:TPU:22 before, /device:TPU:4 now
where the time goes in v2:
time: 244 us
  blocking collectives  102 us (42%)
  waiting for transfers between devices  79.4 us (33%)
  starting transfers between devices  19.3 us (8%)
  Pallas kernels  17.5 us (7%)
  between operations  14.2 us (6%)
  local copies, waits for them, and re-layouts  10.3 us (4%)
    all_to_all x1, blocking collectives, body(): lax.all_to_all(partial.reshape(nodes // 2, units, slots), 'node', split_a...  53.8 us
    all_to_all x1, blocking collectives, body(): lax.all_to_all(back.reshape(experts, rows, LANES), 'local', split_axis=0,...  48.7 us
    all_gather x1, waiting for transfers between devices, body(): gathered = lax.all_gather(piece, 'node', axis=0, tiled=False)  44.4 us
    all_to_all x1, waiting for transfers between devices, body(): lax.all_to_all(send.reshape(experts, rows, LANES), 'local', split_axis=0,...  31.7 us
    pallas_call x7, Pallas kernels, call(): pl.pallas_call(kernel, out_shape=outs, in_specs=spec, out_specs=jax.tree....  17.5 us
    all_to_all x1, starting transfers between devices, body(): lax.all_to_all(send.reshape(experts, rows, LANES), 'local', split_axis=0,...  17.4 us
    unnamed x26, local copies, waits for them, and re-layouts  6.91 us
  transfers between devices with their start and end apart: 3, of which 3 were waited for; matrix products, arithmetic and copies ran while one was open for 0% of the time, Pallas kernels for 0%

profile of v2, /device:TPU:4, one launch (start us, length us, event | category | flops | bytes accessed | tf_op | source)
XLA Modules:
  0.0 243.8 jit_solution(12134638888556052418)
XLA Ops:
  7.2 0.9 copy-done.9
  8.1 0.7 copy-done.10
  8.8 0.7 copy-done.12
  9.4 2.1 shard_map.95
  11.5 1.1 copy-done.3
  12.6 17.4 %all-to-all-start = ((bf16[64,80,128]{2,1,0:T(8,128)(2,1)}), bf16[64,80,128]{2,1,0:T(8,128)(2,1)S(1)}, u32[]{:S(2)}, u32[]{:S(2)}) async-start(bf16[64,80,128]{2,1,0:T(8,128)(2,1)} %bitcast.24), calls=%async_computation | async-start | bytes 2621440 | tf_op jit(solution)/shard_map/all_to_all | solution.py:285
  30.0 0.4 shard_map.96.weight_ref
  30.4 31.7 %all-to-all-done = bf16[64,80,128]{2,1,0:T(8,128)(2,1)S(1)} async-done(((bf16[64,80,128]{2,1,0:T(8,128)(2,1)}), bf16[64,80,128]{2,1,0:T(8,128)(2,1)S(1)}, u32[]{:S(2)}, u32[]{:S(2)}) %all-to-all-start) | async-done | bytes 1310752 | tf_op jit(solution)/shard_map/all_to_all | solution.py:285
  62.2 2.5 %shard_map.97 = (bf16[512,1344]{1,0:T(8,128)(2,1)S(1)}, bf16[1344,512]{1,0:T(8,128)(2,1)S(1)}, f32[8,1344]{1,0:T(8,128)S(1)}) custom-call(bf16[5120,128]{1,0:T(8,128)(2,1)S(1)} %bitcast.22, bf16[2,512,448]{2,1,0:T(8,128)(2,1)S(1)} %shard_map.96.weight_ref), custom_call_target="tpu_custom_call" | custom-call | tf_op jit(solution)/shard_map/pallas_call | solution.py:20
  64.7 1.1 copy-done
  65.8 1.1 copy-done.1
  66.9 1.6 copy.10
  68.5 1.9 collective-permute-start
  70.5 3.2 %collective-permute-done = bf16[512,1344]{0,1:T(8,128)(2,1)} collective-permute-done((bf16[512,1344]{0,1:T(8,128)(2,1)S(1)}, bf16[512,1344]{0,1:T(8,128)(2,1)}, u32[]{:S(2)}, u32[]{:S(2)}) %collective-permute-start) | collective-permute-done | bytes 1376288 | tf_op jit(solution)/shard_map/ppermute | solution.py:303
  73.7 1.8 copy.11.partner_ref
  75.5 1.3 copy-done.2
  76.8 1.0 shard_map.98
  77.9 53.8 %all_to_all.15.parts_ref = bf16[8,64,1344]{2,1,0:T(8,128)(2,1)S(1)} all-to-all(bf16[8,64,1344]{2,1,0:T(8,128)(2,1)S(1)} %bitcast.20), channel_id=1, replica_groups={{0,128,256,384,512,640,768,896},{64,192,320,448,576,704,832,960},{1,129..., dimensions={0} | all-to-all | bytes 2752512 | tf_op jit(solution)/shard_map/all_to_all | solution.py:305
  131.7 1.2 shard_map.99
  132.9 44.4 %all-gather.3.cloned.1.call-done = bf16[2304,1344]{1,0:T(8,128)(2,1)} async-done(((bf16[144,1344]{1,0:T(8,128)(2,1)}), bf16[2304,1344]{1,0:T(8,128)(2,1)}) %all-gather.3.cloned.1.call-update) | async-done | bytes 6193168 | tf_op jit(solution)/shard_map/all_gather | solution.py:321
  177.3 7.6 %shard_map.100 = bf16[5120,128]{1,0:T(8,128)(2,1)S(1)} custom-call(bf16[16,144,1344]{2,1,0:T(8,128)(2,1)} %bitcast.34, bf16[448,1024]{1,0:T(8,128)(2,1)S(1)} %bitcast.25, bf16[448,1024]{1,0:T(8,128)(2,1)S(1)} %bitcast.26), custom_call_target="tpu_custom_call" | custom-call | tf_op jit(solution)/shard_map/pallas_call | solution.py:20
  185.0 48.7 %all_to_all.16 = bf16[64,80,128]{2,1,0:T(8,128)(2,1)S(1)} all-to-all(bf16[64,80,128]{2,1,0:T(8,128)(2,1)S(1)} %bitcast.21), channel_id=1, replica_groups=mesh['node'=16,'local'=64] {'local'}, dimensions={0} | all-to-all | bytes 2621440 | tf_op jit(solution)/shard_map/all_to_all | solution.py:331
  233.6 2.7 %shard_map.101 = (bf16[448,128]{1,0:T(8,128)(2,1)}, f32[8,128]{1,0:T(8,128)S(1)}) custom-call(bf16[5120,128]{1,0:T(8,128)(2,1)S(1)} %bitcast.23, f32[64,128]{1,0:T(8,128)S(1)} %get-tuple-element.13.rank_ref, s32[8,128]{1,0:T(8,128)S(1)} %bitcast.32), custom_call_target="tpu_custom_call" | custom-call | tf_op jit(solution)/shard_map/pallas_call | solution.py:20
  236.3 0.6 convert_bitcast_fusion
  (21 shorter events, 0.1 us)
Async XLA Ops:
  7.2 0.9 copy-start.9
  8.1 0.7 copy-start.10
  8.8 0.7 copy-start.12
  9.4 20.6 %copy-start.6 = (bf16[1,1024,448]{1,2,0:T(8,128)(2,1)S(1)}, bf16[1,1024,448]{1,2,0:T(8,128)(2,1)}, u32[]{:S(2)}) copy-start(bf16[1,1024,448]{1,2,0:T(8,128)(2,1)} %param.13) | copy-start | bytes 2752516
  11.5 1.1 copy-start.3
  12.6 49.6 %all-to-all-start = ((bf16[64,80,128]{2,1,0:T(8,128)(2,1)}), bf16[64,80,128]{2,1,0:T(8,128)(2,1)S(1)}, u32[]{:S(2)}, u32[]{:S(2)}) async-start(bf16[64,80,128]{2,1,0:T(8,128)(2,1)} %bitcast.24), calls=%async_computation | async-start | bytes 2621440 | tf_op jit(solution)/shard_map/all_to_all | solution.py:285
  30.0 147.4 %all-gather.3.cloned.1.call-start = ((), (), s32[]{:S(2)}) async-start(), calls=%async_computation.3 | async-start | bytes 6893568 | tf_op jit(solution)/shard_map/all_gather | solution.py:321
  64.7 1.1 copy-start
  65.8 1.1 copy-start.1
  68.5 5.2 %collective-permute-start = (bf16[512,1344]{0,1:T(8,128)(2,1)S(1)}, bf16[512,1344]{0,1:T(8,128)(2,1)}, u32[]{:S(2)}, u32[]{:S(2)}) collective-permute-start(bf16[512,1344]{0,1:T(8,128)(2,1)S(1)} %copy.10), channel_id=1, source_target_pairs={{0,64},{64,0},{128,192},{192,128},{256,320},{320,256},{384,448},{4... | collective-permute-start | bytes 4128776 | tf_op jit(solution)/shard_map/ppermute | solution.py:303
  75.5 1.3 copy-start.2
  77.9 53.8 %copy-start.7 = (bf16[1,64,1344]{2,1,0:T(8,128)(2,1)S(1)}, bf16[1,64,1344]{2,1,0:T(8,128)(2,1)}, u32[]{:S(2)}) copy-start(bf16[1,64,1344]{2,1,0:T(8,128)(2,1)} %param.14) | copy-start | bytes 516100
  77.9 53.8 %copy-start.8 = (bf16[1,64,1344]{2,1,0:T(8,128)(2,1)S(1)}, bf16[1,64,1344]{2,1,0:T(8,128)(2,1)}, u32[]{:S(2)}) copy-start(bf16[1,64,1344]{2,1,0:T(8,128)(2,1)} %param.15) | copy-start | bytes 516100
  131.7 45.6 %copy-start.4 = (bf16[1,448,1024]{2,1,0:T(8,128)(2,1)S(1)}, bf16[1,448,1024]{2,1,0:T(8,128)(2,1)}, u32[]{:S(2)}) copy-start(bf16[1,448,1024]{2,1,0:T(8,128)(2,1)} %param.11) | copy-start | bytes 2752516
  131.7 45.6 %copy-start.5 = (bf16[1,448,1024]{2,1,0:T(8,128)(2,1)S(1)}, bf16[1,448,1024]{2,1,0:T(8,128)(2,1)}, u32[]{:S(2)}) copy-start(bf16[1,448,1024]{2,1,0:T(8,128)(2,1)} %param.12) | copy-start | bytes 2752516
  185.0 48.7 %copy-start.11 = (s32[128,8]{0,1:T(8,128)S(1)}, s32[128,8]{0,1:T(8,128)}, u32[]{:S(2)}) copy-start(s32[128,8]{0,1:T(8,128)} %param.10) | copy-start | bytes 12292
Sparse Core Ops, SparseCore 0:
  133.0 44.2 all-gather.2

commit v3 on v2

--- a/solution.py
+++ b/solution.py
@@ -14,16 +14,17 @@
 EXTRA = 16
 
 
-def call(kernel, outs, *operands, smem=0, scratch=()):
+def call(kernel, outs, *operands, smem=0, scratch=(), plain=False):
+    vmem = pl.BlockSpec() if plain else pl.BlockSpec(memory_space=pltpu.VMEM)
     spec = [pl.BlockSpec(memory_space=pltpu.SMEM)] * smem
-    spec += [pl.BlockSpec(memory_space=pltpu.VMEM)] * (len(operands) - smem)
+    spec += [vmem] * (len(operands) - smem)
     return pl.pallas_call(
         kernel,
         out_shape=outs,
         in_specs=spec,
-        out_specs=jax.tree.map(lambda _: pl.BlockSpec(memory_space=pltpu.VMEM), outs),
+        out_specs=jax.tree.map(lambda _: vmem, outs),
         scratch_shapes=list(scratch),
-        compiler_params=pltpu.CompilerParams(vmem_limit_bytes=48 * 2**20),
+        compiler_params=pltpu.CompilerParams(vmem_limit_bytes=32 * 2**20),
     )(*operands)
 
 
@@ -129,14 +130,18 @@
     send_ref[...] = total.reshape(experts * rows, LANES).astype(BF)
 
 
-def weights_kernel(core_ref, down_ref, out_ref):
-    core = core_ref[0]
+def weights_kernel(place_ref, down_ref, out_ref, rows_ref):
+    core, start = place_ref[0], place_ref[1]
     features, hidden = down_ref.shape
-    half = hidden // 2
-    rows = down_ref[...].astype(F32).T.reshape(hidden // LANES, LANES, features)
+    blocks = hidden // LANES
+    rows = down_ref[...].astype(F32).T.reshape(blocks, LANES, features)
     low, high = rows[:, :64], rows[:, 64:]
-    out_ref[0] = jnp.where(core == 0, low, high).reshape(half, features).astype(BF)
-    out_ref[1] = jnp.where(core == 0, high, low).reshape(half, features).astype(BF)
+    rows_ref[0] = jnp.where(core == 0, low, high)
+    rows_ref[1] = jnp.where(core == 0, high, low)
+    for step in range(blocks):
+        block = lax.rem(start + step, blocks)
+        for half in range(2):
+            out_ref[half, step * 64 : (step + 1) * 64, :] = rows_ref[half, block].astype(BF)
 
 
 def other_half_kernel(capacity, arrived_ref, weight_ref, out_ref, rows_ref, gate_ref):
@@ -164,22 +169,32 @@
                     piece = jnp.where(lane < 64, piece, gate)
                 halves.append(piece)
             rows_ref[at, c * LANES : (c + 1) * LANES] = jnp.concatenate(halves, axis=0).astype(BF)
-    out_ref[...] = dot(weight_ref[1], rows_ref[:, :features], NT).astype(BF)
+    slots = rows_ref.shape[0]
+    out_ref[:, :slots] = dot(weight_ref[1], rows_ref[:, :features], NT).astype(BF)
+    if out_ref.shape[1] > slots:
+        out_ref[:, slots:] = jnp.zeros((out_ref.shape[0], out_ref.shape[1] - slots), BF)
     lane = lax.broadcasted_iota(jnp.int32, (8, LANES), 1)
     at = jnp.where(lane == 64, 1.0, 0.0).astype(BF)
     gate_ref[...] = dot(at, rows_ref[:, full * LANES :], NT)
 
 
-def own_half_kernel(rows_ref, weight_ref, partner_ref, out_ref):
+def own_half_kernel(rows_ref, weight_ref, partner_ref, *out_refs):
     features = weight_ref.shape[2]
-    total = dot(weight_ref[0], rows_ref[:, :features], NT)
-    out_ref[...] = (total + partner_ref[...].astype(F32)).astype(BF)
-
-
-def hidden_kernel(parts_ref, gate_ref, up_ref, slot_gate_ref, out_ref):
-    raw = parts_ref[0].astype(F32)
-    for i in range(1, parts_ref.shape[0]):
-        raw += parts_ref[i].astype(F32)
+    slots = rows_ref.shape[0]
+    units = out_refs[0].shape[0]
+    total = dot(weight_ref[0], rows_ref[:, :features], NT) + partner_ref[:, :slots].astype(F32)
+    for step, out_ref in enumerate(out_refs):
+        out_ref[:, :slots] = total[step * units : (step + 1) * units].astype(out_ref.dtype)
+        if out_ref.shape[1] > slots:
+            out_ref[:, slots:] = jnp.zeros((units, out_ref.shape[1] - slots), out_ref.dtype)
+
+
+def hidden_kernel(gate_ref, up_ref, slot_gate_ref, *refs):
+    *parts, out_ref = refs
+    slots = gate_ref.shape[1]
+    raw = parts[0][:, :slots].astype(F32)
+    for part in parts[1:]:
+        raw += part[:, :slots].astype(F32)
     g = gate_ref[...].astype(F32)
     u = up_ref[...].astype(F32)
     sigma = 1.0 / (1.0 + jnp.exp(-g))
@@ -269,7 +284,6 @@
     hidden = w_down.shape[1]
     shape = jax.ShapeDtypeStruct
     swap = [(i, i ^ 1) for i in range(nodes)]
-    columns = [list(range(core, nodes, 2)) for core in range(2)]
 
     capacity = slots // experts
     rows = layout(features, capacity)[2]
@@ -281,45 +295,48 @@
         ids,
         gate_weights.T,
         out_grad.T,
+        plain=True,
     )
     arrived = lax.all_to_all(
         send.reshape(experts, rows, LANES), "local", split_axis=0, concat_axis=0, tiled=True
     )
-    core = (lax.axis_index("node") % 2).astype(jnp.int32).reshape(1)
+    node = lax.axis_index("node")
     weights = call(
-        weights_kernel, shape((2, hidden // 2, features), BF), core, w_down[0].T, smem=1
-    )
+        weights_kernel,
+        shape((2, hidden // 2, features), BF),
+        jnp.stack([node % 2, node // 2]).astype(jnp.int32),
+        w_down[0].T,
+        smem=1,
+        scratch=[pltpu.VMEM((2, hidden // LANES, 64, features), F32)],
+    )
+    rounded = -(-slots // LANES) * LANES
     other, packed, slot_gate = call(
         functools.partial(other_half_kernel, capacity),
-        (shape((hidden // 2, slots), BF), shape((slots, lanes), BF), shape((8, slots), F32)),
+        (shape((hidden // 2, rounded), BF), shape((slots, lanes), BF), shape((8, slots), F32)),
         arrived.reshape(experts * rows, LANES),
         weights,
     )
-    partial = call(
+    depth = nodes // 2
+    own, *others = call(
         own_half_kernel,
-        shape((hidden // 2, slots), BF),
+        [shape((units, rounded), BF if step else F32) for step in range(depth)],
         packed,
         weights,
         lax.ppermute(other, "node", swap),
     )
-    parts = lax.all_to_all(
-        partial.reshape(nodes // 2, units, slots),
-        "node",
-        split_axis=0,
-        concat_axis=0,
-        tiled=True,
-        axis_index_groups=columns,
-    )
+    parts = [own]
+    for step in sorted(range(1, depth), key=lambda step: -min(step, depth - step)):
+        onward = [(n, (n + 2 * step) % nodes) for n in range(nodes)]
+        parts.append(lax.ppermute(others[step - 1], "node", onward))
     piece = call(
         hidden_kernel,
         shape((2 * units + EXTRA, slots), BF),
-        parts,
         saved_gate[0],
         saved_up[0],
         slot_gate,
+        *parts,
     )
     gathered = lax.all_gather(piece, "node", axis=0, tiled=False)
-    rounded = -(-slots // 128) * 128
     back = call(
         functools.partial(input_kernel, capacity),
         shape((experts * rows, LANES), BF),

time: 244 us -> 235 us (0.963)
  blocking collectives: 102 us -> 48.7 us
  starting transfers between devices: 19.3 us -> 56.6 us
  waiting for transfers between devices: 79.4 us -> 92.8 us
  local copies, waits for them, and re-layouts: 10.3 us -> 5.12 us
    all_to_all x1 -> x0, blocking collectives: 53.8 us -> none  [body(): lax.all_to_all(partial.reshape(nodes // 2, units, slots), 'node', split_a...]
    ppermute x0 -> x7, starting transfers between devices: none -> 37.3 us  [body(): parts.append(lax.ppermute(others[step - 1], 'node', onward))]
    ppermute x0 -> x7, waiting for transfers between devices: none -> 11.6 us  [body(): parts.append(lax.ppermute(others[step - 1], 'node', onward))]
    all_gather x1, waiting for transfers between devices: 44.4 us -> 47 us  [body(): gathered = lax.all_gather(piece, 'node', axis=0, tiled=False)]
    unnamed x26 -> x20, local copies, waits for them, and re-layouts: 6.91 us -> 5.12 us
  transfers between devices with their start and end apart: 3 -> 10, of which waited for: 3 -> 7; matrix products, arithmetic and copies ran while one was open for 0% -> 0% of each run, Pallas kernels for 0% -> 0%
where the time goes in v3:
time: 235 us; the launch traced here: 234 us
  waiting for transfers between devices  92.8 us (39%)
  starting transfers between devices  56.6 us (24%)
  blocking collectives  48.7 us (21%)
  Pallas kernels  16.5 us (7%)
  between operations  14.2 us (6%)
  local copies, waits for them, and re-layouts  5.12 us (2%)
    all_to_all x1, blocking collectives, body(): lax.all_to_all(back.reshape(experts, rows, LANES), 'local', split_axis=0,...  48.7 us
    all_gather x1, waiting for transfers between devices, body(): gathered = lax.all_gather(piece, 'node', axis=0, tiled=False)  47 us
    ppermute x7, starting transfers between devices, body(): parts.append(lax.ppermute(others[step - 1], 'node', onward))  37.3 us
    all_to_all x1, waiting for transfers between devices, body(): lax.all_to_all(send.reshape(experts, rows, LANES), 'local', split_axis=0,...  30.9 us
    all_to_all x1, starting transfers between devices, body(): lax.all_to_all(send.reshape(experts, rows, LANES), 'local', split_axis=0,...  17.3 us
    pallas_call x7, Pallas kernels, call(): pl.pallas_call(kernel, out_shape=outs, in_specs=spec, out_specs=jax.tree....  16.5 us
    ppermute x7, waiting for transfers between devices, body(): parts.append(lax.ppermute(others[step - 1], 'node', onward))  11.6 us
    unnamed x20, local copies, waits for them, and re-layouts  5.12 us
  transfers between devices with their start and end apart: 10, of which 7 were waited for; matrix products, arithmetic and copies ran while one was open for 0% of the time, Pallas kernels for 0%

profile of v3, /device:TPU:4, one launch (start us, length us, event | category | flops | bytes accessed | tf_op | source)
XLA Modules:
  0.0 234.5 jit_solution(7417812548218511695)
XLA Ops:
  9.4 3.2 %shard_map.95 = (bf16[5120,128]{1,0:T(8,128)(2,1)}, f32[64,128]{1,0:T(8,128)S(1)}) custom-call(s32[8,128]{1,0:T(8,128)S(1)} %bitcast.30, bf16[8,128]{1,0:T(8,128)(2,1)S(1)} %bitcast.32, bf16[448,128]{1,0:T(8,128)(2,1)S(1)} %bitcast.29), custom_call_target="tpu_custom_call" | custom-call | tf_op jit(solution)/shard_map/pallas_call | solution.py:21
  12.6 17.3 %all-to-all-start = ((bf16[64,80,128]{2,1,0:T(8,128)(2,1)}), bf16[64,80,128]{2,1,0:T(8,128)(2,1)S(1)}, u32[]{:S(2)}, u32[]{:S(2)}) async-start(bf16[64,80,128]{2,1,0:T(8,128)(2,1)} %bitcast.5), calls=%async_computation | async-start | bytes 2621440 | tf_op jit(solution)/shard_map/all_to_all | solution.py:300
  30.1 1.1 shard_map.96.weight_ref
  31.2 30.9 %all-to-all-done = bf16[64,80,128]{2,1,0:T(8,128)(2,1)S(1)} async-done(((bf16[64,80,128]{2,1,0:T(8,128)(2,1)}), bf16[64,80,128]{2,1,0:T(8,128)(2,1)S(1)}, u32[]{:S(2)}, u32[]{:S(2)}) %all-to-all-start) | async-done | bytes 1310752 | tf_op jit(solution)/shard_map/all_to_all | solution.py:300
  62.2 2.5 %shard_map.97 = (bf16[512,1408]{1,0:T(8,128)(2,1)S(1)}, bf16[1344,512]{1,0:T(8,128)(2,1)S(1)}, f32[8,1344]{1,0:T(8,128)S(1)}) custom-call(bf16[5120,128]{1,0:T(8,128)(2,1)S(1)} %bitcast.22, bf16[2,512,448]{2,1,0:T(8,128)(2,1)S(1)} %shard_map.96.weight_ref), custom_call_target="tpu_custom_call" | custom-call | tf_op jit(solution)/shard_map/pallas_call | solution.py:21
  64.7 1.9 collective-permute-start
  66.6 3.2 %collective-permute-done.partner_ref = bf16[512,1408]{1,0:T(8,128)(2,1)S(1)} collective-permute-done((bf16[512,1408]{1,0:T(8,128)(2,1)S(1)}, bf16[512,1408]{1,0:T(8,128)(2,1)S(1)}, u32[]{:S(2)}, u32[]{:S(2)}) %collective-permute-start) | collective-permute-done | bytes 1441824 | tf_op jit(solution)/shard_map/ppermute | solution.py:325
  70.8 14.3 %collective-permute-start.1 = (bf16[64,1408]{1,0:T(8,128)(2,1)S(1)}, bf16[64,1408]{1,0:T(8,128)(2,1)S(1)}, u32[]{:S(2)}, u32[]{:S(2)}) collective-permute-start(bf16[64,1408]{1,0:T(8,128)(2,1)S(1)} %get-tuple-element.22), channel_id=1, source_target_pairs={{0,512},{64,576},{128,640},{192,704},{256,768},{320,832},{384,896}... | collective-permute-start | bytes 540680 | tf_op jit(solution)/shard_map/ppermute | solution.py:330
  85.1 7.9 %collective-permute-start.2 = (bf16[64,1408]{1,0:T(8,128)(2,1)S(1)}, bf16[64,1408]{1,0:T(8,128)(2,1)S(1)}, u32[]{:S(2)}, u32[]{:S(2)}) collective-permute-start(bf16[64,1408]{1,0:T(8,128)(2,1)S(1)} %get-tuple-element.23), channel_id=1, source_target_pairs={{0,384},{64,448},{128,512},{192,576},{256,640},{320,704},{384,768}... | collective-permute-start | bytes 540680 | tf_op jit(solution)/shard_map/ppermute | solution.py:330
  93.0 1.9 collective-permute-start.3
  95.0 5.1 %collective-permute-start.4 = (bf16[64,1408]{1,0:T(8,128)(2,1)S(1)}, bf16[64,1408]{1,0:T(8,128)(2,1)S(1)}, u32[]{:S(2)}, u32[]{:S(2)}) collective-permute-start(bf16[64,1408]{1,0:T(8,128)(2,1)S(1)} %get-tuple-element.25), channel_id=1, source_target_pairs={{0,256},{64,320},{128,384},{192,448},{256,512},{320,576},{384,640}... | collective-permute-start | bytes 540680 | tf_op jit(solution)/shard_map/ppermute | solution.py:330
  100.1 2.8 %collective-permute-start.5 = (bf16[64,1408]{1,0:T(8,128)(2,1)S(1)}, bf16[64,1408]{1,0:T(8,128)(2,1)S(1)}, u32[]{:S(2)}, u32[]{:S(2)}) collective-permute-start(bf16[64,1408]{1,0:T(8,128)(2,1)S(1)} %get-tuple-element.26), channel_id=1, source_target_pairs={{0,768},{64,832},{128,896},{192,960},{256,0},{320,64},{384,128},{4... | collective-permute-start | bytes 540680 | tf_op jit(solution)/shard_map/ppermute | solution.py:330
  102.9 3.3 %collective-permute-start.6 = (bf16[64,1408]{1,0:T(8,128)(2,1)S(1)}, bf16[64,1408]{1,0:T(8,128)(2,1)S(1)}, u32[]{:S(2)}, u32[]{:S(2)}) collective-permute-start(bf16[64,1408]{1,0:T(8,128)(2,1)S(1)} %get-tuple-element.27), channel_id=1, source_target_pairs={{0,128},{64,192},{128,256},{192,320},{256,384},{320,448},{384,512}... | collective-permute-start | bytes 540680 | tf_op jit(solution)/shard_map/ppermute | solution.py:330
  106.2 4.2 %collective-permute-done.2.refs_2_ = bf16[64,1408]{1,0:T(8,128)(2,1)S(1)} collective-permute-done((bf16[64,1408]{1,0:T(8,128)(2,1)S(1)}, bf16[64,1408]{1,0:T(8,128)(2,1)S(1)}, u32[]{:S(2)}, u32[]{:S(2)}) %collective-permute-start.2) | collective-permute-done | bytes 180256 | tf_op jit(solution)/shard_map/ppermute | solution.py:330
  110.4 1.9 collective-permute-start.7
  112.4 1.5 collective-permute-done.4.refs_4_
  113.9 3.9 %collective-permute-done.5.refs_5_ = bf16[64,1408]{1,0:T(8,128)(2,1)S(1)} collective-permute-done((bf16[64,1408]{1,0:T(8,128)(2,1)S(1)}, bf16[64,1408]{1,0:T(8,128)(2,1)S(1)}, u32[]{:S(2)}, u32[]{:S(2)}) %collective-permute-start.5) | collective-permute-done | bytes 180256 | tf_op jit(solution)/shard_map/ppermute | solution.py:330
  117.8 2.0 collective-permute-done.7.refs_7_
  119.8 1.2 shard_map.99
  121.0 47.0 %all-gather.3.cloned.1.call-done = bf16[2304,1344]{1,0:T(8,128)(2,1)} async-done(((bf16[144,1344]{1,0:T(8,128)(2,1)}), bf16[2304,1344]{1,0:T(8,128)(2,1)}) %all-gather.3.cloned.1.call-update) | async-done | bytes 6193168 | tf_op jit(solution)/shard_map/all_gather | solution.py:339
  168.0 2.8 %copy-done = bf16[2304,1344]{1,0:T(8,128)(2,1)S(1)} copy-done((bf16[2304,1344]{1,0:T(8,128)(2,1)S(1)}, bf16[2304,1344]{1,0:T(8,128)(2,1)}, u32[]{:S(2)}) %copy-start) | copy-done | bytes 6193176
  170.9 4.8 %shard_map.100 = bf16[5120,128]{1,0:T(8,128)(2,1)S(1)} custom-call(bf16[16,144,1344]{2,1,0:T(8,128)(2,1)S(1)} %bitcast.20, bf16[448,1024]{1,0:T(8,128)(2,1)S(1)} %bitcast.24, bf16[448,1024]{1,0:T(8,128)(2,1)S(1)} %bitcast.25), custom_call_target="tpu_custom_call" | custom-call | tf_op jit(solution)/shard_map/pallas_call | solution.py:21
  175.7 48.7 %all_to_all.10 = bf16[64,80,128]{2,1,0:T(8,128)(2,1)S(1)} all-to-all(bf16[64,80,128]{2,1,0:T(8,128)(2,1)S(1)} %bitcast.21), channel_id=1, replica_groups=mesh['node'=16,'local'=64] {'local'}, dimensions={0} | all-to-all | bytes 2621440 | tf_op jit(solution)/shard_map/all_to_all | solution.py:348
  224.4 2.7 %shard_map.101 = (bf16[448,128]{1,0:T(8,128)(2,1)}, f32[8,128]{1,0:T(8,128)S(1)}) custom-call(bf16[5120,128]{1,0:T(8,128)(2,1)S(1)} %bitcast.23, f32[64,128]{1,0:T(8,128)S(1)} %get-tuple-element.29.rank_ref, s32[8,128]{1,0:T(8,128)S(1)} %bitcast.31), custom_call_target="tpu_custom_call" | custom-call | tf_op jit(solution)/shard_map/pallas_call | solution.py:21
  (27 shorter events, 4.0 us)
Async XLA Ops:
  7.2 0.9 copy-start.6
  8.1 0.7 copy-start.7
  8.8 0.7 copy-start.9
  9.4 20.7 %copy-start.3 = (bf16[1,1024,448]{1,2,0:T(8,128)(2,1)S(1)}, bf16[1,1024,448]{1,2,0:T(8,128)(2,1)}, u32[]{:S(2)}) copy-start(bf16[1,1024,448]{1,2,0:T(8,128)(2,1)} %param.13) | copy-start | bytes 2752516
  12.6 49.6 %all-to-all-start = ((bf16[64,80,128]{2,1,0:T(8,128)(2,1)}), bf16[64,80,128]{2,1,0:T(8,128)(2,1)S(1)}, u32[]{:S(2)}, u32[]{:S(2)}) async-start(bf16[64,80,128]{2,1,0:T(8,128)(2,1)} %bitcast.5), calls=%async_computation | async-start | bytes 2621440 | tf_op jit(solution)/shard_map/all_to_all | solution.py:300
  30.0 138.1 %all-gather.3.cloned.1.call-start = ((), (), s32[]{:S(2)}) async-start(), calls=%async_computation.2 | async-start | bytes 6893568 | tf_op jit(solution)/shard_map/all_gather | solution.py:339
  64.7 5.1 %collective-permute-start = (bf16[512,1408]{1,0:T(8,128)(2,1)S(1)}, bf16[512,1408]{1,0:T(8,128)(2,1)S(1)}, u32[]{:S(2)}, u32[]{:S(2)}) collective-permute-start(bf16[512,1408]{1,0:T(8,128)(2,1)S(1)} %get-tuple-element.20), channel_id=1, source_target_pairs={{0,64},{64,0},{128,192},{192,128},{256,320},{320,256},{384,448},{4... | collective-permute-start | bytes 4325384 | tf_op jit(solution)/shard_map/ppermute | solution.py:325
  69.8 50.0 %copy-start.4 = (bf16[1,64,1344]{2,1,0:T(8,128)(2,1)S(1)}, bf16[1,64,1344]{2,1,0:T(8,128)(2,1)}, u32[]{:S(2)}) copy-start(bf16[1,64,1344]{2,1,0:T(8,128)(2,1)} %param.14) | copy-start | bytes 516100
  69.8 50.0 %copy-start.5 = (bf16[1,64,1344]{2,1,0:T(8,128)(2,1)S(1)}, bf16[1,64,1344]{2,1,0:T(8,128)(2,1)}, u32[]{:S(2)}) copy-start(bf16[1,64,1344]{2,1,0:T(8,128)(2,1)} %param.15) | copy-start | bytes 516100
  70.8 32.1 %collective-permute-start.1 = (bf16[64,1408]{1,0:T(8,128)(2,1)S(1)}, bf16[64,1408]{1,0:T(8,128)(2,1)S(1)}, u32[]{:S(2)}, u32[]{:S(2)}) collective-permute-start(bf16[64,1408]{1,0:T(8,128)(2,1)S(1)} %get-tuple-element.22), channel_id=1, source_target_pairs={{0,512},{64,576},{128,640},{192,704},{256,768},{320,832},{384,896}... | collective-permute-start | bytes 540680 | tf_op jit(solution)/shard_map/ppermute | solution.py:330
  85.1 25.4 %collective-permute-start.2 = (bf16[64,1408]{1,0:T(8,128)(2,1)S(1)}, bf16[64,1408]{1,0:T(8,128)(2,1)S(1)}, u32[]{:S(2)}, u32[]{:S(2)}) collective-permute-start(bf16[64,1408]{1,0:T(8,128)(2,1)S(1)} %get-tuple-element.23), channel_id=1, source_target_pairs={{0,384},{64,448},{128,512},{192,576},{256,640},{320,704},{384,768}... | collective-permute-start | bytes 540680 | tf_op jit(solution)/shard_map/ppermute | solution.py:330
  93.0 19.3 %collective-permute-start.3 = (bf16[64,1408]{1,0:T(8,128)(2,1)S(1)}, bf16[64,1408]{1,0:T(8,128)(2,1)S(1)}, u32[]{:S(2)}, u32[]{:S(2)}) collective-permute-start(bf16[64,1408]{1,0:T(8,128)(2,1)S(1)} %get-tuple-element.24), channel_id=1, source_target_pairs={{0,640},{64,704},{128,768},{192,832},{256,896},{320,960},{384,0},{... | collective-permute-start | bytes 540680 | tf_op jit(solution)/shard_map/ppermute | solution.py:330
  95.0 18.9 %collective-permute-start.4 = (bf16[64,1408]{1,0:T(8,128)(2,1)S(1)}, bf16[64,1408]{1,0:T(8,128)(2,1)S(1)}, u32[]{:S(2)}, u32[]{:S(2)}) collective-permute-start(bf16[64,1408]{1,0:T(8,128)(2,1)S(1)} %get-tuple-element.25), channel_id=1, source_target_pairs={{0,256},{64,320},{128,384},{192,448},{256,512},{320,576},{384,640}... | collective-permute-start | bytes 540680 | tf_op jit(solution)/shard_map/ppermute | solution.py:330
  100.1 17.7 %collective-permute-start.5 = (bf16[64,1408]{1,0:T(8,128)(2,1)S(1)}, bf16[64,1408]{1,0:T(8,128)(2,1)S(1)}, u32[]{:S(2)}, u32[]{:S(2)}) collective-permute-start(bf16[64,1408]{1,0:T(8,128)(2,1)S(1)} %get-tuple-element.26), channel_id=1, source_target_pairs={{0,768},{64,832},{128,896},{192,960},{256,0},{320,64},{384,128},{4... | collective-permute-start | bytes 540680 | tf_op jit(solution)/shard_map/ppermute | solution.py:330
  102.9 14.8 %collective-permute-start.6 = (bf16[64,1408]{1,0:T(8,128)(2,1)S(1)}, bf16[64,1408]{1,0:T(8,128)(2,1)S(1)}, u32[]{:S(2)}, u32[]{:S(2)}) collective-permute-start(bf16[64,1408]{1,0:T(8,128)(2,1)S(1)} %get-tuple-element.27), channel_id=1, source_target_pairs={{0,128},{64,192},{128,256},{192,320},{256,384},{320,448},{384,512}... | collective-permute-start | bytes 540680 | tf_op jit(solution)/shard_map/ppermute | solution.py:330
  110.4 9.3 %collective-permute-start.7 = (bf16[64,1408]{1,0:T(8,128)(2,1)S(1)}, bf16[64,1408]{1,0:T(8,128)(2,1)S(1)}, u32[]{:S(2)}, u32[]{:S(2)}) collective-permute-start(bf16[64,1408]{1,0:T(8,128)(2,1)S(1)} %get-tuple-element.28), channel_id=1, source_target_pairs={{0,896},{64,960},{128,0},{192,64},{256,128},{320,192},{384,256},{4... | collective-permute-start | bytes 540680 | tf_op jit(solution)/shard_map/ppermute | solution.py:330
  119.8 48.2 %copy-start.1 = (bf16[1,448,1024]{2,1,0:T(8,128)(2,1)S(1)}, bf16[1,448,1024]{2,1,0:T(8,128)(2,1)}, u32[]{:S(2)}) copy-start(bf16[1,448,1024]{2,1,0:T(8,128)(2,1)} %param.11) | copy-start | bytes 2752516
  119.8 48.2 %copy-start.2 = (bf16[1,448,1024]{2,1,0:T(8,128)(2,1)S(1)}, bf16[1,448,1024]{2,1,0:T(8,128)(2,1)}, u32[]{:S(2)}) copy-start(bf16[1,448,1024]{2,1,0:T(8,128)(2,1)} %param.12) | copy-start | bytes 2752516
  168.0 2.8 %copy-start = (bf16[2304,1344]{1,0:T(8,128)(2,1)S(1)}, bf16[2304,1344]{1,0:T(8,128)(2,1)}, u32[]{:S(2)}) copy-start(bf16[2304,1344]{1,0:T(8,128)(2,1)} %all-gather.3.cloned.1.call-done) | copy-start | bytes 18579460
  175.7 48.7 %copy-start.8 = (s32[128,8]{0,1:T(8,128)S(1)}, s32[128,8]{0,1:T(8,128)}, u32[]{:S(2)}) copy-start(s32[128,8]{0,1:T(8,128)} %param.10) | copy-start | bytes 12292
Sparse Core Ops, SparseCore 0:
  121.1 46.8 all-gather.2

commit v4 on v3

--- a/solution.py
+++ b/solution.py
@@ -14,7 +14,7 @@
 EXTRA = 16
 
 
-def call(kernel, outs, *operands, smem=0, scratch=(), plain=False):
+def call(kernel, outs, *operands, smem=0, scratch=(), plain=False, mib=32):
     vmem = pl.BlockSpec() if plain else pl.BlockSpec(memory_space=pltpu.VMEM)
     spec = [pl.BlockSpec(memory_space=pltpu.SMEM)] * smem
     spec += [vmem] * (len(operands) - smem)
@@ -24,7 +24,7 @@
         in_specs=spec,
         out_specs=jax.tree.map(lambda _: vmem, outs),
         scratch_shapes=list(scratch),
-        compiler_params=pltpu.CompilerParams(vmem_limit_bytes=32 * 2**20),
+        compiler_params=pltpu.CompilerParams(vmem_limit_bytes=mib * 2**20),
     )(*operands)
 
 
@@ -212,20 +212,30 @@
 
 
 def input_kernel(capacity, all_ref, gate_ref, up_ref, out_ref, wide_ref, rows_ref):
-    nodes, height, slots = all_ref.shape
+    part, height, slots = all_ref.shape
     units = (height - EXTRA) // 2
     features = gate_ref.shape[0]
-    gate_pre = all_ref[:, :units, :].reshape(nodes * units, slots)
-    up_pre = all_ref[:, units : 2 * units, :].reshape(nodes * units, slots)
-    wide_ref[:features, :slots] = dot(gate_ref[...], gate_pre, NN) + dot(up_ref[...], up_pre, NN)
+    step = pl.program_id(0)
+
+    @pl.when(step == 0)
+    def _():
+        wide_ref[...] = jnp.zeros(wide_ref.shape, F32)
+
+    gate_pre = all_ref[:, :units, :].reshape(part * units, slots)
+    up_pre = all_ref[:, units : 2 * units, :].reshape(part * units, slots)
+    wide_ref[:features, :slots] += dot(gate_ref[...], gate_pre, NN) + dot(up_ref[...], up_pre, NN)
     extra = all_ref[0, 2 * units :, :].astype(F32)
-    for n in range(1, nodes):
+    for n in range(1, part):
         extra += all_ref[n, 2 * units :, :].astype(F32)
     spare = wide_ref.shape[0] - features
-    wide_ref[features:, :slots] = jnp.broadcast_to(extra[0:1] + extra[1:2], (spare, slots))
-    beyond = wide_ref.shape[1] - slots
-    if beyond:
-        wide_ref[:, slots:] = jnp.zeros((wide_ref.shape[0], beyond), F32)
+    wide_ref[features:, :slots] += jnp.broadcast_to(extra[0:1] + extra[1:2], (spare, slots))
+
+    @pl.when(step == pl.num_programs(0) - 1)
+    def _():
+        pack_rows(capacity, slots, features, out_ref, wide_ref, rows_ref)
+
+
+def pack_rows(capacity, slots, features, out_ref, wide_ref, rows_ref):
     rows_ref[...] = wide_ref[...].T
     full, _, rows = layout(features, capacity)
     tight, wide = GROUP * capacity, GROUP * rows
@@ -270,9 +280,11 @@
     j = lax.broadcasted_iota(jnp.int32, (experts, height, tokens), 1).astype(F32)
     chosen = jnp.sum(jnp.where(rank[:, None, :] == j, column, 0.0), axis=1)
     expert = lax.broadcasted_iota(jnp.int32, (experts, tokens), 0)
+    combine = []
     for k in range(ids_ref.shape[0]):
         hit = ids_ref[k : k + 1, :] == expert
-        combine_ref[k : k + 1, :] = jnp.sum(jnp.where(hit, chosen, 0.0), axis=0, keepdims=True)
+        combine.append(jnp.sum(jnp.where(hit, chosen, 0.0), axis=0, keepdims=True))
+    combine_ref[...] = jnp.concatenate(combine, axis=0).astype(BF)
 
 
 def body(out_grad, gate_weights, expert_ids, w_gate, w_up, w_down, saved_gate, saved_up):
@@ -296,6 +308,7 @@
         gate_weights.T,
         out_grad.T,
         plain=True,
+        mib=60,
     )
     arrived = lax.all_to_all(
         send.reshape(experts, rows, LANES), "local", split_axis=0, concat_axis=0, tiled=True
@@ -337,25 +350,32 @@
         *parts,
     )
     gathered = lax.all_gather(piece, "node", axis=0, tiled=False)
-    back = call(
+    part = 4 if nodes >= 8 else 2
+    weight_spec = pl.BlockSpec((features, part * units), lambda n: (0, n))
+    back = pl.pallas_call(
         functools.partial(input_kernel, capacity),
-        shape((experts * rows, LANES), BF),
-        gathered,
-        w_gate[0],
-        w_up[0],
-        scratch=[pltpu.VMEM((lanes, rounded), F32), pltpu.VMEM((rounded, lanes), F32)],
-    )
+        out_shape=shape((experts * rows, LANES), BF),
+        grid=(nodes // part,),
+        in_specs=[
+            pl.BlockSpec((part, 2 * units + EXTRA, slots), lambda n: (n, 0, 0)),
+            weight_spec,
+            weight_spec,
+        ],
+        out_specs=pl.BlockSpec((experts * rows, LANES), lambda n: (0, 0)),
+        scratch_shapes=[pltpu.VMEM((lanes, rounded), F32), pltpu.VMEM((rounded, lanes), F32)],
+        compiler_params=pltpu.CompilerParams(vmem_limit_bytes=60 * 2**20),
+    )(gathered, w_gate[0], w_up[0])
     returned = lax.all_to_all(
         back.reshape(experts, rows, LANES), "local", split_axis=0, concat_axis=0, tiled=True
     )
     grad, combine = call(
         functools.partial(collect_kernel, capacity),
-        (shape((features, tokens), BF), shape((top, tokens), F32)),
+        (shape((features, tokens), BF), shape((top, tokens), BF)),
         returned.reshape(experts * rows, LANES),
         rank,
         ids,
     )
-    return grad.T, combine.T.astype(BF)
+    return grad.T, combine.T
 
 
 def solution(mesh):

time: 235 us -> 235 us (level)
  Pallas kernels: 16.5 us -> 21.9 us
  local copies, waits for them, and re-layouts: 5.12 us -> 0.02 us
    pallas_call x0 -> x1, Pallas kernels: none -> 9.17 us  [body(): pl.pallas_call(functools.partial(input_kernel, capacity), out_shape=shape...]
    unnamed x20 -> x10, local copies, waits for them, and re-layouts: 5.12 us -> 0.02 us
    pallas_call x7 -> x6, Pallas kernels: 16.5 us -> 12.7 us  [call(): pl.pallas_call(kernel, out_shape=outs, in_specs=spec, out_specs=jax.tree....]
where the time goes in v4:
time: 235 us
  waiting for transfers between devices  92.8 us (39%)
  starting transfers between devices  56.6 us (24%)
  blocking collectives  49 us (21%)
  Pallas kernels  21.9 us (9%)
  between operations  14.2 us (6%)
    all_to_all x1, blocking collectives, body(): lax.all_to_all(back.reshape(experts, rows, LANES), 'local', split_axis=0,...  49 us
    all_gather x1, waiting for transfers between devices, body(): gathered = lax.all_gather(piece, 'node', axis=0, tiled=False)  47.1 us
    ppermute x7, starting transfers between devices, body(): parts.append(lax.ppermute(others[step - 1], 'node', onward))  37.3 us
    all_to_all x1, waiting for transfers between devices, body(): lax.all_to_all(send.reshape(experts, rows, LANES), 'local', split_axis=0,...  30.9 us
    all_to_all x1, starting transfers between devices, body(): lax.all_to_all(send.reshape(experts, rows, LANES), 'local', split_axis=0,...  17.4 us
    pallas_call x6, Pallas kernels, call(): pl.pallas_call(kernel, out_shape=outs, in_specs=spec, out_specs=jax.tree....  12.7 us
    ppermute x7, waiting for transfers between devices, body(): parts.append(lax.ppermute(others[step - 1], 'node', onward))  11.5 us
    pallas_call x1, Pallas kernels, body(): pl.pallas_call(functools.partial(input_kernel, capacity), out_shape=shape...  9.17 us
  transfers between devices with their start and end apart: 10, of which 7 were waited for; matrix products, arithmetic and copies ran while one was open for 0% of the time, Pallas kernels for 0%

profile of v4, /device:TPU:4, one launch (start us, length us, event | category | flops | bytes accessed | tf_op | source)
XLA Modules:
  0.0 234.5 jit_solution(7495589215504188340)
XLA Ops:
  7.2 4.2 %shard_map.95 = (bf16[5120,128]{1,0:T(8,128)(2,1)}, f32[64,128]{1,0:T(8,128)}) custom-call(s32[8,128]{1,0:T(8,128)} %bitcast.24, bf16[8,128]{1,0:T(8,128)(2,1)} %bitcast.32, bf16[448,128]{1,0:T(8,128)(2,1)} %bitcast.31), custom_call_target="tpu_custom_call" | custom-call | tf_op jit(solution)/shard_map/pallas_call | solution.py:21
  11.3 17.4 %all-to-all-start = ((bf16[64,80,128]{2,1,0:T(8,128)(2,1)}), bf16[64,80,128]{2,1,0:T(8,128)(2,1)S(1)}, u32[]{:S(2)}, u32[]{:S(2)}) async-start(bf16[64,80,128]{2,1,0:T(8,128)(2,1)} %bitcast.28), calls=%async_computation | async-start | bytes 2621440 | tf_op jit(solution)/shard_map/all_to_all | solution.py:313
  28.9 1.1 shard_map.96.weight_ref
  30.0 30.9 %all-to-all-done = bf16[64,80,128]{2,1,0:T(8,128)(2,1)S(1)} async-done(((bf16[64,80,128]{2,1,0:T(8,128)(2,1)}), bf16[64,80,128]{2,1,0:T(8,128)(2,1)S(1)}, u32[]{:S(2)}, u32[]{:S(2)}) %all-to-all-start) | async-done | bytes 1310752 | tf_op jit(solution)/shard_map/all_to_all | solution.py:313
  60.9 2.5 %shard_map.97 = (bf16[512,1408]{1,0:T(8,128)(2,1)S(1)}, bf16[1344,512]{1,0:T(8,128)(2,1)S(1)}, f32[8,1344]{1,0:T(8,128)S(1)}) custom-call(bf16[5120,128]{1,0:T(8,128)(2,1)S(1)} %bitcast.19, bf16[2,512,448]{2,1,0:T(8,128)(2,1)S(1)} %shard_map.96.weight_ref), custom_call_target="tpu_custom_call" | custom-call | tf_op jit(solution)/shard_map/pallas_call | solution.py:21
  63.4 1.9 collective-permute-start
  65.4 3.2 %collective-permute-done.partner_ref = bf16[512,1408]{1,0:T(8,128)(2,1)S(1)} collective-permute-done((bf16[512,1408]{1,0:T(8,128)(2,1)S(1)}, bf16[512,1408]{1,0:T(8,128)(2,1)S(1)}, u32[]{:S(2)}, u32[]{:S(2)}) %collective-permute-start) | collective-permute-done | bytes 1441824 | tf_op jit(solution)/shard_map/ppermute | solution.py:338
  68.6 1.0 shard_map.98
  69.6 14.3 %collective-permute-start.1 = (bf16[64,1408]{1,0:T(8,128)(2,1)S(1)}, bf16[64,1408]{1,0:T(8,128)(2,1)S(1)}, u32[]{:S(2)}, u32[]{:S(2)}) collective-permute-start(bf16[64,1408]{1,0:T(8,128)(2,1)S(1)} %get-tuple-element.22), channel_id=1, source_target_pairs={{0,512},{64,576},{128,640},{192,704},{256,768},{320,832},{384,896}... | collective-permute-start | bytes 540680 | tf_op jit(solution)/shard_map/ppermute | solution.py:343
  83.9 7.9 %collective-permute-start.2 = (bf16[64,1408]{1,0:T(8,128)(2,1)S(1)}, bf16[64,1408]{1,0:T(8,128)(2,1)S(1)}, u32[]{:S(2)}, u32[]{:S(2)}) collective-permute-start(bf16[64,1408]{1,0:T(8,128)(2,1)S(1)} %get-tuple-element.23), channel_id=1, source_target_pairs={{0,384},{64,448},{128,512},{192,576},{256,640},{320,704},{384,768}... | collective-permute-start | bytes 540680 | tf_op jit(solution)/shard_map/ppermute | solution.py:343
  91.8 1.9 collective-permute-start.3
  93.7 5.1 %collective-permute-start.4 = (bf16[64,1408]{1,0:T(8,128)(2,1)S(1)}, bf16[64,1408]{1,0:T(8,128)(2,1)S(1)}, u32[]{:S(2)}, u32[]{:S(2)}) collective-permute-start(bf16[64,1408]{1,0:T(8,128)(2,1)S(1)} %get-tuple-element.25), channel_id=1, source_target_pairs={{0,256},{64,320},{128,384},{192,448},{256,512},{320,576},{384,640}... | collective-permute-start | bytes 540680 | tf_op jit(solution)/shard_map/ppermute | solution.py:343
  98.9 2.8 %collective-permute-start.5 = (bf16[64,1408]{1,0:T(8,128)(2,1)S(1)}, bf16[64,1408]{1,0:T(8,128)(2,1)S(1)}, u32[]{:S(2)}, u32[]{:S(2)}) collective-permute-start(bf16[64,1408]{1,0:T(8,128)(2,1)S(1)} %get-tuple-element.26), channel_id=1, source_target_pairs={{0,768},{64,832},{128,896},{192,960},{256,0},{320,64},{384,128},{4... | collective-permute-start | bytes 540680 | tf_op jit(solution)/shard_map/ppermute | solution.py:343
  101.7 3.3 %collective-permute-start.6 = (bf16[64,1408]{1,0:T(8,128)(2,1)S(1)}, bf16[64,1408]{1,0:T(8,128)(2,1)S(1)}, u32[]{:S(2)}, u32[]{:S(2)}) collective-permute-start(bf16[64,1408]{1,0:T(8,128)(2,1)S(1)} %get-tuple-element.27), channel_id=1, source_target_pairs={{0,128},{64,192},{128,256},{192,320},{256,384},{320,448},{384,512}... | collective-permute-start | bytes 540680 | tf_op jit(solution)/shard_map/ppermute | solution.py:343
  105.0 4.2 %collective-permute-done.2.refs_2_ = bf16[64,1408]{1,0:T(8,128)(2,1)S(1)} collective-permute-done((bf16[64,1408]{1,0:T(8,128)(2,1)S(1)}, bf16[64,1408]{1,0:T(8,128)(2,1)S(1)}, u32[]{:S(2)}, u32[]{:S(2)}) %collective-permute-start.2) | collective-permute-done | bytes 180256 | tf_op jit(solution)/shard_map/ppermute | solution.py:343
  109.2 1.9 collective-permute-start.7
  111.1 1.5 collective-permute-done.4.refs_4_
  112.7 3.9 %collective-permute-done.5.refs_5_ = bf16[64,1408]{1,0:T(8,128)(2,1)S(1)} collective-permute-done((bf16[64,1408]{1,0:T(8,128)(2,1)S(1)}, bf16[64,1408]{1,0:T(8,128)(2,1)S(1)}, u32[]{:S(2)}, u32[]{:S(2)}) %collective-permute-start.5) | collective-permute-done | bytes 180256 | tf_op jit(solution)/shard_map/ppermute | solution.py:343
  116.6 1.9 collective-permute-done.7.refs_7_
  118.5 1.2 shard_map.99
  119.7 47.1 %all-gather.3.cloned.1.call-done = bf16[2304,1344]{1,0:T(8,128)(2,1)} async-done(((bf16[144,1344]{1,0:T(8,128)(2,1)}), bf16[2304,1344]{1,0:T(8,128)(2,1)}) %all-gather.3.cloned.1.call-update) | async-done | bytes 6193168 | tf_op jit(solution)/shard_map/all_gather | solution.py:352
  166.8 9.2 %shard_map.100 = bf16[5120,128]{1,0:T(8,128)(2,1)} custom-call(bf16[16,144,1344]{2,1,0:T(8,128)(2,1)} %bitcast.26, bf16[448,1024]{1,0:T(8,128)(2,1)} %bitcast.29, bf16[448,1024]{1,0:T(8,128)(2,1)} %bitcast.30), custom_call_target="tpu_custom_call" | custom-call | tf_op jit(solution)/shard_map/pallas_call | solution.py:355
  176.0 49.0 %all_to_all.10 = bf16[64,80,128]{2,1,0:T(8,128)(2,1)S(1)} all-to-all(bf16[64,80,128]{2,1,0:T(8,128)(2,1)} %bitcast.27), channel_id=1, replica_groups=mesh['node'=16,'local'=64] {'local'}, dimensions={0} | all-to-all | bytes 2621440 | tf_op jit(solution)/shard_map/all_to_all | solution.py:368
  225.0 2.7 %shard_map.101 = (bf16[448,128]{1,0:T(8,128)(2,1)}, bf16[8,128]{1,0:T(8,128)(2,1)}) custom-call(bf16[5120,128]{1,0:T(8,128)(2,1)S(1)} %bitcast.20, f32[64,128]{1,0:T(8,128)S(1)} %copy-done.3, s32[8,128]{1,0:T(8,128)S(1)} %bitcast.25), custom_call_target="tpu_custom_call" | custom-call | tf_op jit(solution)/shard_map/pallas_call | solution.py:21
  (16 shorter events, 0.2 us)
Async XLA Ops:
  7.2 21.7 %copy-start = (bf16[1,1024,448]{1,2,0:T(8,128)(2,1)S(1)}, bf16[1,1024,448]{1,2,0:T(8,128)(2,1)}, u32[]{:S(2)}) copy-start(bf16[1,1024,448]{1,2,0:T(8,128)(2,1)} %param.13) | copy-start | bytes 2752516
  11.3 49.6 %all-to-all-start = ((bf16[64,80,128]{2,1,0:T(8,128)(2,1)}), bf16[64,80,128]{2,1,0:T(8,128)(2,1)S(1)}, u32[]{:S(2)}, u32[]{:S(2)}) async-start(bf16[64,80,128]{2,1,0:T(8,128)(2,1)} %bitcast.28), calls=%async_computation | async-start | bytes 2621440 | tf_op jit(solution)/shard_map/all_to_all | solution.py:313
  28.7 138.1 %all-gather.3.cloned.1.call-start = ((), (), s32[]{:S(2)}) async-start(), calls=%async_computation.2 | async-start | bytes 6893568 | tf_op jit(solution)/shard_map/all_gather | solution.py:352
  63.4 5.1 %collective-permute-start = (bf16[512,1408]{1,0:T(8,128)(2,1)S(1)}, bf16[512,1408]{1,0:T(8,128)(2,1)S(1)}, u32[]{:S(2)}, u32[]{:S(2)}) collective-permute-start(bf16[512,1408]{1,0:T(8,128)(2,1)S(1)} %get-tuple-element.20), channel_id=1, source_target_pairs={{0,64},{64,0},{128,192},{192,128},{256,320},{320,256},{384,448},{4... | collective-permute-start | bytes 4325384 | tf_op jit(solution)/shard_map/ppermute | solution.py:338
  68.6 49.9 %copy-start.1 = (bf16[1,64,1344]{2,1,0:T(8,128)(2,1)S(1)}, bf16[1,64,1344]{2,1,0:T(8,128)(2,1)}, u32[]{:S(2)}) copy-start(bf16[1,64,1344]{2,1,0:T(8,128)(2,1)} %param.14) | copy-start | bytes 516100
  68.6 49.9 %copy-start.2 = (bf16[1,64,1344]{2,1,0:T(8,128)(2,1)S(1)}, bf16[1,64,1344]{2,1,0:T(8,128)(2,1)}, u32[]{:S(2)}) copy-start(bf16[1,64,1344]{2,1,0:T(8,128)(2,1)} %param.15) | copy-start | bytes 516100
  69.6 32.1 %collective-permute-start.1 = (bf16[64,1408]{1,0:T(8,128)(2,1)S(1)}, bf16[64,1408]{1,0:T(8,128)(2,1)S(1)}, u32[]{:S(2)}, u32[]{:S(2)}) collective-permute-start(bf16[64,1408]{1,0:T(8,128)(2,1)S(1)} %get-tuple-element.22), channel_id=1, source_target_pairs={{0,512},{64,576},{128,640},{192,704},{256,768},{320,832},{384,896}... | collective-permute-start | bytes 540680 | tf_op jit(solution)/shard_map/ppermute | solution.py:343
  83.9 25.3 %collective-permute-start.2 = (bf16[64,1408]{1,0:T(8,128)(2,1)S(1)}, bf16[64,1408]{1,0:T(8,128)(2,1)S(1)}, u32[]{:S(2)}, u32[]{:S(2)}) collective-permute-start(bf16[64,1408]{1,0:T(8,128)(2,1)S(1)} %get-tuple-element.23), channel_id=1, source_target_pairs={{0,384},{64,448},{128,512},{192,576},{256,640},{320,704},{384,768}... | collective-permute-start | bytes 540680 | tf_op jit(solution)/shard_map/ppermute | solution.py:343
  91.8 19.3 %collective-permute-start.3 = (bf16[64,1408]{1,0:T(8,128)(2,1)S(1)}, bf16[64,1408]{1,0:T(8,128)(2,1)S(1)}, u32[]{:S(2)}, u32[]{:S(2)}) collective-permute-start(bf16[64,1408]{1,0:T(8,128)(2,1)S(1)} %get-tuple-element.24), channel_id=1, source_target_pairs={{0,640},{64,704},{128,768},{192,832},{256,896},{320,960},{384,0},{... | collective-permute-start | bytes 540680 | tf_op jit(solution)/shard_map/ppermute | solution.py:343
  93.7 18.9 %collective-permute-start.4 = (bf16[64,1408]{1,0:T(8,128)(2,1)S(1)}, bf16[64,1408]{1,0:T(8,128)(2,1)S(1)}, u32[]{:S(2)}, u32[]{:S(2)}) collective-permute-start(bf16[64,1408]{1,0:T(8,128)(2,1)S(1)} %get-tuple-element.25), channel_id=1, source_target_pairs={{0,256},{64,320},{128,384},{192,448},{256,512},{320,576},{384,640}... | collective-permute-start | bytes 540680 | tf_op jit(solution)/shard_map/ppermute | solution.py:343
  98.9 17.7 %collective-permute-start.5 = (bf16[64,1408]{1,0:T(8,128)(2,1)S(1)}, bf16[64,1408]{1,0:T(8,128)(2,1)S(1)}, u32[]{:S(2)}, u32[]{:S(2)}) collective-permute-start(bf16[64,1408]{1,0:T(8,128)(2,1)S(1)} %get-tuple-element.26), channel_id=1, source_target_pairs={{0,768},{64,832},{128,896},{192,960},{256,0},{320,64},{384,128},{4... | collective-permute-start | bytes 540680 | tf_op jit(solution)/shard_map/ppermute | solution.py:343
  101.7 14.8 %collective-permute-start.6 = (bf16[64,1408]{1,0:T(8,128)(2,1)S(1)}, bf16[64,1408]{1,0:T(8,128)(2,1)S(1)}, u32[]{:S(2)}, u32[]{:S(2)}) collective-permute-start(bf16[64,1408]{1,0:T(8,128)(2,1)S(1)} %get-tuple-element.27), channel_id=1, source_target_pairs={{0,128},{64,192},{128,256},{192,320},{256,384},{320,448},{384,512}... | collective-permute-start | bytes 540680 | tf_op jit(solution)/shard_map/ppermute | solution.py:343
  109.2 9.3 %collective-permute-start.7 = (bf16[64,1408]{1,0:T(8,128)(2,1)S(1)}, bf16[64,1408]{1,0:T(8,128)(2,1)S(1)}, u32[]{:S(2)}, u32[]{:S(2)}) collective-permute-start(bf16[64,1408]{1,0:T(8,128)(2,1)S(1)} %get-tuple-element.28), channel_id=1, source_target_pairs={{0,896},{64,960},{128,0},{192,64},{256,128},{320,192},{384,256},{4... | collective-permute-start | bytes 540680 | tf_op jit(solution)/shard_map/ppermute | solution.py:343
  176.0 49.0 %copy-start.3 = (f32[64,128]{1,0:T(8,128)S(1)}, f32[64,128]{1,0:T(8,128)}, u32[]{:S(2)}) copy-start(f32[64,128]{1,0:T(8,128)} %get-tuple-element.29.rank_ref) | copy-start | bytes 98308
  176.0 49.0 %copy-start.4 = (s32[128,8]{0,1:T(8,128)S(1)}, s32[128,8]{0,1:T(8,128)}, u32[]{:S(2)}) copy-start(s32[128,8]{0,1:T(8,128)} %param.10) | copy-start | bytes 12292
Sparse Core Ops, SparseCore 0:
  119.8 46.9 all-gather.2

commit v5 on v3

--- a/solution.py
+++ b/solution.py
@@ -14,7 +14,7 @@
 EXTRA = 16
 
 
-def call(kernel, outs, *operands, smem=0, scratch=(), plain=False):
+def call(kernel, outs, *operands, smem=0, scratch=(), plain=False, mib=32):
     vmem = pl.BlockSpec() if plain else pl.BlockSpec(memory_space=pltpu.VMEM)
     spec = [pl.BlockSpec(memory_space=pltpu.SMEM)] * smem
     spec += [vmem] * (len(operands) - smem)
@@ -24,7 +24,7 @@
         in_specs=spec,
         out_specs=jax.tree.map(lambda _: vmem, outs),
         scratch_shapes=list(scratch),
-        compiler_params=pltpu.CompilerParams(vmem_limit_bytes=32 * 2**20),
+        compiler_params=pltpu.CompilerParams(vmem_limit_bytes=mib * 2**20),
     )(*operands)
 
 
@@ -138,10 +138,17 @@
     low, high = rows[:, :64], rows[:, 64:]
     rows_ref[0] = jnp.where(core == 0, low, high)
     rows_ref[1] = jnp.where(core == 0, high, low)
-    for step in range(blocks):
-        block = lax.rem(start + step, blocks)
-        for half in range(2):
-            out_ref[half, step * 64 : (step + 1) * 64, :] = rows_ref[half, block].astype(BF)
+    kept = blocks // 2
+    for half in range(2):
+        for i in range(kept):
+            block = lax.rem(start + 2 * i, blocks)
+            out_ref[half, i * 64 : (i + 1) * 64, :] = rows_ref[half, block].astype(BF)
+        for side in range(2):
+            at = kept * (64 + side * 32)
+            for i in range(kept):
+                block = lax.rem(place_ref[2 + side] + 2 * i, blocks)
+                part = rows_ref[half, block, side * 32 : (side + 1) * 32, :]
+                out_ref[half, at + i * 32 : at + (i + 1) * 32, :] = part.astype(BF)
 
 
 def other_half_kernel(capacity, arrived_ref, weight_ref, out_ref, rows_ref, gate_ref):
@@ -178,15 +185,35 @@
     gate_ref[...] = dot(at, rows_ref[:, full * LANES :], NT)
 
 
-def own_half_kernel(rows_ref, weight_ref, partner_ref, *out_refs):
+def store_wide(out_ref, at, value):
+    slots = value.shape[1]
+    out_ref[at, :slots] = value.astype(out_ref.dtype)
+    if out_ref.shape[1] > slots:
+        rest = (value.shape[0], out_ref.shape[1] - slots)
+        out_ref[at, slots:] = jnp.zeros(rest, out_ref.dtype)
+
+
+def swapped_rows_kernel(rows_ref, weight_ref, partner_ref, *out_refs):
     features = weight_ref.shape[2]
     slots = rows_ref.shape[0]
-    units = out_refs[0].shape[0]
-    total = dot(weight_ref[0], rows_ref[:, :features], NT) + partner_ref[:, :slots].astype(F32)
-    for step, out_ref in enumerate(out_refs):
-        out_ref[:, :slots] = total[step * units : (step + 1) * units].astype(out_ref.dtype)
-        if out_ref.shape[1] > slots:
-            out_ref[:, slots:] = jnp.zeros((units, out_ref.shape[1] - slots), out_ref.dtype)
+    kept = weight_ref.shape[1] // 2
+    total = dot(weight_ref[0, kept:, :], rows_ref[:, :features], NT)
+    total += partner_ref[kept:, :slots].astype(F32)
+    for side, out_ref in enumerate(out_refs):
+        store_wide(out_ref, slice(None), total[side * kept // 2 : (side + 1) * kept // 2])
+
+
+def kept_rows_kernel(rows_ref, weight_ref, partner_ref, low_ref, high_ref, *out_refs):
+    features = weight_ref.shape[2]
+    slots = rows_ref.shape[0]
+    kept = weight_ref.shape[1] // 2
+    total = dot(weight_ref[0, :kept, :], rows_ref[:, :features], NT)
+    total += partner_ref[:kept, :slots].astype(F32)
+    for i, out_ref in enumerate(out_refs):
+        for side, swapped_ref in enumerate((low_ref, high_ref)):
+            at = slice(i * 64 + side * 32, i * 64 + (side + 1) * 32)
+            value = total[at] + swapped_ref[i * 32 : (i + 1) * 32, :slots].astype(F32)
+            store_wide(out_ref, slice(side * 32, (side + 1) * 32), value)
 
 
 def hidden_kernel(gate_ref, up_ref, slot_gate_ref, *refs):
@@ -270,9 +297,11 @@
     j = lax.broadcasted_iota(jnp.int32, (experts, height, tokens), 1).astype(F32)
     chosen = jnp.sum(jnp.where(rank[:, None, :] == j, column, 0.0), axis=1)
     expert = lax.broadcasted_iota(jnp.int32, (experts, tokens), 0)
+    combine = []
     for k in range(ids_ref.shape[0]):
         hit = ids_ref[k : k + 1, :] == expert
-        combine_ref[k : k + 1, :] = jnp.sum(jnp.where(hit, chosen, 0.0), axis=0, keepdims=True)
+        combine.append(jnp.sum(jnp.where(hit, chosen, 0.0), axis=0, keepdims=True))
+    combine_ref[...] = jnp.concatenate(combine, axis=0).astype(BF)
 
 
 def body(out_grad, gate_weights, expert_ids, w_gate, w_up, w_down, saved_gate, saved_up):
@@ -296,15 +325,19 @@
         gate_weights.T,
         out_grad.T,
         plain=True,
+        mib=60,
     )
     arrived = lax.all_to_all(
         send.reshape(experts, rows, LANES), "local", split_axis=0, concat_axis=0, tiled=True
     )
     node = lax.axis_index("node")
+    depth = nodes // 2
+    z = node // 2
+    toward = 1 - 2 * (z % 2)
     weights = call(
         weights_kernel,
         shape((2, hidden // 2, features), BF),
-        jnp.stack([node % 2, node // 2]).astype(jnp.int32),
+        jnp.stack([node % 2, z, (z + toward) % depth, (z - toward) % depth]).astype(jnp.int32),
         w_down[0].T,
         smem=1,
         scratch=[pltpu.VMEM((2, hidden // LANES, 64, features), F32)],
@@ -316,17 +349,31 @@
         arrived.reshape(experts * rows, LANES),
         weights,
     )
-    depth = nodes // 2
-    own, *others = call(
-        own_half_kernel,
-        [shape((units, rounded), BF if step else F32) for step in range(depth)],
+    partner = lax.ppermute(other, "node", swap)
+    sides = call(
+        swapped_rows_kernel,
+        [shape((hidden // 8, rounded), BF)] * 2,
         packed,
         weights,
-        lax.ppermute(other, "node", swap),
+        partner,
+    )
+    pairs = [
+        [(n, (n + 2 * sign * (1 - 2 * (n // 2 % 2))) % nodes) for n in range(nodes)]
+        for sign in (1, -1)
+    ]
+    low, high = (lax.ppermute(side, "node", pair) for side, pair in zip(sides, pairs))
+    own, *others = call(
+        kept_rows_kernel,
+        [shape((units, rounded), BF if step else F32) for step in range(depth // 2)],
+        packed,
+        weights,
+        partner,
+        low,
+        high,
     )
     parts = [own]
-    for step in sorted(range(1, depth), key=lambda step: -min(step, depth - step)):
-        onward = [(n, (n + 2 * step) % nodes) for n in range(nodes)]
+    for step in sorted(range(1, depth // 2), key=lambda step: abs(step - depth // 4)):
+        onward = [(n, (n + 4 * step) % nodes) for n in range(nodes)]
         parts.append(lax.ppermute(others[step - 1], "node", onward))
     piece = call(
         hidden_kernel,
@@ -350,12 +397,12 @@
     )
     grad, combine = call(
         functools.partial(collect_kernel, capacity),
-        (shape((features, tokens), BF), shape((top, tokens), F32)),
+        (shape((features, tokens), BF), shape((top, tokens), BF)),
         returned.reshape(experts * rows, LANES),
         rank,
         ids,
     )
-    return grad.T, combine.T.astype(BF)
+    return grad.T, combine.T
 
 
 def solution(mesh):

time: 235 us -> 234 us (level)
  waiting for transfers between devices: 92.8 us -> 99.8 us
  starting transfers between devices: 56.6 us -> 50.8 us
    ppermute x7 -> x3, starting transfers between devices: 37.3 us -> 12.3 us  [body(): parts.append(lax.ppermute(others[step - 1], 'node', onward))]
    ppermute x1 -> x3, starting transfers between devices: 1.92 us -> 21 us  [the longest x2 19.1 us: body(): lax.ppermute(side, 'node', pair)]
    ppermute x1 -> x3, waiting for transfers between devices: 3.19 us -> 11.9 us  [the longest x2 8.69 us: body(): lax.ppermute(side, 'node', pair)]
    ppermute x7 -> x3, waiting for transfers between devices: 11.6 us -> 9.18 us  [body(): parts.append(lax.ppermute(others[step - 1], 'node', onward))]
    unnamed x20 -> x16, local copies, waits for them, and re-layouts: 5.12 us -> 2.88 us
    pallas_call x7 -> x8, Pallas kernels: 16.5 us -> 17.5 us  [call(): pl.pallas_call(kernel, out_shape=outs, in_specs=spec, out_specs=jax.tree....]
  transfers between devices with their start and end apart: 10 -> 8, of which waited for: 7 -> 6; matrix products, arithmetic and copies ran while one was open for 0% -> 0% of each run, Pallas kernels for 0% -> 0%
where the time goes in v5:
time: 234 us
  waiting for transfers between devices  99.8 us (43%)
  starting transfers between devices  50.8 us (22%)
  blocking collectives  48.7 us (21%)
  Pallas kernels  17.5 us (7%)
  between operations  14.2 us (6%)
  local copies, waits for them, and re-layouts  2.88 us (1%)
    all_to_all x1, blocking collectives, body(): lax.all_to_all(back.reshape(experts, rows, LANES), 'local', split_axis=0,...  48.7 us
    all_gather x1, waiting for transfers between devices, body(): gathered = lax.all_gather(piece, 'node', axis=0, tiled=False)  47.8 us
    all_to_all x1, waiting for transfers between devices, body(): lax.all_to_all(send.reshape(experts, rows, LANES), 'local', split_axis=0,...  30.9 us
    ppermute x2, starting transfers between devices, body(): lax.ppermute(side, 'node', pair)  19.1 us
    pallas_call x8, Pallas kernels, call(): pl.pallas_call(kernel, out_shape=outs, in_specs=spec, out_specs=jax.tree....  17.5 us
    all_to_all x1, starting transfers between devices, body(): lax.all_to_all(send.reshape(experts, rows, LANES), 'local', split_axis=0,...  17.5 us
    ppermute x3, starting transfers between devices, body(): parts.append(lax.ppermute(others[step - 1], 'node', onward))  12.3 us
    ppermute x3, waiting for transfers between devices, body(): parts.append(lax.ppermute(others[step - 1], 'node', onward))  9.18 us
  transfers between devices with their start and end apart: 8, of which 6 were waited for; matrix products, arithmetic and copies ran while one was open for 0% of the time, Pallas kernels for 0%

profile of v5, /device:TPU:4, one launch (start us, length us, event | category | flops | bytes accessed | tf_op | source)
XLA Modules:
  0.0 233.9 jit_solution(12434947922112474393)
XLA Ops:
  7.2 4.1 %shard_map.95 = (bf16[5120,128]{1,0:T(8,128)(2,1)}, f32[64,128]{1,0:T(8,128)}) custom-call(s32[8,128]{1,0:T(8,128)} %bitcast.30, bf16[8,128]{1,0:T(8,128)(2,1)} %bitcast.34, bf16[448,128]{1,0:T(8,128)(2,1)} %bitcast.33), custom_call_target="tpu_custom_call" | custom-call | tf_op jit(solution)/shard_map/pallas_call | solution.py:21
  11.2 17.5 %all-to-all-start = ((bf16[64,80,128]{2,1,0:T(8,128)(2,1)}), bf16[64,80,128]{2,1,0:T(8,128)(2,1)S(1)}, u32[]{:S(2)}, u32[]{:S(2)}) async-start(bf16[64,80,128]{2,1,0:T(8,128)(2,1)} %bitcast.32), calls=%async_computation | async-start | bytes 2621440 | tf_op jit(solution)/shard_map/all_to_all | solution.py:330
  28.9 0.1 pad_add_fusion.place_ref
  28.9 1.1 shard_map.96.weight_ref
  30.1 30.9 %all-to-all-done = bf16[64,80,128]{2,1,0:T(8,128)(2,1)S(1)} async-done(((bf16[64,80,128]{2,1,0:T(8,128)(2,1)}), bf16[64,80,128]{2,1,0:T(8,128)(2,1)S(1)}, u32[]{:S(2)}, u32[]{:S(2)}) %all-to-all-start) | async-done | bytes 1310752 | tf_op jit(solution)/shard_map/all_to_all | solution.py:330
  60.9 2.5 %shard_map.97 = (bf16[512,1408]{1,0:T(8,128)(2,1)S(1)}, bf16[1344,512]{1,0:T(8,128)(2,1)S(1)}, f32[8,1344]{1,0:T(8,128)S(1)}) custom-call(bf16[5120,128]{1,0:T(8,128)(2,1)S(1)} %bitcast.23, bf16[2,512,448]{2,1,0:T(8,128)(2,1)S(1)} %shard_map.96.weight_ref), custom_call_target="tpu_custom_call" | custom-call | tf_op jit(solution)/shard_map/pallas_call | solution.py:21
  63.5 1.9 collective-permute-start
  65.4 3.2 %collective-permute-done.partner_ref = bf16[512,1408]{1,0:T(8,128)(2,1)S(1)} collective-permute-done((bf16[512,1408]{1,0:T(8,128)(2,1)S(1)}, bf16[512,1408]{1,0:T(8,128)(2,1)S(1)}, u32[]{:S(2)}, u32[]{:S(2)}) %collective-permute-start) | collective-permute-done | bytes 1441824 | tf_op jit(solution)/shard_map/ppermute | solution.py:352
  68.6 0.6 shard_map.98
  69.2 4.9 %collective-permute-start.1 = (bf16[128,1408]{1,0:T(8,128)(2,1)S(1)}, bf16[128,1408]{1,0:T(8,128)(2,1)S(1)}, u32[]{:S(2)}, u32[]{:S(2)}) collective-permute-start(bf16[128,1408]{1,0:T(8,128)(2,1)S(1)} %get-tuple-element.19), channel_id=1, source_target_pairs={{0,128},{64,192},{128,0},{192,64},{256,384},{320,448},{384,256},{4... | collective-permute-start | bytes 1081352 | tf_op jit(solution)/shard_map/ppermute | solution.py:364
  74.1 14.2 %collective-permute-start.2 = (bf16[128,1408]{1,0:T(8,128)(2,1)S(1)}, bf16[128,1408]{1,0:T(8,128)(2,1)S(1)}, u32[]{:S(2)}, u32[]{:S(2)}) collective-permute-start(bf16[128,1408]{1,0:T(8,128)(2,1)S(1)} %get-tuple-element.20), channel_id=1, source_target_pairs={{0,896},{64,960},{128,256},{192,320},{256,128},{320,192},{384,512}... | collective-permute-start | bytes 1081352 | tf_op jit(solution)/shard_map/ppermute | solution.py:364
  88.3 8.7 %collective-permute-done.2.high_ref = bf16[128,1408]{1,0:T(8,128)(2,1)S(1)} collective-permute-done((bf16[128,1408]{1,0:T(8,128)(2,1)S(1)}, bf16[128,1408]{1,0:T(8,128)(2,1)S(1)}, u32[]{:S(2)}, u32[]{:S(2)}) %collective-permute-start.2) | collective-permute-done | bytes 360480 | tf_op jit(solution)/shard_map/ppermute | solution.py:364
  97.0 0.6 shard_map.99
  97.7 4.3 %collective-permute-start.3 = (bf16[64,1408]{1,0:T(8,128)(2,1)S(1)}, bf16[64,1408]{1,0:T(8,128)(2,1)S(1)}, u32[]{:S(2)}, u32[]{:S(2)}) collective-permute-start(bf16[64,1408]{1,0:T(8,128)(2,1)S(1)} %get-tuple-element.22), channel_id=1, source_target_pairs={{0,512},{64,576},{128,640},{192,704},{256,768},{320,832},{384,896}... | collective-permute-start | bytes 540680 | tf_op jit(solution)/shard_map/ppermute | solution.py:377
  102.0 4.9 %collective-permute-start.4 = (bf16[64,1408]{1,0:T(8,128)(2,1)S(1)}, bf16[64,1408]{1,0:T(8,128)(2,1)S(1)}, u32[]{:S(2)}, u32[]{:S(2)}) collective-permute-start(bf16[64,1408]{1,0:T(8,128)(2,1)S(1)} %get-tuple-element.23), channel_id=1, source_target_pairs={{0,256},{64,320},{128,384},{192,448},{256,512},{320,576},{384,640}... | collective-permute-start | bytes 540680 | tf_op jit(solution)/shard_map/ppermute | solution.py:377
  106.9 3.0 %collective-permute-start.5 = (bf16[64,1408]{1,0:T(8,128)(2,1)S(1)}, bf16[64,1408]{1,0:T(8,128)(2,1)S(1)}, u32[]{:S(2)}, u32[]{:S(2)}) collective-permute-start(bf16[64,1408]{1,0:T(8,128)(2,1)S(1)} %get-tuple-element.24), channel_id=1, source_target_pairs={{0,768},{64,832},{128,896},{192,960},{256,0},{320,64},{384,128},{4... | collective-permute-start | bytes 540680 | tf_op jit(solution)/shard_map/ppermute | solution.py:377
  109.9 5.0 %collective-permute-done.3.refs_1_ = bf16[64,1408]{1,0:T(8,128)(2,1)S(1)} collective-permute-done((bf16[64,1408]{1,0:T(8,128)(2,1)S(1)}, bf16[64,1408]{1,0:T(8,128)(2,1)S(1)}, u32[]{:S(2)}, u32[]{:S(2)}) %collective-permute-start.3) | collective-permute-done | bytes 180256 | tf_op jit(solution)/shard_map/ppermute | solution.py:377
  114.9 4.2 %collective-permute-done.5.refs_3_ = bf16[64,1408]{1,0:T(8,128)(2,1)S(1)} collective-permute-done((bf16[64,1408]{1,0:T(8,128)(2,1)S(1)}, bf16[64,1408]{1,0:T(8,128)(2,1)S(1)}, u32[]{:S(2)}, u32[]{:S(2)}) %collective-permute-start.5) | collective-permute-done | bytes 180256 | tf_op jit(solution)/shard_map/ppermute | solution.py:377
  119.1 1.1 shard_map.100
  120.3 47.8 %all-gather.3.cloned.1.call-done = bf16[2304,1344]{1,0:T(8,128)(2,1)} async-done(((bf16[144,1344]{1,0:T(8,128)(2,1)}), bf16[2304,1344]{1,0:T(8,128)(2,1)}) %all-gather.3.cloned.1.call-update) | async-done | bytes 6193168 | tf_op jit(solution)/shard_map/all_gather | solution.py:386
  168.1 2.8 %copy-done = bf16[2304,1344]{1,0:T(8,128)(2,1)S(1)} copy-done((bf16[2304,1344]{1,0:T(8,128)(2,1)S(1)}, bf16[2304,1344]{1,0:T(8,128)(2,1)}, u32[]{:S(2)}) %copy-start) | copy-done | bytes 6193176
  170.9 4.8 %shard_map.101 = bf16[5120,128]{1,0:T(8,128)(2,1)S(1)} custom-call(bf16[16,144,1344]{2,1,0:T(8,128)(2,1)S(1)} %bitcast.21, bf16[448,1024]{1,0:T(8,128)(2,1)S(1)} %bitcast.25, bf16[448,1024]{1,0:T(8,128)(2,1)S(1)} %bitcast.26), custom_call_target="tpu_custom_call" | custom-call | tf_op jit(solution)/shard_map/pallas_call | solution.py:21
  175.7 48.7 %all_to_all.10 = bf16[64,80,128]{2,1,0:T(8,128)(2,1)S(1)} all-to-all(bf16[64,80,128]{2,1,0:T(8,128)(2,1)S(1)} %bitcast.22), channel_id=1, replica_groups=mesh['node'=16,'local'=64] {'local'}, dimensions={0} | all-to-all | bytes 2621440 | tf_op jit(solution)/shard_map/all_to_all | solution.py:395
  224.4 2.7 %shard_map.102 = (bf16[448,128]{1,0:T(8,128)(2,1)}, bf16[8,128]{1,0:T(8,128)(2,1)}) custom-call(bf16[5120,128]{1,0:T(8,128)(2,1)S(1)} %bitcast.24, f32[64,128]{1,0:T(8,128)S(1)} %copy-done.6, s32[8,128]{1,0:T(8,128)S(1)} %bitcast.31), custom_call_target="tpu_custom_call" | custom-call | tf_op jit(solution)/shard_map/pallas_call | solution.py:21
  (19 shorter events, 0.1 us)
Async XLA Ops:
  11.2 17.7 %copy-start.3 = (bf16[1,1024,448]{1,2,0:T(8,128)(2,1)S(1)}, bf16[1,1024,448]{1,2,0:T(8,128)(2,1)}, u32[]{:S(2)}) copy-start(bf16[1,1024,448]{1,2,0:T(8,128)(2,1)} %param.13) | copy-start | bytes 2752516
  11.2 49.7 %all-to-all-start = ((bf16[64,80,128]{2,1,0:T(8,128)(2,1)}), bf16[64,80,128]{2,1,0:T(8,128)(2,1)S(1)}, u32[]{:S(2)}, u32[]{:S(2)}) async-start(bf16[64,80,128]{2,1,0:T(8,128)(2,1)} %bitcast.32), calls=%async_computation | async-start | bytes 2621440 | tf_op jit(solution)/shard_map/all_to_all | solution.py:330
  28.7 139.3 %all-gather.3.cloned.1.call-start = ((), (), s32[]{:S(2)}) async-start(), calls=%async_computation.2 | async-start | bytes 6893568 | tf_op jit(solution)/shard_map/all_gather | solution.py:386
  63.5 5.1 %collective-permute-start = (bf16[512,1408]{1,0:T(8,128)(2,1)S(1)}, bf16[512,1408]{1,0:T(8,128)(2,1)S(1)}, u32[]{:S(2)}, u32[]{:S(2)}) collective-permute-start(bf16[512,1408]{1,0:T(8,128)(2,1)S(1)} %get-tuple-element.18), channel_id=1, source_target_pairs={{0,64},{64,0},{128,192},{192,128},{256,320},{320,256},{384,448},{4... | collective-permute-start | bytes 4325384 | tf_op jit(solution)/shard_map/ppermute | solution.py:352
  69.2 19.1 %collective-permute-start.1 = (bf16[128,1408]{1,0:T(8,128)(2,1)S(1)}, bf16[128,1408]{1,0:T(8,128)(2,1)S(1)}, u32[]{:S(2)}, u32[]{:S(2)}) collective-permute-start(bf16[128,1408]{1,0:T(8,128)(2,1)S(1)} %get-tuple-element.19), channel_id=1, source_target_pairs={{0,128},{64,192},{128,0},{192,64},{256,384},{320,448},{384,256},{4... | collective-permute-start | bytes 1081352 | tf_op jit(solution)/shard_map/ppermute | solution.py:364
  74.1 45.0 %copy-start.4 = (bf16[1,64,1344]{2,1,0:T(8,128)(2,1)S(1)}, bf16[1,64,1344]{2,1,0:T(8,128)(2,1)}, u32[]{:S(2)}) copy-start(bf16[1,64,1344]{2,1,0:T(8,128)(2,1)} %param.14) | copy-start | bytes 516100
  74.1 45.0 %copy-start.5 = (bf16[1,64,1344]{2,1,0:T(8,128)(2,1)S(1)}, bf16[1,64,1344]{2,1,0:T(8,128)(2,1)}, u32[]{:S(2)}) copy-start(bf16[1,64,1344]{2,1,0:T(8,128)(2,1)} %param.15) | copy-start | bytes 516100
  74.1 22.9 %collective-permute-start.2 = (bf16[128,1408]{1,0:T(8,128)(2,1)S(1)}, bf16[128,1408]{1,0:T(8,128)(2,1)S(1)}, u32[]{:S(2)}, u32[]{:S(2)}) collective-permute-start(bf16[128,1408]{1,0:T(8,128)(2,1)S(1)} %get-tuple-element.20), channel_id=1, source_target_pairs={{0,896},{64,960},{128,256},{192,320},{256,128},{320,192},{384,512}... | collective-permute-start | bytes 1081352 | tf_op jit(solution)/shard_map/ppermute | solution.py:364
  97.6 70.4 %copy-start.1 = (bf16[1,448,1024]{2,1,0:T(8,128)(2,1)S(1)}, bf16[1,448,1024]{2,1,0:T(8,128)(2,1)}, u32[]{:S(2)}) copy-start(bf16[1,448,1024]{2,1,0:T(8,128)(2,1)} %param.11) | copy-start | bytes 2752516
  97.6 70.4 %copy-start.2 = (bf16[1,448,1024]{2,1,0:T(8,128)(2,1)S(1)}, bf16[1,448,1024]{2,1,0:T(8,128)(2,1)}, u32[]{:S(2)}) copy-start(bf16[1,448,1024]{2,1,0:T(8,128)(2,1)} %param.12) | copy-start | bytes 2752516
  97.7 17.3 %collective-permute-start.3 = (bf16[64,1408]{1,0:T(8,128)(2,1)S(1)}, bf16[64,1408]{1,0:T(8,128)(2,1)S(1)}, u32[]{:S(2)}, u32[]{:S(2)}) collective-permute-start(bf16[64,1408]{1,0:T(8,128)(2,1)S(1)} %get-tuple-element.22), channel_id=1, source_target_pairs={{0,512},{64,576},{128,640},{192,704},{256,768},{320,832},{384,896}... | collective-permute-start | bytes 540680 | tf_op jit(solution)/shard_map/ppermute | solution.py:377
  102.0 12.9 %collective-permute-start.4 = (bf16[64,1408]{1,0:T(8,128)(2,1)S(1)}, bf16[64,1408]{1,0:T(8,128)(2,1)S(1)}, u32[]{:S(2)}, u32[]{:S(2)}) collective-permute-start(bf16[64,1408]{1,0:T(8,128)(2,1)S(1)} %get-tuple-element.23), channel_id=1, source_target_pairs={{0,256},{64,320},{128,384},{192,448},{256,512},{320,576},{384,640}... | collective-permute-start | bytes 540680 | tf_op jit(solution)/shard_map/ppermute | solution.py:377
  106.9 12.2 %collective-permute-start.5 = (bf16[64,1408]{1,0:T(8,128)(2,1)S(1)}, bf16[64,1408]{1,0:T(8,128)(2,1)S(1)}, u32[]{:S(2)}, u32[]{:S(2)}) collective-permute-start(bf16[64,1408]{1,0:T(8,128)(2,1)S(1)} %get-tuple-element.24), channel_id=1, source_target_pairs={{0,768},{64,832},{128,896},{192,960},{256,0},{320,64},{384,128},{4... | collective-permute-start | bytes 540680 | tf_op jit(solution)/shard_map/ppermute | solution.py:377
  168.1 2.8 %copy-start = (bf16[2304,1344]{1,0:T(8,128)(2,1)S(1)}, bf16[2304,1344]{1,0:T(8,128)(2,1)}, u32[]{:S(2)}) copy-start(bf16[2304,1344]{1,0:T(8,128)(2,1)} %all-gather.3.cloned.1.call-done) | copy-start | bytes 18579460
  175.7 48.7 %copy-start.6 = (f32[64,128]{1,0:T(8,128)S(1)}, f32[64,128]{1,0:T(8,128)}, u32[]{:S(2)}) copy-start(f32[64,128]{1,0:T(8,128)} %get-tuple-element.25.rank_ref) | copy-start | bytes 98308
  175.7 48.7 %copy-start.7 = (s32[128,8]{0,1:T(8,128)S(1)}, s32[128,8]{0,1:T(8,128)}, u32[]{:S(2)}) copy-start(s32[128,8]{0,1:T(8,128)} %param.10) | copy-start | bytes 12292
Sparse Core Ops, SparseCore 0:
  120.4 47.6 all-gather.2

commit v6 on v3

--- a/solution.py
+++ b/solution.py
@@ -14,7 +14,7 @@
 EXTRA = 16
 
 
-def call(kernel, outs, *operands, smem=0, scratch=(), plain=False):
+def call(kernel, outs, *operands, smem=0, scratch=(), plain=False, mib=32):
     vmem = pl.BlockSpec() if plain else pl.BlockSpec(memory_space=pltpu.VMEM)
     spec = [pl.BlockSpec(memory_space=pltpu.SMEM)] * smem
     spec += [vmem] * (len(operands) - smem)
@@ -24,7 +24,7 @@
         in_specs=spec,
         out_specs=jax.tree.map(lambda _: vmem, outs),
         scratch_shapes=list(scratch),
-        compiler_params=pltpu.CompilerParams(vmem_limit_bytes=32 * 2**20),
+        compiler_params=pltpu.CompilerParams(vmem_limit_bytes=mib * 2**20),
     )(*operands)
 
 
@@ -122,9 +122,11 @@
     empty = jnp.zeros((LANES - tail.shape[0], tokens), BF)
     pieces = [grad_ref[c * LANES : (c + 1) * LANES, :] for c in range(full)]
     pieces += [jnp.concatenate([tail, empty], axis=0), jnp.concatenate([empty, tail], axis=0)]
-    total = jnp.zeros((experts * rows, LANES), F32)
-    for pick, piece in zip(picks(rank, features, capacity), pieces):
-        total += dot(pick, piece, NT)
+    total = dot(
+        jnp.concatenate(picks(rank, features, capacity), axis=1),
+        jnp.concatenate(pieces, axis=1),
+        NT,
+    )
     q = lax.broadcasted_iota(jnp.int32, (experts, rows, LANES), 1)
     total = jnp.where(q == scalars, gate, total.reshape(experts, rows, LANES))
     send_ref[...] = total.reshape(experts * rows, LANES).astype(BF)
@@ -178,15 +180,33 @@
     gate_ref[...] = dot(at, rows_ref[:, full * LANES :], NT)
 
 
+def store_wide(out_ref, at, value):
+    slots = value.shape[1]
+    out_ref[at, :slots] = value.astype(out_ref.dtype)
+    if out_ref.shape[1] > slots:
+        rest = (value.shape[0], out_ref.shape[1] - slots)
+        out_ref[at, slots:] = jnp.zeros(rest, out_ref.dtype)
+
+
 def own_half_kernel(rows_ref, weight_ref, partner_ref, *out_refs):
     features = weight_ref.shape[2]
     slots = rows_ref.shape[0]
-    units = out_refs[0].shape[0]
+    depth = len(out_refs) - 1
     total = dot(weight_ref[0], rows_ref[:, :features], NT) + partner_ref[:, :slots].astype(F32)
-    for step, out_ref in enumerate(out_refs):
-        out_ref[:, :slots] = total[step * units : (step + 1) * units].astype(out_ref.dtype)
-        if out_ref.shape[1] > slots:
-            out_ref[:, slots:] = jnp.zeros((units, out_ref.shape[1] - slots), out_ref.dtype)
+    for step in range(depth):
+        block = total[step * 64 : (step + 1) * 64]
+        if step == depth // 2:
+            store_wide(out_refs[step], slice(None), block[:32])
+            store_wide(out_refs[depth], slice(None), block[32:])
+        else:
+            store_wide(out_refs[step], slice(None), block)
+
+
+def relay_kernel(up_ref, down_ref, low_ref, high_ref, up_out_ref, down_out_ref):
+    up_out_ref[:32, :] = (up_ref[:32, :] + low_ref[...].astype(F32)).astype(BF)
+    up_out_ref[32:, :] = up_ref[32:, :].astype(BF)
+    down_out_ref[:32, :] = down_ref[:32, :].astype(BF)
+    down_out_ref[32:, :] = (down_ref[32:, :] + high_ref[...].astype(F32)).astype(BF)
 
 
 def hidden_kernel(gate_ref, up_ref, slot_gate_ref, *refs):
@@ -270,9 +290,11 @@
     j = lax.broadcasted_iota(jnp.int32, (experts, height, tokens), 1).astype(F32)
     chosen = jnp.sum(jnp.where(rank[:, None, :] == j, column, 0.0), axis=1)
     expert = lax.broadcasted_iota(jnp.int32, (experts, tokens), 0)
+    combine = []
     for k in range(ids_ref.shape[0]):
         hit = ids_ref[k : k + 1, :] == expert
-        combine_ref[k : k + 1, :] = jnp.sum(jnp.where(hit, chosen, 0.0), axis=0, keepdims=True)
+        combine.append(jnp.sum(jnp.where(hit, chosen, 0.0), axis=0, keepdims=True))
+    combine_ref[...] = jnp.concatenate(combine, axis=0).astype(BF)
 
 
 def body(out_grad, gate_weights, expert_ids, w_gate, w_up, w_down, saved_gate, saved_up):
@@ -296,11 +318,13 @@
         gate_weights.T,
         out_grad.T,
         plain=True,
+        mib=60,
     )
     arrived = lax.all_to_all(
         send.reshape(experts, rows, LANES), "local", split_axis=0, concat_axis=0, tiled=True
     )
     node = lax.axis_index("node")
+    depth = nodes // 2
     weights = call(
         weights_kernel,
         shape((2, hidden // 2, features), BF),
@@ -316,18 +340,34 @@
         arrived.reshape(experts * rows, LANES),
         weights,
     )
-    depth = nodes // 2
-    own, *others = call(
+    partner = lax.ppermute(other, "node", swap)
+    far, relay = depth // 2, depth // 4
+    wide = {0: F32, relay: F32, depth - relay: F32}
+    blocks = call(
         own_half_kernel,
-        [shape((units, rounded), BF if step else F32) for step in range(depth)],
+        [shape((units // 2 if i in (far, depth) else units, rounded), wide.get(i, BF)) for i in range(depth + 1)],
         packed,
         weights,
-        lax.ppermute(other, "node", swap),
-    )
-    parts = [own]
-    for step in sorted(range(1, depth), key=lambda step: -min(step, depth - step)):
-        onward = [(n, (n + 2 * step) % nodes) for n in range(nodes)]
-        parts.append(lax.ppermute(others[step - 1], "node", onward))
+        partner,
+    )
+
+    def send(value, step):
+        return lax.ppermute(value, "node", [(n, (n + 2 * step) % nodes) for n in range(nodes)])
+
+    low, high = send(blocks[far], relay), send(blocks[depth], -relay)
+    parts = [blocks[0]]
+    for step in range(far - 1, 0, -1):
+        if step != relay:
+            parts += [send(blocks[step], step), send(blocks[depth - step], -step)]
+    up, down = call(
+        relay_kernel,
+        [shape((units, rounded), BF)] * 2,
+        blocks[relay],
+        blocks[depth - relay],
+        low,
+        high,
+    )
+    parts += [send(up, relay), send(down, -relay)]
     piece = call(
         hidden_kernel,
         shape((2 * units + EXTRA, slots), BF),
@@ -350,12 +390,12 @@
     )
     grad, combine = call(
         functools.partial(collect_kernel, capacity),
-        (shape((features, tokens), BF), shape((top, tokens), F32)),
+        (shape((features, tokens), BF), shape((top, tokens), BF)),
         returned.reshape(experts * rows, LANES),
         rank,
         ids,
     )
-    return grad.T, combine.T.astype(BF)
+    return grad.T, combine.T
 
 
 def solution(mesh):

time: 235 us -> 237 us (level)
  starting transfers between devices: 56.6 us -> 61 us
    ppermute x8 -> x9, starting transfers between devices: 39.2 us -> 43.6 us  [the longest x8 41.7 us: send(): lax.ppermute(value, 'node', [(n, (n + 2 * step) % nodes) for n in range(n...]
    unnamed x20 -> x16, local copies, waits for them, and re-layouts: 5.12 us -> 2.88 us
    pallas_call x7 -> x8, Pallas kernels: 16.5 us -> 17.6 us  [call(): pl.pallas_call(kernel, out_shape=outs, in_specs=spec, out_specs=jax.tree....]
    ppermute x8 -> x9, waiting for transfers between devices: 14.8 us -> 13.8 us  [the longest x8 10.6 us: send(): lax.ppermute(value, 'node', [(n, (n + 2 * step) % nodes) for n in range(n...]
  transfers between devices with their start and end apart: 10 -> 11, of which waited for: 7 -> 7; matrix products, arithmetic and copies ran while one was open for 0% -> 0% of each run, Pallas kernels for 0% -> 0%
where the time goes in v6:
time: 237 us; the launch traced here: 236 us
  waiting for transfers between devices  92 us (39%)
  starting transfers between devices  61 us (26%)
  blocking collectives  48.7 us (21%)
  Pallas kernels  17.6 us (7%)
  between operations  14.2 us (6%)
  local copies, waits for them, and re-layouts  2.88 us (1%)
    all_to_all x1, blocking collectives, body(): lax.all_to_all(back.reshape(experts, rows, LANES), 'local', split_axis=0,...  48.7 us
    all_gather x1, waiting for transfers between devices, body(): gathered = lax.all_gather(piece, 'node', axis=0, tiled=False)  47.3 us
    ppermute x8, starting transfers between devices, send(): lax.ppermute(value, 'node', [(n, (n + 2 * step) % nodes) for n in range(n...  41.7 us
    all_to_all x1, waiting for transfers between devices, body(): lax.all_to_all(send.reshape(experts, rows, LANES), 'local', split_axis=0,...  30.9 us
    pallas_call x8, Pallas kernels, call(): pl.pallas_call(kernel, out_shape=outs, in_specs=spec, out_specs=jax.tree....  17.6 us
    all_to_all x1, starting transfers between devices, body(): lax.all_to_all(send.reshape(experts, rows, LANES), 'local', split_axis=0,...  17.4 us
    ppermute x8, waiting for transfers between devices, send(): lax.ppermute(value, 'node', [(n, (n + 2 * step) % nodes) for n in range(n...  10.6 us
  transfers between devices with their start and end apart: 11, of which 7 were waited for; matrix products, arithmetic and copies ran while one was open for 0% of the time, Pallas kernels for 0%

profile of v6, /device:TPU:4, one launch (start us, length us, event | category | flops | bytes accessed | tf_op | source)
XLA Modules:
  0.0 236.5 jit_solution(10569832812185819064)
XLA Ops:
  7.2 4.1 %shard_map.95 = (bf16[5120,128]{1,0:T(8,128)(2,1)}, f32[64,128]{1,0:T(8,128)}) custom-call(s32[8,128]{1,0:T(8,128)} %bitcast.28, bf16[8,128]{1,0:T(8,128)(2,1)} %bitcast.32, bf16[448,128]{1,0:T(8,128)(2,1)} %bitcast.31), custom_call_target="tpu_custom_call" | custom-call | tf_op jit(solution)/shard_map/pallas_call | solution.py:21
  11.3 17.4 %all-to-all-start = ((bf16[64,80,128]{2,1,0:T(8,128)(2,1)}), bf16[64,80,128]{2,1,0:T(8,128)(2,1)S(1)}, u32[]{:S(2)}, u32[]{:S(2)}) async-start(bf16[64,80,128]{2,1,0:T(8,128)(2,1)} %bitcast.30), calls=%async_computation | async-start | bytes 2621440 | tf_op jit(solution)/shard_map/all_to_all | solution.py:323
  29.9 30.9 %all-to-all-done = bf16[64,80,128]{2,1,0:T(8,128)(2,1)S(1)} async-done(((bf16[64,80,128]{2,1,0:T(8,128)(2,1)}), bf16[64,80,128]{2,1,0:T(8,128)(2,1)S(1)}, u32[]{:S(2)}, u32[]{:S(2)}) %all-to-all-start) | async-done | bytes 1310752 | tf_op jit(solution)/shard_map/all_to_all | solution.py:323
  60.9 2.5 %shard_map.97 = (bf16[512,1408]{1,0:T(8,128)(2,1)S(1)}, bf16[1344,512]{1,0:T(8,128)(2,1)S(1)}, f32[8,1344]{1,0:T(8,128)S(1)}) custom-call(bf16[5120,128]{1,0:T(8,128)(2,1)S(1)} %bitcast.21, bf16[2,512,448]{2,1,0:T(8,128)(2,1)S(1)} %shard_map.96.weight_ref), custom_call_target="tpu_custom_call" | custom-call | tf_op jit(solution)/shard_map/pallas_call | solution.py:21
  63.4 1.9 collective-permute-start
  65.3 3.2 %collective-permute-done.partner_ref = bf16[512,1408]{1,0:T(8,128)(2,1)S(1)} collective-permute-done((bf16[512,1408]{1,0:T(8,128)(2,1)S(1)}, bf16[512,1408]{1,0:T(8,128)(2,1)S(1)}, u32[]{:S(2)}, u32[]{:S(2)}) %collective-permute-start) | collective-permute-done | bytes 1441824 | tf_op jit(solution)/shard_map/ppermute | solution.py:343
  69.6 10.4 %collective-permute-start.1 = (bf16[64,1408]{1,0:T(8,128)(2,1)S(1)}, bf16[64,1408]{1,0:T(8,128)(2,1)S(1)}, u32[]{:S(2)}, u32[]{:S(2)}) collective-permute-start(bf16[64,1408]{1,0:T(8,128)(2,1)S(1)} %get-tuple-element.25), channel_id=1, source_target_pairs={{0,384},{64,448},{128,512},{192,576},{256,640},{320,704},{384,768}... | collective-permute-start | bytes 540680 | tf_op jit(solution)/shard_map/ppermute | solution.py:355
  79.9 8.2 %collective-permute-start.5 = (bf16[32,1408]{1,0:T(8,128)(2,1)S(1)}, bf16[32,1408]{1,0:T(8,128)(2,1)S(1)}, u32[]{:S(2)}, u32[]{:S(2)}) collective-permute-start(bf16[32,1408]{1,0:T(8,128)(2,1)S(1)} %get-tuple-element.31), channel_id=1, source_target_pairs={{0,256},{64,320},{128,384},{192,448},{256,512},{320,576},{384,640}... | collective-permute-start | bytes 270344 | tf_op jit(solution)/shard_map/ppermute | solution.py:355
  88.1 1.9 collective-permute-start.6
  90.1 6.4 %collective-permute-start.2 = (bf16[64,1408]{1,0:T(8,128)(2,1)S(1)}, bf16[64,1408]{1,0:T(8,128)(2,1)S(1)}, u32[]{:S(2)}, u32[]{:S(2)}) collective-permute-start(bf16[64,1408]{1,0:T(8,128)(2,1)S(1)} %get-tuple-element.26), channel_id=1, source_target_pairs={{0,640},{64,704},{128,768},{192,832},{256,896},{320,960},{384,0},{... | collective-permute-start | bytes 540680 | tf_op jit(solution)/shard_map/ppermute | solution.py:355
  96.5 3.1 %collective-permute-start.3 = (bf16[64,1408]{1,0:T(8,128)(2,1)S(1)}, bf16[64,1408]{1,0:T(8,128)(2,1)S(1)}, u32[]{:S(2)}, u32[]{:S(2)}) collective-permute-start(bf16[64,1408]{1,0:T(8,128)(2,1)S(1)} %get-tuple-element.27), channel_id=1, source_target_pairs={{0,128},{64,192},{128,256},{192,320},{256,384},{320,448},{384,512}... | collective-permute-start | bytes 540680 | tf_op jit(solution)/shard_map/ppermute | solution.py:355
  99.6 1.7 collective-permute-done.5.low_ref
  101.2 2.9 %collective-permute-start.4 = (bf16[64,1408]{1,0:T(8,128)(2,1)S(1)}, bf16[64,1408]{1,0:T(8,128)(2,1)S(1)}, u32[]{:S(2)}, u32[]{:S(2)}) collective-permute-start(bf16[64,1408]{1,0:T(8,128)(2,1)S(1)} %get-tuple-element.28), channel_id=1, source_target_pairs={{0,896},{64,960},{128,0},{192,64},{256,128},{320,192},{384,256},{4... | collective-permute-start | bytes 540680 | tf_op jit(solution)/shard_map/ppermute | solution.py:355
  104.3 4.4 %collective-permute-start.7 = (bf16[64,1408]{1,0:T(8,128)(2,1)S(1)}, bf16[64,1408]{1,0:T(8,128)(2,1)S(1)}, u32[]{:S(2)}, u32[]{:S(2)}) collective-permute-start(bf16[64,1408]{1,0:T(8,128)(2,1)S(1)} %get-tuple-element.33), channel_id=1, source_target_pairs={{0,256},{64,320},{128,384},{192,448},{256,512},{320,576},{384,640}... | collective-permute-start | bytes 540680 | tf_op jit(solution)/shard_map/ppermute | solution.py:355
  108.7 4.4 %collective-permute-start.8 = (bf16[64,1408]{1,0:T(8,128)(2,1)S(1)}, bf16[64,1408]{1,0:T(8,128)(2,1)S(1)}, u32[]{:S(2)}, u32[]{:S(2)}) collective-permute-start(bf16[64,1408]{1,0:T(8,128)(2,1)S(1)} %get-tuple-element.34), channel_id=1, source_target_pairs={{0,768},{64,832},{128,896},{192,960},{256,0},{320,64},{384,128},{4... | collective-permute-start | bytes 540680 | tf_op jit(solution)/shard_map/ppermute | solution.py:355
  113.1 1.2 collective-permute-done.4.refs_4_
  114.3 4.3 %collective-permute-done.7.refs_5_ = bf16[64,1408]{1,0:T(8,128)(2,1)S(1)} collective-permute-done((bf16[64,1408]{1,0:T(8,128)(2,1)S(1)}, bf16[64,1408]{1,0:T(8,128)(2,1)S(1)}, u32[]{:S(2)}, u32[]{:S(2)}) %collective-permute-start.7) | collective-permute-done | bytes 180256 | tf_op jit(solution)/shard_map/ppermute | solution.py:355
  118.6 3.4 %collective-permute-done.8.refs_6_ = bf16[64,1408]{1,0:T(8,128)(2,1)S(1)} collective-permute-done((bf16[64,1408]{1,0:T(8,128)(2,1)S(1)}, bf16[64,1408]{1,0:T(8,128)(2,1)S(1)}, u32[]{:S(2)}, u32[]{:S(2)}) %collective-permute-start.8) | collective-permute-done | bytes 180256 | tf_op jit(solution)/shard_map/ppermute | solution.py:355
  122.0 1.2 shard_map.100
  123.2 47.3 %all-gather.3.cloned.1.call-done = bf16[2304,1344]{1,0:T(8,128)(2,1)} async-done(((bf16[144,1344]{1,0:T(8,128)(2,1)}), bf16[2304,1344]{1,0:T(8,128)(2,1)}) %all-gather.3.cloned.1.call-update) | async-done | bytes 6193168 | tf_op jit(solution)/shard_map/all_gather | solution.py:379
  170.5 2.8 %copy-done = bf16[2304,1344]{1,0:T(8,128)(2,1)S(1)} copy-done((bf16[2304,1344]{1,0:T(8,128)(2,1)S(1)}, bf16[2304,1344]{1,0:T(8,128)(2,1)}, u32[]{:S(2)}) %copy-start) | copy-done | bytes 6193176
  173.4 4.8 %shard_map.101 = bf16[5120,128]{1,0:T(8,128)(2,1)S(1)} custom-call(bf16[16,144,1344]{2,1,0:T(8,128)(2,1)S(1)} %bitcast.19, bf16[448,1024]{1,0:T(8,128)(2,1)S(1)} %bitcast.23, bf16[448,1024]{1,0:T(8,128)(2,1)S(1)} %bitcast.24), custom_call_target="tpu_custom_call" | custom-call | tf_op jit(solution)/shard_map/pallas_call | solution.py:21
  178.2 48.7 %all_to_all.10 = bf16[64,80,128]{2,1,0:T(8,128)(2,1)S(1)} all-to-all(bf16[64,80,128]{2,1,0:T(8,128)(2,1)S(1)} %bitcast.20), channel_id=1, replica_groups=mesh['node'=16,'local'=64] {'local'}, dimensions={0} | all-to-all | bytes 2621440 | tf_op jit(solution)/shard_map/all_to_all | solution.py:388
  226.9 2.7 %shard_map.102 = (bf16[448,128]{1,0:T(8,128)(2,1)}, bf16[8,128]{1,0:T(8,128)(2,1)}) custom-call(bf16[5120,128]{1,0:T(8,128)(2,1)S(1)} %bitcast.22, f32[64,128]{1,0:T(8,128)S(1)} %copy-done.6, s32[8,128]{1,0:T(8,128)S(1)} %bitcast.29), custom_call_target="tpu_custom_call" | custom-call | tf_op jit(solution)/shard_map/pallas_call | solution.py:21
  (25 shorter events, 2.4 us)
Async XLA Ops:
  7.2 21.7 %copy-start.3 = (bf16[1,1024,448]{1,2,0:T(8,128)(2,1)S(1)}, bf16[1,1024,448]{1,2,0:T(8,128)(2,1)}, u32[]{:S(2)}) copy-start(bf16[1,1024,448]{1,2,0:T(8,128)(2,1)} %param.13) | copy-start | bytes 2752516
  11.3 49.6 %all-to-all-start = ((bf16[64,80,128]{2,1,0:T(8,128)(2,1)}), bf16[64,80,128]{2,1,0:T(8,128)(2,1)S(1)}, u32[]{:S(2)}, u32[]{:S(2)}) async-start(bf16[64,80,128]{2,1,0:T(8,128)(2,1)} %bitcast.30), calls=%async_computation | async-start | bytes 2621440 | tf_op jit(solution)/shard_map/all_to_all | solution.py:323
  28.7 141.8 %all-gather.3.cloned.1.call-start = ((), (), s32[]{:S(2)}) async-start(), calls=%async_computation.2 | async-start | bytes 6893568 | tf_op jit(solution)/shard_map/all_gather | solution.py:379
  63.4 5.1 %collective-permute-start = (bf16[512,1408]{1,0:T(8,128)(2,1)S(1)}, bf16[512,1408]{1,0:T(8,128)(2,1)S(1)}, u32[]{:S(2)}, u32[]{:S(2)}) collective-permute-start(bf16[512,1408]{1,0:T(8,128)(2,1)S(1)} %get-tuple-element.23), channel_id=1, source_target_pairs={{0,64},{64,0},{128,192},{192,128},{256,320},{320,256},{384,448},{4... | collective-permute-start | bytes 4325384 | tf_op jit(solution)/shard_map/ppermute | solution.py:343
  68.5 53.5 %copy-start.4 = (bf16[1,64,1344]{2,1,0:T(8,128)(2,1)S(1)}, bf16[1,64,1344]{2,1,0:T(8,128)(2,1)}, u32[]{:S(2)}) copy-start(bf16[1,64,1344]{2,1,0:T(8,128)(2,1)} %param.14) | copy-start | bytes 516100
  68.5 53.5 %copy-start.5 = (bf16[1,64,1344]{2,1,0:T(8,128)(2,1)S(1)}, bf16[1,64,1344]{2,1,0:T(8,128)(2,1)}, u32[]{:S(2)}) copy-start(bf16[1,64,1344]{2,1,0:T(8,128)(2,1)} %param.15) | copy-start | bytes 516100
  69.6 39.1 %collective-permute-start.1 = (bf16[64,1408]{1,0:T(8,128)(2,1)S(1)}, bf16[64,1408]{1,0:T(8,128)(2,1)S(1)}, u32[]{:S(2)}, u32[]{:S(2)}) collective-permute-start(bf16[64,1408]{1,0:T(8,128)(2,1)S(1)} %get-tuple-element.25), channel_id=1, source_target_pairs={{0,384},{64,448},{128,512},{192,576},{256,640},{320,704},{384,768}... | collective-permute-start | bytes 540680 | tf_op jit(solution)/shard_map/ppermute | solution.py:355
  79.9 21.3 %collective-permute-start.5 = (bf16[32,1408]{1,0:T(8,128)(2,1)S(1)}, bf16[32,1408]{1,0:T(8,128)(2,1)S(1)}, u32[]{:S(2)}, u32[]{:S(2)}) collective-permute-start(bf16[32,1408]{1,0:T(8,128)(2,1)S(1)} %get-tuple-element.31), channel_id=1, source_target_pairs={{0,256},{64,320},{128,384},{192,448},{256,512},{320,576},{384,640}... | collective-permute-start | bytes 270344 | tf_op jit(solution)/shard_map/ppermute | solution.py:355
  88.1 16.0 %collective-permute-start.6 = (bf16[32,1408]{1,0:T(8,128)(2,1)S(1)}, bf16[32,1408]{1,0:T(8,128)(2,1)S(1)}, u32[]{:S(2)}, u32[]{:S(2)}) collective-permute-start(bf16[32,1408]{1,0:T(8,128)(2,1)S(1)} %get-tuple-element.32), channel_id=1, source_target_pairs={{0,768},{64,832},{128,896},{192,960},{256,0},{320,64},{384,128},{4... | collective-permute-start | bytes 270344 | tf_op jit(solution)/shard_map/ppermute | solution.py:355
  90.1 23.0 %collective-permute-start.2 = (bf16[64,1408]{1,0:T(8,128)(2,1)S(1)}, bf16[64,1408]{1,0:T(8,128)(2,1)S(1)}, u32[]{:S(2)}, u32[]{:S(2)}) collective-permute-start(bf16[64,1408]{1,0:T(8,128)(2,1)S(1)} %get-tuple-element.26), channel_id=1, source_target_pairs={{0,640},{64,704},{128,768},{192,832},{256,896},{320,960},{384,0},{... | collective-permute-start | bytes 540680 | tf_op jit(solution)/shard_map/ppermute | solution.py:355
  96.5 16.6 %collective-permute-start.3 = (bf16[64,1408]{1,0:T(8,128)(2,1)S(1)}, bf16[64,1408]{1,0:T(8,128)(2,1)S(1)}, u32[]{:S(2)}, u32[]{:S(2)}) collective-permute-start(bf16[64,1408]{1,0:T(8,128)(2,1)S(1)} %get-tuple-element.27), channel_id=1, source_target_pairs={{0,128},{64,192},{128,256},{192,320},{256,384},{320,448},{384,512}... | collective-permute-start | bytes 540680 | tf_op jit(solution)/shard_map/ppermute | solution.py:355
  101.2 13.0 %collective-permute-start.4 = (bf16[64,1408]{1,0:T(8,128)(2,1)S(1)}, bf16[64,1408]{1,0:T(8,128)(2,1)S(1)}, u32[]{:S(2)}, u32[]{:S(2)}) collective-permute-start(bf16[64,1408]{1,0:T(8,128)(2,1)S(1)} %get-tuple-element.28), channel_id=1, source_target_pairs={{0,896},{64,960},{128,0},{192,64},{256,128},{320,192},{384,256},{4... | collective-permute-start | bytes 540680 | tf_op jit(solution)/shard_map/ppermute | solution.py:355
  104.2 66.3 %copy-start.1 = (bf16[1,448,1024]{2,1,0:T(8,128)(2,1)S(1)}, bf16[1,448,1024]{2,1,0:T(8,128)(2,1)}, u32[]{:S(2)}) copy-start(bf16[1,448,1024]{2,1,0:T(8,128)(2,1)} %param.11) | copy-start | bytes 2752516
  104.2 66.3 %copy-start.2 = (bf16[1,448,1024]{2,1,0:T(8,128)(2,1)S(1)}, bf16[1,448,1024]{2,1,0:T(8,128)(2,1)}, u32[]{:S(2)}) copy-start(bf16[1,448,1024]{2,1,0:T(8,128)(2,1)} %param.12) | copy-start | bytes 2752516
  104.3 14.3 %collective-permute-start.7 = (bf16[64,1408]{1,0:T(8,128)(2,1)S(1)}, bf16[64,1408]{1,0:T(8,128)(2,1)S(1)}, u32[]{:S(2)}, u32[]{:S(2)}) collective-permute-start(bf16[64,1408]{1,0:T(8,128)(2,1)S(1)} %get-tuple-element.33), channel_id=1, source_target_pairs={{0,256},{64,320},{128,384},{192,448},{256,512},{320,576},{384,640}... | collective-permute-start | bytes 540680 | tf_op jit(solution)/shard_map/ppermute | solution.py:355
  108.7 13.3 %collective-permute-start.8 = (bf16[64,1408]{1,0:T(8,128)(2,1)S(1)}, bf16[64,1408]{1,0:T(8,128)(2,1)S(1)}, u32[]{:S(2)}, u32[]{:S(2)}) collective-permute-start(bf16[64,1408]{1,0:T(8,128)(2,1)S(1)} %get-tuple-element.34), channel_id=1, source_target_pairs={{0,768},{64,832},{128,896},{192,960},{256,0},{320,64},{384,128},{4... | collective-permute-start | bytes 540680 | tf_op jit(solution)/shard_map/ppermute | solution.py:355
  170.5 2.8 %copy-start = (bf16[2304,1344]{1,0:T(8,128)(2,1)S(1)}, bf16[2304,1344]{1,0:T(8,128)(2,1)}, u32[]{:S(2)}) copy-start(bf16[2304,1344]{1,0:T(8,128)(2,1)} %all-gather.3.cloned.1.call-done) | copy-start | bytes 18579460
  178.2 48.7 %copy-start.6 = (f32[64,128]{1,0:T(8,128)S(1)}, f32[64,128]{1,0:T(8,128)}, u32[]{:S(2)}) copy-start(f32[64,128]{1,0:T(8,128)} %get-tuple-element.35.rank_ref) | copy-start | bytes 98308
  178.2 48.7 %copy-start.7 = (s32[128,8]{0,1:T(8,128)S(1)}, s32[128,8]{0,1:T(8,128)}, u32[]{:S(2)}) copy-start(s32[128,8]{0,1:T(8,128)} %param.10) | copy-start | bytes 12292
Sparse Core Ops, SparseCore 0:
  123.3 47.1 all-gather.2

commit v7 on v3

--- a/solution.py
+++ b/solution.py
@@ -14,7 +14,7 @@
 EXTRA = 16
 
 
-def call(kernel, outs, *operands, smem=0, scratch=(), plain=False):
+def call(kernel, outs, *operands, smem=0, scratch=(), plain=False, mib=32):
     vmem = pl.BlockSpec() if plain else pl.BlockSpec(memory_space=pltpu.VMEM)
     spec = [pl.BlockSpec(memory_space=pltpu.SMEM)] * smem
     spec += [vmem] * (len(operands) - smem)
@@ -24,7 +24,7 @@
         in_specs=spec,
         out_specs=jax.tree.map(lambda _: vmem, outs),
         scratch_shapes=list(scratch),
-        compiler_params=pltpu.CompilerParams(vmem_limit_bytes=32 * 2**20),
+        compiler_params=pltpu.CompilerParams(vmem_limit_bytes=mib * 2**20),
     )(*operands)
 
 
@@ -122,9 +122,11 @@
     empty = jnp.zeros((LANES - tail.shape[0], tokens), BF)
     pieces = [grad_ref[c * LANES : (c + 1) * LANES, :] for c in range(full)]
     pieces += [jnp.concatenate([tail, empty], axis=0), jnp.concatenate([empty, tail], axis=0)]
-    total = jnp.zeros((experts * rows, LANES), F32)
-    for pick, piece in zip(picks(rank, features, capacity), pieces):
-        total += dot(pick, piece, NT)
+    total = dot(
+        jnp.concatenate(picks(rank, features, capacity), axis=1),
+        jnp.concatenate(pieces, axis=1),
+        NT,
+    )
     q = lax.broadcasted_iota(jnp.int32, (experts, rows, LANES), 1)
     total = jnp.where(q == scalars, gate, total.reshape(experts, rows, LANES))
     send_ref[...] = total.reshape(experts * rows, LANES).astype(BF)
@@ -270,9 +272,11 @@
     j = lax.broadcasted_iota(jnp.int32, (experts, height, tokens), 1).astype(F32)
     chosen = jnp.sum(jnp.where(rank[:, None, :] == j, column, 0.0), axis=1)
     expert = lax.broadcasted_iota(jnp.int32, (experts, tokens), 0)
+    combine = []
     for k in range(ids_ref.shape[0]):
         hit = ids_ref[k : k + 1, :] == expert
-        combine_ref[k : k + 1, :] = jnp.sum(jnp.where(hit, chosen, 0.0), axis=0, keepdims=True)
+        combine.append(jnp.sum(jnp.where(hit, chosen, 0.0), axis=0, keepdims=True))
+    combine_ref[...] = jnp.concatenate(combine, axis=0).astype(BF)
 
 
 def body(out_grad, gate_weights, expert_ids, w_gate, w_up, w_down, saved_gate, saved_up):
@@ -296,6 +300,7 @@
         gate_weights.T,
         out_grad.T,
         plain=True,
+        mib=60,
     )
     arrived = lax.all_to_all(
         send.reshape(experts, rows, LANES), "local", split_axis=0, concat_axis=0, tiled=True
@@ -350,12 +355,12 @@
     )
     grad, combine = call(
         functools.partial(collect_kernel, capacity),
-        (shape((features, tokens), BF), shape((top, tokens), F32)),
+        (shape((features, tokens), BF), shape((top, tokens), BF)),
         returned.reshape(experts * rows, LANES),
         rank,
         ids,
     )
-    return grad.T, combine.T.astype(BF)
+    return grad.T, combine.T
 
 
 def solution(mesh):

time: 235 us -> 233 us (level)
    unnamed x20 -> x16, local copies, waits for them, and re-layouts: 5.12 us -> 2.87 us
where the time goes in v7:
time: 233 us
  waiting for transfers between devices  92.8 us (40%)
  starting transfers between devices  56.6 us (24%)
  blocking collectives  48.7 us (21%)
  Pallas kernels  17.5 us (8%)
  between operations  14.2 us (6%)
  local copies, waits for them, and re-layouts  2.87 us (1%)
    all_to_all x1, blocking collectives, body(): lax.all_to_all(back.reshape(experts, rows, LANES), 'local', split_axis=0,...  48.7 us
    all_gather x1, waiting for transfers between devices, body(): gathered = lax.all_gather(piece, 'node', axis=0, tiled=False)  47 us
    ppermute x7, starting transfers between devices, body(): parts.append(lax.ppermute(others[step - 1], 'node', onward))  37.3 us
    all_to_all x1, waiting for transfers between devices, body(): lax.all_to_all(send.reshape(experts, rows, LANES), 'local', split_axis=0,...  30.9 us
    pallas_call x7, Pallas kernels, call(): pl.pallas_call(kernel, out_shape=outs, in_specs=spec, out_specs=jax.tree....  17.5 us
    all_to_all x1, starting transfers between devices, body(): lax.all_to_all(send.reshape(experts, rows, LANES), 'local', split_axis=0,...  17.4 us
    ppermute x7, waiting for transfers between devices, body(): parts.append(lax.ppermute(others[step - 1], 'node', onward))  11.6 us
  transfers between devices with their start and end apart: 10, of which 7 were waited for; matrix products, arithmetic and copies ran while one was open for 0% of the time, Pallas kernels for 0%

profile of v7, /device:TPU:4, one launch (start us, length us, event | category | flops | bytes accessed | tf_op | source)
XLA Modules:
  0.0 232.7 jit_solution(11289412794953215175)
XLA Ops:
  7.2 4.1 %shard_map.95 = (bf16[5120,128]{1,0:T(8,128)(2,1)}, f32[64,128]{1,0:T(8,128)}) custom-call(s32[8,128]{1,0:T(8,128)} %bitcast.28, bf16[8,128]{1,0:T(8,128)(2,1)} %bitcast.32, bf16[448,128]{1,0:T(8,128)(2,1)} %bitcast.31), custom_call_target="tpu_custom_call" | custom-call | tf_op jit(solution)/shard_map/pallas_call | solution.py:21
  11.3 17.4 %all-to-all-start = ((bf16[64,80,128]{2,1,0:T(8,128)(2,1)}), bf16[64,80,128]{2,1,0:T(8,128)(2,1)S(1)}, u32[]{:S(2)}, u32[]{:S(2)}) async-start(bf16[64,80,128]{2,1,0:T(8,128)(2,1)} %bitcast.30), calls=%async_computation | async-start | bytes 2621440 | tf_op jit(solution)/shard_map/all_to_all | solution.py:305
  28.8 1.1 shard_map.96.weight_ref
  29.9 30.9 %all-to-all-done = bf16[64,80,128]{2,1,0:T(8,128)(2,1)S(1)} async-done(((bf16[64,80,128]{2,1,0:T(8,128)(2,1)}), bf16[64,80,128]{2,1,0:T(8,128)(2,1)S(1)}, u32[]{:S(2)}, u32[]{:S(2)}) %all-to-all-start) | async-done | bytes 1310752 | tf_op jit(solution)/shard_map/all_to_all | solution.py:305
  60.9 2.5 %shard_map.97 = (bf16[512,1408]{1,0:T(8,128)(2,1)S(1)}, bf16[1344,512]{1,0:T(8,128)(2,1)S(1)}, f32[8,1344]{1,0:T(8,128)S(1)}) custom-call(bf16[5120,128]{1,0:T(8,128)(2,1)S(1)} %bitcast.21, bf16[2,512,448]{2,1,0:T(8,128)(2,1)S(1)} %shard_map.96.weight_ref), custom_call_target="tpu_custom_call" | custom-call | tf_op jit(solution)/shard_map/pallas_call | solution.py:21
  63.4 1.9 collective-permute-start
  65.3 3.2 %collective-permute-done.partner_ref = bf16[512,1408]{1,0:T(8,128)(2,1)S(1)} collective-permute-done((bf16[512,1408]{1,0:T(8,128)(2,1)S(1)}, bf16[512,1408]{1,0:T(8,128)(2,1)S(1)}, u32[]{:S(2)}, u32[]{:S(2)}) %collective-permute-start) | collective-permute-done | bytes 1441824 | tf_op jit(solution)/shard_map/ppermute | solution.py:330
  69.6 14.3 %collective-permute-start.1 = (bf16[64,1408]{1,0:T(8,128)(2,1)S(1)}, bf16[64,1408]{1,0:T(8,128)(2,1)S(1)}, u32[]{:S(2)}, u32[]{:S(2)}) collective-permute-start(bf16[64,1408]{1,0:T(8,128)(2,1)S(1)} %get-tuple-element.22), channel_id=1, source_target_pairs={{0,512},{64,576},{128,640},{192,704},{256,768},{320,832},{384,896}... | collective-permute-start | bytes 540680 | tf_op jit(solution)/shard_map/ppermute | solution.py:335
  83.8 7.9 %collective-permute-start.2 = (bf16[64,1408]{1,0:T(8,128)(2,1)S(1)}, bf16[64,1408]{1,0:T(8,128)(2,1)S(1)}, u32[]{:S(2)}, u32[]{:S(2)}) collective-permute-start(bf16[64,1408]{1,0:T(8,128)(2,1)S(1)} %get-tuple-element.23), channel_id=1, source_target_pairs={{0,384},{64,448},{128,512},{192,576},{256,640},{320,704},{384,768}... | collective-permute-start | bytes 540680 | tf_op jit(solution)/shard_map/ppermute | solution.py:335
  91.8 1.9 collective-permute-start.3
  93.7 5.1 %collective-permute-start.4 = (bf16[64,1408]{1,0:T(8,128)(2,1)S(1)}, bf16[64,1408]{1,0:T(8,128)(2,1)S(1)}, u32[]{:S(2)}, u32[]{:S(2)}) collective-permute-start(bf16[64,1408]{1,0:T(8,128)(2,1)S(1)} %get-tuple-element.25), channel_id=1, source_target_pairs={{0,256},{64,320},{128,384},{192,448},{256,512},{320,576},{384,640}... | collective-permute-start | bytes 540680 | tf_op jit(solution)/shard_map/ppermute | solution.py:335
  98.8 2.8 %collective-permute-start.5 = (bf16[64,1408]{1,0:T(8,128)(2,1)S(1)}, bf16[64,1408]{1,0:T(8,128)(2,1)S(1)}, u32[]{:S(2)}, u32[]{:S(2)}) collective-permute-start(bf16[64,1408]{1,0:T(8,128)(2,1)S(1)} %get-tuple-element.26), channel_id=1, source_target_pairs={{0,768},{64,832},{128,896},{192,960},{256,0},{320,64},{384,128},{4... | collective-permute-start | bytes 540680 | tf_op jit(solution)/shard_map/ppermute | solution.py:335
  101.7 3.3 %collective-permute-start.6 = (bf16[64,1408]{1,0:T(8,128)(2,1)S(1)}, bf16[64,1408]{1,0:T(8,128)(2,1)S(1)}, u32[]{:S(2)}, u32[]{:S(2)}) collective-permute-start(bf16[64,1408]{1,0:T(8,128)(2,1)S(1)} %get-tuple-element.27), channel_id=1, source_target_pairs={{0,128},{64,192},{128,256},{192,320},{256,384},{320,448},{384,512}... | collective-permute-start | bytes 540680 | tf_op jit(solution)/shard_map/ppermute | solution.py:335
  105.0 4.2 %collective-permute-done.2.refs_2_ = bf16[64,1408]{1,0:T(8,128)(2,1)S(1)} collective-permute-done((bf16[64,1408]{1,0:T(8,128)(2,1)S(1)}, bf16[64,1408]{1,0:T(8,128)(2,1)S(1)}, u32[]{:S(2)}, u32[]{:S(2)}) %collective-permute-start.2) | collective-permute-done | bytes 180256 | tf_op jit(solution)/shard_map/ppermute | solution.py:335
  109.2 1.9 collective-permute-start.7
  111.1 1.5 collective-permute-done.4.refs_4_
  112.6 3.9 %collective-permute-done.5.refs_5_ = bf16[64,1408]{1,0:T(8,128)(2,1)S(1)} collective-permute-done((bf16[64,1408]{1,0:T(8,128)(2,1)S(1)}, bf16[64,1408]{1,0:T(8,128)(2,1)S(1)}, u32[]{:S(2)}, u32[]{:S(2)}) %collective-permute-start.5) | collective-permute-done | bytes 180256 | tf_op jit(solution)/shard_map/ppermute | solution.py:335
  116.5 2.0 collective-permute-done.7.refs_7_
  118.5 1.2 shard_map.99
  119.8 47.0 %all-gather.3.cloned.1.call-done = bf16[2304,1344]{1,0:T(8,128)(2,1)} async-done(((bf16[144,1344]{1,0:T(8,128)(2,1)}), bf16[2304,1344]{1,0:T(8,128)(2,1)}) %all-gather.3.cloned.1.call-update) | async-done | bytes 6193168 | tf_op jit(solution)/shard_map/all_gather | solution.py:344
  166.8 2.8 %copy-done = bf16[2304,1344]{1,0:T(8,128)(2,1)S(1)} copy-done((bf16[2304,1344]{1,0:T(8,128)(2,1)S(1)}, bf16[2304,1344]{1,0:T(8,128)(2,1)}, u32[]{:S(2)}) %copy-start) | copy-done | bytes 6193176
  169.6 4.8 %shard_map.100 = bf16[5120,128]{1,0:T(8,128)(2,1)S(1)} custom-call(bf16[16,144,1344]{2,1,0:T(8,128)(2,1)S(1)} %bitcast.19, bf16[448,1024]{1,0:T(8,128)(2,1)S(1)} %bitcast.23, bf16[448,1024]{1,0:T(8,128)(2,1)S(1)} %bitcast.24), custom_call_target="tpu_custom_call" | custom-call | tf_op jit(solution)/shard_map/pallas_call | solution.py:21
  174.5 48.7 %all_to_all.10 = bf16[64,80,128]{2,1,0:T(8,128)(2,1)S(1)} all-to-all(bf16[64,80,128]{2,1,0:T(8,128)(2,1)S(1)} %bitcast.20), channel_id=1, replica_groups=mesh['node'=16,'local'=64] {'local'}, dimensions={0} | all-to-all | bytes 2621440 | tf_op jit(solution)/shard_map/all_to_all | solution.py:353
  223.2 2.7 %shard_map.101 = (bf16[448,128]{1,0:T(8,128)(2,1)}, bf16[8,128]{1,0:T(8,128)(2,1)}) custom-call(bf16[5120,128]{1,0:T(8,128)(2,1)S(1)} %bitcast.22, f32[64,128]{1,0:T(8,128)S(1)} %copy-done.6, s32[8,128]{1,0:T(8,128)S(1)} %bitcast.29), custom_call_target="tpu_custom_call" | custom-call | tf_op jit(solution)/shard_map/pallas_call | solution.py:21
  (22 shorter events, 1.2 us)
Async XLA Ops:
  7.2 21.6 %copy-start.3 = (bf16[1,1024,448]{1,2,0:T(8,128)(2,1)S(1)}, bf16[1,1024,448]{1,2,0:T(8,128)(2,1)}, u32[]{:S(2)}) copy-start(bf16[1,1024,448]{1,2,0:T(8,128)(2,1)} %param.13) | copy-start | bytes 2752516
  11.3 49.6 %all-to-all-start = ((bf16[64,80,128]{2,1,0:T(8,128)(2,1)}), bf16[64,80,128]{2,1,0:T(8,128)(2,1)S(1)}, u32[]{:S(2)}, u32[]{:S(2)}) async-start(bf16[64,80,128]{2,1,0:T(8,128)(2,1)} %bitcast.30), calls=%async_computation | async-start | bytes 2621440 | tf_op jit(solution)/shard_map/all_to_all | solution.py:305
  28.7 138.1 %all-gather.3.cloned.1.call-start = ((), (), s32[]{:S(2)}) async-start(), calls=%async_computation.2 | async-start | bytes 6893568 | tf_op jit(solution)/shard_map/all_gather | solution.py:344
  63.4 5.1 %collective-permute-start = (bf16[512,1408]{1,0:T(8,128)(2,1)S(1)}, bf16[512,1408]{1,0:T(8,128)(2,1)S(1)}, u32[]{:S(2)}, u32[]{:S(2)}) collective-permute-start(bf16[512,1408]{1,0:T(8,128)(2,1)S(1)} %get-tuple-element.20), channel_id=1, source_target_pairs={{0,64},{64,0},{128,192},{192,128},{256,320},{320,256},{384,448},{4... | collective-permute-start | bytes 4325384 | tf_op jit(solution)/shard_map/ppermute | solution.py:330
  68.5 50.0 %copy-start.4 = (bf16[1,64,1344]{2,1,0:T(8,128)(2,1)S(1)}, bf16[1,64,1344]{2,1,0:T(8,128)(2,1)}, u32[]{:S(2)}) copy-start(bf16[1,64,1344]{2,1,0:T(8,128)(2,1)} %param.14) | copy-start | bytes 516100
  68.5 50.0 %copy-start.5 = (bf16[1,64,1344]{2,1,0:T(8,128)(2,1)S(1)}, bf16[1,64,1344]{2,1,0:T(8,128)(2,1)}, u32[]{:S(2)}) copy-start(bf16[1,64,1344]{2,1,0:T(8,128)(2,1)} %param.15) | copy-start | bytes 516100
  69.6 32.1 %collective-permute-start.1 = (bf16[64,1408]{1,0:T(8,128)(2,1)S(1)}, bf16[64,1408]{1,0:T(8,128)(2,1)S(1)}, u32[]{:S(2)}, u32[]{:S(2)}) collective-permute-start(bf16[64,1408]{1,0:T(8,128)(2,1)S(1)} %get-tuple-element.22), channel_id=1, source_target_pairs={{0,512},{64,576},{128,640},{192,704},{256,768},{320,832},{384,896}... | collective-permute-start | bytes 540680 | tf_op jit(solution)/shard_map/ppermute | solution.py:335
  83.8 25.3 %collective-permute-start.2 = (bf16[64,1408]{1,0:T(8,128)(2,1)S(1)}, bf16[64,1408]{1,0:T(8,128)(2,1)S(1)}, u32[]{:S(2)}, u32[]{:S(2)}) collective-permute-start(bf16[64,1408]{1,0:T(8,128)(2,1)S(1)} %get-tuple-element.23), channel_id=1, source_target_pairs={{0,384},{64,448},{128,512},{192,576},{256,640},{320,704},{384,768}... | collective-permute-start | bytes 540680 | tf_op jit(solution)/shard_map/ppermute | solution.py:335
  91.8 19.3 %collective-permute-start.3 = (bf16[64,1408]{1,0:T(8,128)(2,1)S(1)}, bf16[64,1408]{1,0:T(8,128)(2,1)S(1)}, u32[]{:S(2)}, u32[]{:S(2)}) collective-permute-start(bf16[64,1408]{1,0:T(8,128)(2,1)S(1)} %get-tuple-element.24), channel_id=1, source_target_pairs={{0,640},{64,704},{128,768},{192,832},{256,896},{320,960},{384,0},{... | collective-permute-start | bytes 540680 | tf_op jit(solution)/shard_map/ppermute | solution.py:335
  93.7 18.9 %collective-permute-start.4 = (bf16[64,1408]{1,0:T(8,128)(2,1)S(1)}, bf16[64,1408]{1,0:T(8,128)(2,1)S(1)}, u32[]{:S(2)}, u32[]{:S(2)}) collective-permute-start(bf16[64,1408]{1,0:T(8,128)(2,1)S(1)} %get-tuple-element.25), channel_id=1, source_target_pairs={{0,256},{64,320},{128,384},{192,448},{256,512},{320,576},{384,640}... | collective-permute-start | bytes 540680 | tf_op jit(solution)/shard_map/ppermute | solution.py:335
  98.8 17.7 %collective-permute-start.5 = (bf16[64,1408]{1,0:T(8,128)(2,1)S(1)}, bf16[64,1408]{1,0:T(8,128)(2,1)S(1)}, u32[]{:S(2)}, u32[]{:S(2)}) collective-permute-start(bf16[64,1408]{1,0:T(8,128)(2,1)S(1)} %get-tuple-element.26), channel_id=1, source_target_pairs={{0,768},{64,832},{128,896},{192,960},{256,0},{320,64},{384,128},{4... | collective-permute-start | bytes 540680 | tf_op jit(solution)/shard_map/ppermute | solution.py:335
  101.7 14.8 %collective-permute-start.6 = (bf16[64,1408]{1,0:T(8,128)(2,1)S(1)}, bf16[64,1408]{1,0:T(8,128)(2,1)S(1)}, u32[]{:S(2)}, u32[]{:S(2)}) collective-permute-start(bf16[64,1408]{1,0:T(8,128)(2,1)S(1)} %get-tuple-element.27), channel_id=1, source_target_pairs={{0,128},{64,192},{128,256},{192,320},{256,384},{320,448},{384,512}... | collective-permute-start | bytes 540680 | tf_op jit(solution)/shard_map/ppermute | solution.py:335
  109.2 9.4 %collective-permute-start.7 = (bf16[64,1408]{1,0:T(8,128)(2,1)S(1)}, bf16[64,1408]{1,0:T(8,128)(2,1)S(1)}, u32[]{:S(2)}, u32[]{:S(2)}) collective-permute-start(bf16[64,1408]{1,0:T(8,128)(2,1)S(1)} %get-tuple-element.28), channel_id=1, source_target_pairs={{0,896},{64,960},{128,0},{192,64},{256,128},{320,192},{384,256},{4... | collective-permute-start | bytes 540680 | tf_op jit(solution)/shard_map/ppermute | solution.py:335
  118.5 48.2 %copy-start.1 = (bf16[1,448,1024]{2,1,0:T(8,128)(2,1)S(1)}, bf16[1,448,1024]{2,1,0:T(8,128)(2,1)}, u32[]{:S(2)}) copy-start(bf16[1,448,1024]{2,1,0:T(8,128)(2,1)} %param.11) | copy-start | bytes 2752516
  118.5 48.2 %copy-start.2 = (bf16[1,448,1024]{2,1,0:T(8,128)(2,1)S(1)}, bf16[1,448,1024]{2,1,0:T(8,128)(2,1)}, u32[]{:S(2)}) copy-start(bf16[1,448,1024]{2,1,0:T(8,128)(2,1)} %param.12) | copy-start | bytes 2752516
  166.8 2.8 %copy-start = (bf16[2304,1344]{1,0:T(8,128)(2,1)S(1)}, bf16[2304,1344]{1,0:T(8,128)(2,1)}, u32[]{:S(2)}) copy-start(bf16[2304,1344]{1,0:T(8,128)(2,1)} %all-gather.3.cloned.1.call-done) | copy-start | bytes 18579460
  174.5 48.7 %copy-start.6 = (f32[64,128]{1,0:T(8,128)S(1)}, f32[64,128]{1,0:T(8,128)}, u32[]{:S(2)}) copy-start(f32[64,128]{1,0:T(8,128)} %get-tuple-element.29.rank_ref) | copy-start | bytes 98308
  174.5 48.7 %copy-start.7 = (s32[128,8]{0,1:T(8,128)S(1)}, s32[128,8]{0,1:T(8,128)}, u32[]{:S(2)}) copy-start(s32[128,8]{0,1:T(8,128)} %param.10) | copy-start | bytes 12292
Sparse Core Ops, SparseCore 0:
  119.9 46.8 all-gather.2

commit v8 on v7

--- a/solution.py
+++ b/solution.py
@@ -330,7 +330,7 @@
         lax.ppermute(other, "node", swap),
     )
     parts = [own]
-    for step in sorted(range(1, depth), key=lambda step: -min(step, depth - step)):
+    for step in sorted(range(1, depth), key=lambda step: min(step, depth - step)):
         onward = [(n, (n + 2 * step) % nodes) for n in range(nodes)]
         parts.append(lax.ppermute(others[step - 1], "node", onward))
     piece = call(

time: 233 us -> 241 us (1.034)
  waiting for transfers between devices: 92.8 us -> 99.3 us
    ppermute x7, waiting for transfers between devices: 11.6 us -> 15.8 us  [body(): parts.append(lax.ppermute(others[step - 1], 'node', onward))]
  transfers between devices with their start and end apart: 10 -> 10, of which waited for: 7 -> 5; matrix products, arithmetic and copies ran while one was open for 0% -> 0% of each run, Pallas kernels for 0% -> 0%
where the time goes in v8:
time: 241 us; the launch traced here: 240 us
  waiting for transfers between devices  99.3 us (41%)
  starting transfers between devices  57.4 us (24%)
  blocking collectives  48.7 us (20%)
  Pallas kernels  17.5 us (7%)
  between operations  14.2 us (6%)
  local copies, waits for them, and re-layouts  2.88 us (1%)
    all_gather x1, waiting for transfers between devices, body(): gathered = lax.all_gather(piece, 'node', axis=0, tiled=False)  49.3 us
    all_to_all x1, blocking collectives, body(): lax.all_to_all(back.reshape(experts, rows, LANES), 'local', split_axis=0,...  48.7 us
    ppermute x7, starting transfers between devices, body(): parts.append(lax.ppermute(others[step - 1], 'node', onward))  38.1 us
    all_to_all x1, waiting for transfers between devices, body(): lax.all_to_all(send.reshape(experts, rows, LANES), 'local', split_axis=0,...  30.9 us
    pallas_call x7, Pallas kernels, call(): pl.pallas_call(kernel, out_shape=outs, in_specs=spec, out_specs=jax.tree....  17.5 us
    all_to_all x1, starting transfers between devices, body(): lax.all_to_all(send.reshape(experts, rows, LANES), 'local', split_axis=0,...  17.4 us
    ppermute x7, waiting for transfers between devices, body(): parts.append(lax.ppermute(others[step - 1], 'node', onward))  15.8 us
  transfers between devices with their start and end apart: 10, of which 5 were waited for; matrix products, arithmetic and copies ran while one was open for 0% of the time, Pallas kernels for 0%

profile of v8, /device:TPU:4, one launch (start us, length us, event | category | flops | bytes accessed | tf_op | source)
XLA Modules:
  0.0 240.1 jit_solution(684987160786448508)
XLA Ops:
  7.2 4.1 %shard_map.95 = (bf16[5120,128]{1,0:T(8,128)(2,1)}, f32[64,128]{1,0:T(8,128)}) custom-call(s32[8,128]{1,0:T(8,128)} %bitcast.28, bf16[8,128]{1,0:T(8,128)(2,1)} %bitcast.32, bf16[448,128]{1,0:T(8,128)(2,1)} %bitcast.31), custom_call_target="tpu_custom_call" | custom-call | tf_op jit(solution)/shard_map/pallas_call | solution.py:21
  11.3 17.4 %all-to-all-start = ((bf16[64,80,128]{2,1,0:T(8,128)(2,1)}), bf16[64,80,128]{2,1,0:T(8,128)(2,1)S(1)}, u32[]{:S(2)}, u32[]{:S(2)}) async-start(bf16[64,80,128]{2,1,0:T(8,128)(2,1)} %bitcast.30), calls=%async_computation | async-start | bytes 2621440 | tf_op jit(solution)/shard_map/all_to_all | solution.py:305
  28.7 0.1 pad_add_fusion.place_ref
  28.8 1.1 shard_map.96.weight_ref
  29.9 30.9 %all-to-all-done = bf16[64,80,128]{2,1,0:T(8,128)(2,1)S(1)} async-done(((bf16[64,80,128]{2,1,0:T(8,128)(2,1)}), bf16[64,80,128]{2,1,0:T(8,128)(2,1)S(1)}, u32[]{:S(2)}, u32[]{:S(2)}) %all-to-all-start) | async-done | bytes 1310752 | tf_op jit(solution)/shard_map/all_to_all | solution.py:305
  60.9 2.5 %shard_map.97 = (bf16[512,1408]{1,0:T(8,128)(2,1)S(1)}, bf16[1344,512]{1,0:T(8,128)(2,1)S(1)}, f32[8,1344]{1,0:T(8,128)S(1)}) custom-call(bf16[5120,128]{1,0:T(8,128)(2,1)S(1)} %bitcast.21, bf16[2,512,448]{2,1,0:T(8,128)(2,1)S(1)} %shard_map.96.weight_ref), custom_call_target="tpu_custom_call" | custom-call | tf_op jit(solution)/shard_map/pallas_call | solution.py:21
  63.4 1.9 collective-permute-start
  65.3 3.2 %collective-permute-done.partner_ref = bf16[512,1408]{1,0:T(8,128)(2,1)S(1)} collective-permute-done((bf16[512,1408]{1,0:T(8,128)(2,1)S(1)}, bf16[512,1408]{1,0:T(8,128)(2,1)S(1)}, u32[]{:S(2)}, u32[]{:S(2)}) %collective-permute-start) | collective-permute-done | bytes 1441824 | tf_op jit(solution)/shard_map/ppermute | solution.py:330
  68.5 1.0 shard_map.98
  69.6 4.9 %collective-permute-start.1 = (bf16[64,1408]{1,0:T(8,128)(2,1)S(1)}, bf16[64,1408]{1,0:T(8,128)(2,1)S(1)}, u32[]{:S(2)}, u32[]{:S(2)}) collective-permute-start(bf16[64,1408]{1,0:T(8,128)(2,1)S(1)} %get-tuple-element.22), channel_id=1, source_target_pairs={{0,128},{64,192},{128,256},{192,320},{256,384},{320,448},{384,512}... | collective-permute-start | bytes 540680 | tf_op jit(solution)/shard_map/ppermute | solution.py:335
  74.5 14.1 %collective-permute-start.2 = (bf16[64,1408]{1,0:T(8,128)(2,1)S(1)}, bf16[64,1408]{1,0:T(8,128)(2,1)S(1)}, u32[]{:S(2)}, u32[]{:S(2)}) collective-permute-start(bf16[64,1408]{1,0:T(8,128)(2,1)S(1)} %get-tuple-element.23), channel_id=1, source_target_pairs={{0,896},{64,960},{128,0},{192,64},{256,128},{320,192},{384,256},{4... | collective-permute-start | bytes 540680 | tf_op jit(solution)/shard_map/ppermute | solution.py:335
  88.5 1.9 collective-permute-start.3
  90.4 6.0 %collective-permute-start.4 = (bf16[64,1408]{1,0:T(8,128)(2,1)S(1)}, bf16[64,1408]{1,0:T(8,128)(2,1)S(1)}, u32[]{:S(2)}, u32[]{:S(2)}) collective-permute-start(bf16[64,1408]{1,0:T(8,128)(2,1)S(1)} %get-tuple-element.25), channel_id=1, source_target_pairs={{0,768},{64,832},{128,896},{192,960},{256,0},{320,64},{384,128},{4... | collective-permute-start | bytes 540680 | tf_op jit(solution)/shard_map/ppermute | solution.py:335
  96.5 1.9 collective-permute-start.5
  98.4 6.9 %collective-permute-start.6 = (bf16[64,1408]{1,0:T(8,128)(2,1)S(1)}, bf16[64,1408]{1,0:T(8,128)(2,1)S(1)}, u32[]{:S(2)}, u32[]{:S(2)}) collective-permute-start(bf16[64,1408]{1,0:T(8,128)(2,1)S(1)} %get-tuple-element.27), channel_id=1, source_target_pairs={{0,640},{64,704},{128,768},{192,832},{256,896},{320,960},{384,0},{... | collective-permute-start | bytes 540680 | tf_op jit(solution)/shard_map/ppermute | solution.py:335
  105.4 2.4 collective-permute-start.7
  107.8 12.0 %collective-permute-done.5.refs_5_ = bf16[64,1408]{1,0:T(8,128)(2,1)S(1)} collective-permute-done((bf16[64,1408]{1,0:T(8,128)(2,1)S(1)}, bf16[64,1408]{1,0:T(8,128)(2,1)S(1)}, u32[]{:S(2)}, u32[]{:S(2)}) %collective-permute-start.5) | collective-permute-done | bytes 180256 | tf_op jit(solution)/shard_map/ppermute | solution.py:335
  119.8 3.8 %collective-permute-done.6.refs_6_ = bf16[64,1408]{1,0:T(8,128)(2,1)S(1)} collective-permute-done((bf16[64,1408]{1,0:T(8,128)(2,1)S(1)}, bf16[64,1408]{1,0:T(8,128)(2,1)S(1)}, u32[]{:S(2)}, u32[]{:S(2)}) %collective-permute-start.6) | collective-permute-done | bytes 180256 | tf_op jit(solution)/shard_map/ppermute | solution.py:335
  123.6 1.2 shard_map.99
  124.8 49.3 %all-gather.3.cloned.1.call-done = bf16[2304,1344]{1,0:T(8,128)(2,1)} async-done(((bf16[144,1344]{1,0:T(8,128)(2,1)}), bf16[2304,1344]{1,0:T(8,128)(2,1)}) %all-gather.3.cloned.1.call-update) | async-done | bytes 6193168 | tf_op jit(solution)/shard_map/all_gather | solution.py:344
  174.1 2.8 %copy-done = bf16[2304,1344]{1,0:T(8,128)(2,1)S(1)} copy-done((bf16[2304,1344]{1,0:T(8,128)(2,1)S(1)}, bf16[2304,1344]{1,0:T(8,128)(2,1)}, u32[]{:S(2)}) %copy-start) | copy-done | bytes 6193176
  177.0 4.8 %shard_map.100 = bf16[5120,128]{1,0:T(8,128)(2,1)S(1)} custom-call(bf16[16,144,1344]{2,1,0:T(8,128)(2,1)S(1)} %bitcast.19, bf16[448,1024]{1,0:T(8,128)(2,1)S(1)} %bitcast.23, bf16[448,1024]{1,0:T(8,128)(2,1)S(1)} %bitcast.24), custom_call_target="tpu_custom_call" | custom-call | tf_op jit(solution)/shard_map/pallas_call | solution.py:21
  181.8 48.7 %all_to_all.10 = bf16[64,80,128]{2,1,0:T(8,128)(2,1)S(1)} all-to-all(bf16[64,80,128]{2,1,0:T(8,128)(2,1)S(1)} %bitcast.20), channel_id=1, replica_groups=mesh['node'=16,'local'=64] {'local'}, dimensions={0} | all-to-all | bytes 2621440 | tf_op jit(solution)/shard_map/all_to_all | solution.py:353
  230.5 2.7 %shard_map.101 = (bf16[448,128]{1,0:T(8,128)(2,1)}, bf16[8,128]{1,0:T(8,128)(2,1)}) custom-call(bf16[5120,128]{1,0:T(8,128)(2,1)S(1)} %bitcast.22, f32[64,128]{1,0:T(8,128)S(1)} %copy-done.6, s32[8,128]{1,0:T(8,128)S(1)} %bitcast.29), custom_call_target="tpu_custom_call" | custom-call | tf_op jit(solution)/shard_map/pallas_call | solution.py:21
  (22 shorter events, 0.1 us)
Async XLA Ops:
  7.2 21.6 %copy-start.3 = (bf16[1,1024,448]{1,2,0:T(8,128)(2,1)S(1)}, bf16[1,1024,448]{1,2,0:T(8,128)(2,1)}, u32[]{:S(2)}) copy-start(bf16[1,1024,448]{1,2,0:T(8,128)(2,1)} %param.13) | copy-start | bytes 2752516
  11.3 49.6 %all-to-all-start = ((bf16[64,80,128]{2,1,0:T(8,128)(2,1)}), bf16[64,80,128]{2,1,0:T(8,128)(2,1)S(1)}, u32[]{:S(2)}, u32[]{:S(2)}) async-start(bf16[64,80,128]{2,1,0:T(8,128)(2,1)} %bitcast.30), calls=%async_computation | async-start | bytes 2621440 | tf_op jit(solution)/shard_map/all_to_all | solution.py:305
  28.7 145.5 %all-gather.3.cloned.1.call-start = ((), (), s32[]{:S(2)}) async-start(), calls=%async_computation.2 | async-start | bytes 6893568 | tf_op jit(solution)/shard_map/all_gather | solution.py:344
  63.4 5.1 %collective-permute-start = (bf16[512,1408]{1,0:T(8,128)(2,1)S(1)}, bf16[512,1408]{1,0:T(8,128)(2,1)S(1)}, u32[]{:S(2)}, u32[]{:S(2)}) collective-permute-start(bf16[512,1408]{1,0:T(8,128)(2,1)S(1)} %get-tuple-element.20), channel_id=1, source_target_pairs={{0,64},{64,0},{128,192},{192,128},{256,320},{320,256},{384,448},{4... | collective-permute-start | bytes 4325384 | tf_op jit(solution)/shard_map/ppermute | solution.py:330
  68.5 55.0 %copy-start.4 = (bf16[1,64,1344]{2,1,0:T(8,128)(2,1)S(1)}, bf16[1,64,1344]{2,1,0:T(8,128)(2,1)}, u32[]{:S(2)}) copy-start(bf16[1,64,1344]{2,1,0:T(8,128)(2,1)} %param.14) | copy-start | bytes 516100
  68.5 55.0 %copy-start.5 = (bf16[1,64,1344]{2,1,0:T(8,128)(2,1)S(1)}, bf16[1,64,1344]{2,1,0:T(8,128)(2,1)}, u32[]{:S(2)}) copy-start(bf16[1,64,1344]{2,1,0:T(8,128)(2,1)} %param.15) | copy-start | bytes 516100
  69.6 28.9 %collective-permute-start.1 = (bf16[64,1408]{1,0:T(8,128)(2,1)S(1)}, bf16[64,1408]{1,0:T(8,128)(2,1)S(1)}, u32[]{:S(2)}, u32[]{:S(2)}) collective-permute-start(bf16[64,1408]{1,0:T(8,128)(2,1)S(1)} %get-tuple-element.22), channel_id=1, source_target_pairs={{0,128},{64,192},{128,256},{192,320},{256,384},{320,448},{384,512}... | collective-permute-start | bytes 540680 | tf_op jit(solution)/shard_map/ppermute | solution.py:335
  74.5 30.9 %collective-permute-start.2 = (bf16[64,1408]{1,0:T(8,128)(2,1)S(1)}, bf16[64,1408]{1,0:T(8,128)(2,1)S(1)}, u32[]{:S(2)}, u32[]{:S(2)}) collective-permute-start(bf16[64,1408]{1,0:T(8,128)(2,1)S(1)} %get-tuple-element.23), channel_id=1, source_target_pairs={{0,896},{64,960},{128,0},{192,64},{256,128},{320,192},{384,256},{4... | collective-permute-start | bytes 540680 | tf_op jit(solution)/shard_map/ppermute | solution.py:335
  88.5 19.2 %collective-permute-start.3 = (bf16[64,1408]{1,0:T(8,128)(2,1)S(1)}, bf16[64,1408]{1,0:T(8,128)(2,1)S(1)}, u32[]{:S(2)}, u32[]{:S(2)}) collective-permute-start(bf16[64,1408]{1,0:T(8,128)(2,1)S(1)} %get-tuple-element.24), channel_id=1, source_target_pairs={{0,256},{64,320},{128,384},{192,448},{256,512},{320,576},{384,640}... | collective-permute-start | bytes 540680 | tf_op jit(solution)/shard_map/ppermute | solution.py:335
  90.4 17.3 %collective-permute-start.4 = (bf16[64,1408]{1,0:T(8,128)(2,1)S(1)}, bf16[64,1408]{1,0:T(8,128)(2,1)S(1)}, u32[]{:S(2)}, u32[]{:S(2)}) collective-permute-start(bf16[64,1408]{1,0:T(8,128)(2,1)S(1)} %get-tuple-element.25), channel_id=1, source_target_pairs={{0,768},{64,832},{128,896},{192,960},{256,0},{320,64},{384,128},{4... | collective-permute-start | bytes 540680 | tf_op jit(solution)/shard_map/ppermute | solution.py:335
  96.5 23.3 %collective-permute-start.5 = (bf16[64,1408]{1,0:T(8,128)(2,1)S(1)}, bf16[64,1408]{1,0:T(8,128)(2,1)S(1)}, u32[]{:S(2)}, u32[]{:S(2)}) collective-permute-start(bf16[64,1408]{1,0:T(8,128)(2,1)S(1)} %get-tuple-element.26), channel_id=1, source_target_pairs={{0,384},{64,448},{128,512},{192,576},{256,640},{320,704},{384,768}... | collective-permute-start | bytes 540680 | tf_op jit(solution)/shard_map/ppermute | solution.py:335
  98.4 25.1 %collective-permute-start.6 = (bf16[64,1408]{1,0:T(8,128)(2,1)S(1)}, bf16[64,1408]{1,0:T(8,128)(2,1)S(1)}, u32[]{:S(2)}, u32[]{:S(2)}) collective-permute-start(bf16[64,1408]{1,0:T(8,128)(2,1)S(1)} %get-tuple-element.27), channel_id=1, source_target_pairs={{0,640},{64,704},{128,768},{192,832},{256,896},{320,960},{384,0},{... | collective-permute-start | bytes 540680 | tf_op jit(solution)/shard_map/ppermute | solution.py:335
  105.4 18.2 %collective-permute-start.7 = (bf16[64,1408]{1,0:T(8,128)(2,1)S(1)}, bf16[64,1408]{1,0:T(8,128)(2,1)S(1)}, u32[]{:S(2)}, u32[]{:S(2)}) collective-permute-start(bf16[64,1408]{1,0:T(8,128)(2,1)S(1)} %get-tuple-element.28), channel_id=1, source_target_pairs={{0,512},{64,576},{128,640},{192,704},{256,768},{320,832},{384,896}... | collective-permute-start | bytes 540680 | tf_op jit(solution)/shard_map/ppermute | solution.py:335
  123.5 50.6 %copy-start.1 = (bf16[1,448,1024]{2,1,0:T(8,128)(2,1)S(1)}, bf16[1,448,1024]{2,1,0:T(8,128)(2,1)}, u32[]{:S(2)}) copy-start(bf16[1,448,1024]{2,1,0:T(8,128)(2,1)} %param.11) | copy-start | bytes 2752516
  123.6 50.6 %copy-start.2 = (bf16[1,448,1024]{2,1,0:T(8,128)(2,1)S(1)}, bf16[1,448,1024]{2,1,0:T(8,128)(2,1)}, u32[]{:S(2)}) copy-start(bf16[1,448,1024]{2,1,0:T(8,128)(2,1)} %param.12) | copy-start | bytes 2752516
  174.1 2.8 %copy-start = (bf16[2304,1344]{1,0:T(8,128)(2,1)S(1)}, bf16[2304,1344]{1,0:T(8,128)(2,1)}, u32[]{:S(2)}) copy-start(bf16[2304,1344]{1,0:T(8,128)(2,1)} %all-gather.3.cloned.1.call-done) | copy-start | bytes 18579460
  181.8 48.7 %copy-start.6 = (f32[64,128]{1,0:T(8,128)S(1)}, f32[64,128]{1,0:T(8,128)}, u32[]{:S(2)}) copy-start(f32[64,128]{1,0:T(8,128)} %get-tuple-element.29.rank_ref) | copy-start | bytes 98308
  181.8 48.7 %copy-start.7 = (s32[128,8]{0,1:T(8,128)S(1)}, s32[128,8]{0,1:T(8,128)}, u32[]{:S(2)}) copy-start(s32[128,8]{0,1:T(8,128)} %param.10) | copy-start | bytes 12292
Sparse Core Ops, SparseCore 0:
  124.9 49.1 all-gather.2
